TPU v7x, 256 devices: a whole 4x4x8 slice. The times are simulated.
256 devices in a mesh: partner: 32 (over z, x), row: 8 (over y, core).
Axes of the slice: x: 4, y: 4, z: 8, core: 2. Of those that a mesh axis runs over, the one named last changes fastest.
Arguments:
- rhs: float32 [131072, 1024], P(('partner', 'row')), may hold values from -6 to 6
- leaf_inverse: bfloat16 [131072, 4096], P(('partner', 'row')), may hold values from -0.09375 to 0.09375
- leaf_sizes: int32 [32], P('partner'), may hold values from 2048 to 4096, as said below
- u_tilde: bfloat16 [5, 131072, 128], P(None, ('partner', 'row')), may hold values from -0.25 to 0.25
- v_right: bfloat16 [5, 131072, 128], P(None, ('partner', 'row'))
- cap_factor: float32 [5, 32, 128, 128], P(None, 'partner'), as said below
Outputs:
- solution: float32 [131072, 1024], P(('partner', 'row'))
Inputs may be any that keep to these rules, and one draw needn't show every extreme that they name: `leaf_sizes`: each leaf size lies in 2048 to 4096; some leaf has exactly 4096 and some exactly 2048. cap_factor[l, p] is the same matrix for all leaves p of one node of level l, that is all p that agree above bit l.
All inputs are finite; a program needn't handle non-finite values.
Results may differ from a plain program's by a relative error of at most 0.0095.
Values may be sent and summed in bfloat16 or wider, within the bound.
No kernel may reach another device: no remote copies, remote signals or barrier semaphores. Data moves between devices by JAX's collectives and lax.ppermute only.
A program may use at most 64 MiB of HBM per device.

v0:
```python
import jax
import jax.numpy as jnp
from jax import lax
from jax.sharding import PartitionSpec as P


def partner(block, axis, distance):
    count = lax.axis_size(axis)
    route = []
    for low in range(count):
        high = low | 1 << distance
        if high != low and high < count:
            route += [(low, high), (high, low)]
    return lax.ppermute(block, axis, route)


def halves(data):
    upper_part = data.astype(jnp.bfloat16)
    lower_part = (data - upper_part.astype(jnp.float32)).astype(jnp.bfloat16)
    return (upper_part, lower_part)


def project_rows(factor, data):
    upper_part, lower_part = halves(data)
    first = jnp.einsum("ir,is->rs", factor, upper_part, preferred_element_type=jnp.float32)
    return first + jnp.einsum("ir,is->rs", factor, lower_part, preferred_element_type=jnp.float32)


def expand_rows(factor, data):
    upper_part, lower_part = halves(data)
    first = jnp.dot(factor, upper_part, preferred_element_type=jnp.float32)
    return first + jnp.dot(factor, lower_part, preferred_element_type=jnp.float32)


def shards(rhs, leaf_inverse, leaf_sizes, u_tilde, v_right, cap_factor):
    highest = lax.Precision.HIGHEST
    rows = rhs.shape[0]
    levels = u_tilde.shape[0]
    place = lax.axis_index("row") * rows + jnp.arange(rows, dtype=jnp.int32)
    live = (place < leaf_sizes[0]).astype(jnp.float32)[:, None]
    rhs_b = (rhs * live).astype(jnp.bfloat16)
    solution = live * jnp.dot(
        leaf_inverse,
        lax.all_gather(rhs_b, "row", axis=0, tiled=True),
        preferred_element_type=jnp.float32,
    )
    basis = u_tilde * live.astype(jnp.bfloat16)[None]
    cap_local = jnp.einsum("lir,lit->lrt", v_right, basis, preferred_element_type=jnp.float32)
    partner_index = lax.axis_index("partner")
    for level in range(levels):
        proj_local = project_rows(v_right[level], solution)
        proj, own_cap = lax.psum((proj_local, cap_local[level]), "row")
        cols = proj.shape[1]
        joined = jnp.concatenate([proj, own_cap], axis=1)
        for bit in range(level):
            joined = joined + partner(joined, "partner", bit)
        sibling = partner(joined, "partner", level)
        proj = joined[:, :cols]
        own_cap = joined[:, cols:]
        sib_proj = sibling[:, :cols]
        sib_cap = sibling[:, cols:]
        upper = partner_index >> level & 1 == 1
        first_proj = jnp.where(upper, sib_proj, proj)
        second_proj = jnp.where(upper, proj, sib_proj)
        first_cap = jnp.where(upper, sib_cap, own_cap)
        second_cap = jnp.where(upper, own_cap, sib_cap)
        factor = cap_factor[level, 0]
        inner = first_proj - jnp.dot(first_cap, second_proj, precision=highest)
        coeff_second = jnp.dot(factor, inner, precision=highest)
        coeff_first = second_proj - jnp.dot(second_cap, coeff_second, precision=highest)
        coeff = jnp.where(upper, coeff_second, coeff_first)
        solution = solution - expand_rows(basis[level], coeff)
    return solution


def solution(mesh):
    return jax.shard_map(
        shards,
        mesh=mesh,
        in_specs=(
            P(("partner", "row"), None),
            P(("partner", "row"), None),
            P("partner"),
            P(None, ("partner", "row"), None),
            P(None, ("partner", "row"), None),
            P(None, "partner", None, None),
        ),
        out_specs=P(("partner", "row"), None),
        check_vma=False,
    )
```

profile of v0, /device:TPU:1, one launch (start us, length us, event | category | flops | bytes accessed | tf_op | source)
XLA Modules:
  0.0 726.5 jit_solution(11884844995092441596)
XLA Ops:
  11.5 55.3 %all-gather.2.cloned.1.call-done = bf16[4096,1024]{1,0:T(8,128)(2,1)} async-done(((bf16[512,1024]{1,0:T(8,128)(2,1)}), bf16[4096,1024]{1,0:T(8,128)(2,1)}) %all-gather.2.cloned.1.call-update) | async-done | bytes 8388624 | tf_op jit(solution)/shard_map/all_gather | solution.py:44
  66.8 8.2 %fusion.146 = f32[1024,512]{1,0:T(8,128)S(1)} fusion(bf16[4096,1024]{1,0:T(8,128)(2,1)} %all-gather.2.cloned.1.call-done, bf16[512,4096]{1,0:T(8,128)(2,1)} %param.7), kind=kOutput, calls=%fused_computation.194 | convolution fusion | flops 4294967296 | bytes 14680064 | tf_op jit(solution)/shard_map/dot_general | solution.py:42
  76.8 64.1 %all-reduce.19.cloned.1.call-done = (f32[128,1024]{0,1:T(8,128)}, f32[128,128]{0,1:T(8,128)}) async-done(((f32[128,1024]{0,1:T(8,128)}, f32[128,128]{0,1:T(8,128)}), (f32[128,1024]{0,1:T(8,128)}, f32[128,128]{0,1:T(8,128)})) %all-reduce.19.cloned.1.call-update) | async-done | bytes 589840 | tf_op jit(solution)/shard_map/psum | solution.py:52
  144.1 11.2 %collective-permute-done = f32[128,1152]{0,1:T(8,128)} collective-permute-done((f32[128,1152]{0,1:T(8,128)}, f32[128,1152]{0,1:T(8,128)}, u32[]{:S(2)}, u32[]{:S(2)}) %collective-permute-start) | collective-permute-done | bytes 589856 | tf_op jit(solution)/shard_map/ppermute | solution.py:14
  163.6 69.2 %all-reduce.17.cloned.1.call-done = (f32[128,1024]{0,1:T(8,128)}, f32[128,128]{0,1:T(8,128)}) async-done(((f32[128,1024]{0,1:T(8,128)}, f32[128,128]{0,1:T(8,128)}), (f32[128,1024]{0,1:T(8,128)}, f32[128,128]{0,1:T(8,128)})) %all-reduce.17.cloned.1.call-update) | async-done | bytes 589840 | tf_op jit(solution)/shard_map/psum | solution.py:52
  235.9 10.9 %collective-permute-done.1 = f32[128,1152]{0,1:T(8,128)S(1)} collective-permute-done((f32[128,1152]{0,1:T(8,128)S(1)}, f32[128,1152]{0,1:T(8,128)S(1)}, u32[]{:S(2)}, u32[]{:S(2)}) %collective-permute-start.1) | collective-permute-done | bytes 589856 | tf_op jit(solution)/shard_map/ppermute | solution.py:14
  246.9 3.0 collective-permute-start.2
  249.9 11.7 %collective-permute-done.2 = f32[128,1152]{0,1:T(8,128)S(1)} collective-permute-done((f32[128,1152]{0,1:T(8,128)S(1)}, f32[128,1152]{0,1:T(8,128)S(1)}, u32[]{:S(2)}, u32[]{:S(2)}) %collective-permute-start.2) | collective-permute-done | bytes 589856 | tf_op jit(solution)/shard_map/ppermute | solution.py:14
  267.3 71.6 %all-reduce.15.cloned.1.call-done = (f32[128,1024]{0,1:T(8,128)}, f32[128,128]{0,1:T(8,128)}) async-done(((f32[128,1024]{0,1:T(8,128)}, f32[128,128]{0,1:T(8,128)}), (f32[128,1024]{0,1:T(8,128)}, f32[128,128]{0,1:T(8,128)})) %all-reduce.15.cloned.1.call-update) | async-done | bytes 589840 | tf_op jit(solution)/shard_map/psum | solution.py:52
  342.0 10.9 %collective-permute-done.3 = f32[128,1152]{0,1:T(8,128)S(1)} collective-permute-done((f32[128,1152]{0,1:T(8,128)S(1)}, f32[128,1152]{0,1:T(8,128)S(1)}, u32[]{:S(2)}, u32[]{:S(2)}) %collective-permute-start.3) | collective-permute-done | bytes 589856 | tf_op jit(solution)/shard_map/ppermute | solution.py:14
  355.7 12.0 %collective-permute-done.4 = f32[128,1152]{0,1:T(8,128)S(1)} collective-permute-done((f32[128,1152]{0,1:T(8,128)S(1)}, f32[128,1152]{0,1:T(8,128)S(1)}, u32[]{:S(2)}, u32[]{:S(2)}) %collective-permute-start.4) | collective-permute-done | bytes 589856 | tf_op jit(solution)/shard_map/ppermute | solution.py:14
  369.9 10.3 %collective-permute-done.5 = f32[128,1152]{0,1:T(8,128)} collective-permute-done((f32[128,1152]{0,1:T(8,128)}, f32[128,1152]{0,1:T(8,128)}, u32[]{:S(2)}, u32[]{:S(2)}) %collective-permute-start.5) | collective-permute-done | bytes 589856 | tf_op jit(solution)/shard_map/ppermute | solution.py:14
  388.5 74.2 %all-reduce.13.cloned.1.call-done = (f32[128,1024]{0,1:T(8,128)}, f32[128,128]{0,1:T(8,128)}) async-done(((f32[128,1024]{0,1:T(8,128)}, f32[128,128]{0,1:T(8,128)}), (f32[128,1024]{0,1:T(8,128)}, f32[128,128]{0,1:T(8,128)})) %all-reduce.13.cloned.1.call-update) | async-done | bytes 589840 | tf_op jit(solution)/shard_map/psum | solution.py:52
  465.8 10.9 %collective-permute-done.6 = f32[128,1152]{0,1:T(8,128)S(1)} collective-permute-done((f32[128,1152]{0,1:T(8,128)S(1)}, f32[128,1152]{0,1:T(8,128)S(1)}, u32[]{:S(2)}, u32[]{:S(2)}) %collective-permute-start.6) | collective-permute-done | bytes 589856 | tf_op jit(solution)/shard_map/ppermute | solution.py:14
  479.5 12.0 %collective-permute-done.7 = f32[128,1152]{0,1:T(8,128)S(1)} collective-permute-done((f32[128,1152]{0,1:T(8,128)S(1)}, f32[128,1152]{0,1:T(8,128)S(1)}, u32[]{:S(2)}, u32[]{:S(2)}) %collective-permute-start.7) | collective-permute-done | bytes 589856 | tf_op jit(solution)/shard_map/ppermute | solution.py:14
  493.0 10.0 %collective-permute-done.8 = f32[128,1152]{0,1:T(8,128)S(1)} collective-permute-done((f32[128,1152]{0,1:T(8,128)S(1)}, f32[128,1152]{0,1:T(8,128)S(1)}, u32[]{:S(2)}, u32[]{:S(2)}) %collective-permute-start.8) | collective-permute-done | bytes 589856 | tf_op jit(solution)/shard_map/ppermute | solution.py:14
  505.6 24.5 %collective-permute-done.9 = f32[128,1152]{0,1:T(8,128)S(1)} collective-permute-done((f32[128,1152]{0,1:T(8,128)S(1)}, f32[128,1152]{0,1:T(8,128)S(1)}, u32[]{:S(2)}, u32[]{:S(2)}) %collective-permute-start.9) | collective-permute-done | bytes 589856 | tf_op jit(solution)/shard_map/ppermute | solution.py:14
  535.8 74.5 %all-reduce.11.cloned.1.call-done = (f32[128,1024]{0,1:T(8,128)}, f32[128,128]{0,1:T(8,128)}) async-done(((f32[128,1024]{0,1:T(8,128)}, f32[128,128]{0,1:T(8,128)}), (f32[128,1024]{0,1:T(8,128)}, f32[128,128]{0,1:T(8,128)})) %all-reduce.11.cloned.1.call-update) | async-done | bytes 589840 | tf_op jit(solution)/shard_map/psum | solution.py:52
  613.4 10.9 %collective-permute-done.10 = f32[128,1152]{0,1:T(8,128)S(1)} collective-permute-done((f32[128,1152]{0,1:T(8,128)S(1)}, f32[128,1152]{0,1:T(8,128)S(1)}, u32[]{:S(2)}, u32[]{:S(2)}) %collective-permute-start.10) | collective-permute-done | bytes 589856 | tf_op jit(solution)/shard_map/ppermute | solution.py:14
  627.2 12.0 %collective-permute-done.11 = f32[128,1152]{0,1:T(8,128)S(1)} collective-permute-done((f32[128,1152]{0,1:T(8,128)S(1)}, f32[128,1152]{0,1:T(8,128)S(1)}, u32[]{:S(2)}, u32[]{:S(2)}) %collective-permute-start.11) | collective-permute-done | bytes 589856 | tf_op jit(solution)/shard_map/ppermute | solution.py:14
  640.6 10.0 %collective-permute-done.12 = f32[128,1152]{0,1:T(8,128)S(1)} collective-permute-done((f32[128,1152]{0,1:T(8,128)S(1)}, f32[128,1152]{0,1:T(8,128)S(1)}, u32[]{:S(2)}, u32[]{:S(2)}) %collective-permute-start.12) | collective-permute-done | bytes 589856 | tf_op jit(solution)/shard_map/ppermute | solution.py:14
  653.0 24.2 %collective-permute-done.13 = f32[128,1152]{0,1:T(8,128)S(1)} collective-permute-done((f32[128,1152]{0,1:T(8,128)S(1)}, f32[128,1152]{0,1:T(8,128)S(1)}, u32[]{:S(2)}, u32[]{:S(2)}) %collective-permute-start.13) | collective-permute-done | bytes 589856 | tf_op jit(solution)/shard_map/ppermute | solution.py:14
  677.3 7.3 collective-permute-start.14
  684.6 24.8 %collective-permute-done.14 = f32[128,1152]{0,1:T(8,128)} collective-permute-done((f32[128,1152]{0,1:T(8,128)S(1)}, f32[128,1152]{0,1:T(8,128)}, u32[]{:S(2)}, u32[]{:S(2)}) %collective-permute-start.14) | collective-permute-done | bytes 589856 | tf_op jit(solution)/shard_map/ppermute | solution.py:14
  (104 shorter events, 78.2 us)
Async XLA Ops:
  6.5 60.2 %all-gather.2.cloned.1.call-start = ((), (), s32[]{:S(2)}) async-start(), calls=%async_computation | async-start | bytes 9437184 | tf_op jit(solution)/shard_map/all_gather | solution.py:44
  7.2 3.1 copy-start.5
  10.1 130.8 %all-reduce.19.cloned.1.call-start = ((), (), s32[]{:S(2)}) async-start(), calls=%async_computation.5 | async-start | bytes 1179648 | tf_op jit(solution)/shard_map/psum | solution.py:52
  76.7 156.1 %all-reduce.17.cloned.1.call-start = ((), (), s32[]{:S(2)}) async-start(), calls=%async_computation.4 | async-start | bytes 1179648 | tf_op jit(solution)/shard_map/psum | solution.py:52
  140.9 16.1 %copy-start.4 = (f32[128,1024]{0,1:T(8,128)S(1)}, f32[128,1024]{0,1:T(8,128)}, u32[]{:S(2)}) copy-start(f32[128,1024]{0,1:T(8,128)} %get-tuple-element.13) | copy-start | bytes 1572868
  142.9 15.7 %copy-start.8 = (f32[128,128]{0,1:T(8,128)S(1)}, f32[128,128]{0,1:T(8,128)}, u32[]{:S(2)}) copy-start(f32[128,128]{0,1:T(8,128)} %get-tuple-element.14) | copy-start | bytes 196612
  142.9 12.4 %collective-permute-start = (f32[128,1152]{0,1:T(8,128)}, f32[128,1152]{0,1:T(8,128)}, u32[]{:S(2)}, u32[]{:S(2)}) collective-permute-start(f32[128,1152]{0,1:T(8,128)} %pad_maximum_fusion), channel_id=1, source_target_pairs={{0,8},{8,0},{16,24},{24,16},{32,40},{40,32},{48,56},{56,48},{64,72... | collective-permute-start | bytes 1769480 | tf_op jit(solution)/shard_map/ppermute | solution.py:14
  163.6 175.3 %all-reduce.15.cloned.1.call-start = ((), (), s32[]{:S(2)}) async-start(), calls=%async_computation.3 | async-start | bytes 1179648 | tf_op jit(solution)/shard_map/psum | solution.py:52
  234.8 12.1 %collective-permute-start.1 = (f32[128,1152]{0,1:T(8,128)S(1)}, f32[128,1152]{0,1:T(8,128)S(1)}, u32[]{:S(2)}, u32[]{:S(2)}) collective-permute-start(f32[128,1152]{0,1:T(8,128)S(1)} %constant_dynamic-update-slice_fusion), channel_id=1, source_target_pairs={{0,8},{8,0},{16,24},{24,16},{32,40},{40,32},{48,56},{56,48},{64,72... | collective-permute-start | bytes 1769480 | tf_op jit(solution)/shard_map/ppermute | solution.py:14
  246.9 14.6 %collective-permute-start.2 = (f32[128,1152]{0,1:T(8,128)S(1)}, f32[128,1152]{0,1:T(8,128)S(1)}, u32[]{:S(2)}, u32[]{:S(2)}) collective-permute-start(f32[128,1152]{0,1:T(8,128)S(1)} %add.117), channel_id=1, source_target_pairs={{0,16},{16,0},{8,24},{24,8},{32,48},{48,32},{40,56},{56,40},{64,80... | collective-permute-start | bytes 1769480 | tf_op jit(solution)/shard_map/ppermute | solution.py:14
  267.3 195.4 %all-reduce.13.cloned.1.call-start = ((), (), s32[]{:S(2)}) async-start(), calls=%async_computation.2 | async-start | bytes 1179648 | tf_op jit(solution)/shard_map/psum | solution.py:52
  340.8 12.1 %collective-permute-start.3 = (f32[128,1152]{0,1:T(8,128)S(1)}, f32[128,1152]{0,1:T(8,128)S(1)}, u32[]{:S(2)}, u32[]{:S(2)}) collective-permute-start(f32[128,1152]{0,1:T(8,128)S(1)} %constant_dynamic-update-slice_fusion.2), channel_id=1, source_target_pairs={{0,8},{8,0},{16,24},{24,16},{32,40},{40,32},{48,56},{56,48},{64,72... | collective-permute-start | bytes 1769480 | tf_op jit(solution)/shard_map/ppermute | solution.py:14
  352.9 14.8 %collective-permute-start.4 = (f32[128,1152]{0,1:T(8,128)S(1)}, f32[128,1152]{0,1:T(8,128)S(1)}, u32[]{:S(2)}, u32[]{:S(2)}) collective-permute-start(f32[128,1152]{0,1:T(8,128)S(1)} %add.121), channel_id=1, source_target_pairs={{0,16},{16,0},{8,24},{24,8},{32,48},{48,32},{40,56},{56,40},{64,80... | collective-permute-start | bytes 1769480 | tf_op jit(solution)/shard_map/ppermute | solution.py:14
  368.6 11.6 %collective-permute-start.5 = (f32[128,1152]{0,1:T(8,128)}, f32[128,1152]{0,1:T(8,128)}, u32[]{:S(2)}, u32[]{:S(2)}) collective-permute-start(f32[128,1152]{0,1:T(8,128)} %add.122), channel_id=1, source_target_pairs={{0,32},{32,0},{8,40},{40,8},{16,48},{48,16},{24,56},{56,24},{64,96... | collective-permute-start | bytes 1769480 | tf_op jit(solution)/shard_map/ppermute | solution.py:14
  388.4 221.9 %all-reduce.11.cloned.1.call-start = ((), (), s32[]{:S(2)}) async-start(), calls=%async_computation.1 | async-start | bytes 1179648 | tf_op jit(solution)/shard_map/psum | solution.py:52
  464.6 12.1 %collective-permute-start.6 = (f32[128,1152]{0,1:T(8,128)S(1)}, f32[128,1152]{0,1:T(8,128)S(1)}, u32[]{:S(2)}, u32[]{:S(2)}) collective-permute-start(f32[128,1152]{0,1:T(8,128)S(1)} %constant_dynamic-update-slice_fusion.4), channel_id=1, source_target_pairs={{0,8},{8,0},{16,24},{24,16},{32,40},{40,32},{48,56},{56,48},{64,72... | collective-permute-start | bytes 1769480 | tf_op jit(solution)/shard_map/ppermute | solution.py:14
  476.8 14.8 %collective-permute-start.7 = (f32[128,1152]{0,1:T(8,128)S(1)}, f32[128,1152]{0,1:T(8,128)S(1)}, u32[]{:S(2)}, u32[]{:S(2)}) collective-permute-start(f32[128,1152]{0,1:T(8,128)S(1)} %add.126), channel_id=1, source_target_pairs={{0,16},{16,0},{8,24},{24,8},{32,48},{48,32},{40,56},{56,40},{64,80... | collective-permute-start | bytes 1769480 | tf_op jit(solution)/shard_map/ppermute | solution.py:14
  491.6 11.4 %collective-permute-start.8 = (f32[128,1152]{0,1:T(8,128)S(1)}, f32[128,1152]{0,1:T(8,128)S(1)}, u32[]{:S(2)}, u32[]{:S(2)}) collective-permute-start(f32[128,1152]{0,1:T(8,128)S(1)} %add.127), channel_id=1, source_target_pairs={{0,32},{32,0},{8,40},{40,8},{16,48},{48,16},{24,56},{56,24},{64,96... | collective-permute-start | bytes 1769480 | tf_op jit(solution)/shard_map/ppermute | solution.py:14
  503.1 27.0 %collective-permute-start.9 = (f32[128,1152]{0,1:T(8,128)S(1)}, f32[128,1152]{0,1:T(8,128)S(1)}, u32[]{:S(2)}, u32[]{:S(2)}) collective-permute-start(f32[128,1152]{0,1:T(8,128)S(1)} %add.128), channel_id=1, source_target_pairs={{0,64},{64,0},{8,72},{72,8},{16,80},{80,16},{24,88},{88,24},{32,96... | collective-permute-start | bytes 1769480 | tf_op jit(solution)/shard_map/ppermute | solution.py:14
  612.2 12.1 %collective-permute-start.10 = (f32[128,1152]{0,1:T(8,128)S(1)}, f32[128,1152]{0,1:T(8,128)S(1)}, u32[]{:S(2)}, u32[]{:S(2)}) collective-permute-start(f32[128,1152]{0,1:T(8,128)S(1)} %constant_dynamic-update-slice_fusion.6), channel_id=1, source_target_pairs={{0,8},{8,0},{16,24},{24,16},{32,40},{40,32},{48,56},{56,48},{64,72... | collective-permute-start | bytes 1769480 | tf_op jit(solution)/shard_map/ppermute | solution.py:14
  624.4 14.8 %collective-permute-start.11 = (f32[128,1152]{0,1:T(8,128)S(1)}, f32[128,1152]{0,1:T(8,128)S(1)}, u32[]{:S(2)}, u32[]{:S(2)}) collective-permute-start(f32[128,1152]{0,1:T(8,128)S(1)} %add.132), channel_id=1, source_target_pairs={{0,16},{16,0},{8,24},{24,8},{32,48},{48,32},{40,56},{56,40},{64,80... | collective-permute-start | bytes 1769480 | tf_op jit(solution)/shard_map/ppermute | solution.py:14
  639.3 11.4 %collective-permute-start.12 = (f32[128,1152]{0,1:T(8,128)S(1)}, f32[128,1152]{0,1:T(8,128)S(1)}, u32[]{:S(2)}, u32[]{:S(2)}) collective-permute-start(f32[128,1152]{0,1:T(8,128)S(1)} %add.133), channel_id=1, source_target_pairs={{0,32},{32,0},{8,40},{40,8},{16,48},{48,16},{24,56},{56,24},{64,96... | collective-permute-start | bytes 1769480 | tf_op jit(solution)/shard_map/ppermute | solution.py:14
  650.7 26.6 %collective-permute-start.13 = (f32[128,1152]{0,1:T(8,128)S(1)}, f32[128,1152]{0,1:T(8,128)S(1)}, u32[]{:S(2)}, u32[]{:S(2)}) collective-permute-start(f32[128,1152]{0,1:T(8,128)S(1)} %add.134), channel_id=1, source_target_pairs={{0,64},{64,0},{8,72},{72,8},{16,80},{80,16},{24,88},{88,24},{32,96... | collective-permute-start | bytes 1769480 | tf_op jit(solution)/shard_map/ppermute | solution.py:14
  677.3 32.1 %collective-permute-start.14 = (f32[128,1152]{0,1:T(8,128)S(1)}, f32[128,1152]{0,1:T(8,128)}, u32[]{:S(2)}, u32[]{:S(2)}) collective-permute-start(f32[128,1152]{0,1:T(8,128)S(1)} %add.135), channel_id=1, source_target_pairs={{0,128},{128,0},{8,136},{136,8},{16,144},{144,16},{24,152},{152,24... | collective-permute-start | bytes 1769480 | tf_op jit(solution)/shard_map/ppermute | solution.py:14
  (6 other events, 10.7 us)
Sparse Core Ops, SparseCore 0:
  10.2 56.5 all-gather.1
  76.9 64.0 all-reduce.18
  163.7 69.0 all-reduce.16
  267.4 71.4 all-reduce.14
  388.5 74.1 all-reduce.12
  536.0 74.3 all-reduce.10
where the time goes:
time: 736 us; the launch traced here: 726 us
  waiting for transfers between devices  615 us (84%)
  matrix products  43.5 us (6%)
  starting transfers between devices  33.6 us (5%)
  between operations  14.5 us (2%)
  local copies, waits for them, and re-layouts  13.1 us (2%)
    psum x5, waiting for transfers between devices, shards(): proj, own_cap = lax.psum((proj_local, cap_local[level]), 'row')  354 us
    ppermute x15, waiting for transfers between devices, partner(): return lax.ppermute(block, axis, route)  206 us
    all_gather x1, waiting for transfers between devices, shards(): lax.all_gather(rhs_b, 'row', axis=0, tiled=True)  55.3 us
    ppermute x15, starting transfers between devices, partner(): return lax.ppermute(block, axis, route)  33.4 us
  transfers between devices with their start and end apart: 21, of which 21 were waited for; matrix products, arithmetic and copies ran while one was open for 0% of the time, Pallas kernels for 0%

commit v1 on v0

v1 whole, which is shorter than its diff:
```python
import jax
import jax.numpy as jnp
from jax import lax
from jax.experimental import pallas as pl
from jax.experimental.pallas import tpu as pltpu
from jax.sharding import PartitionSpec as P

Z, X, Y, C = 8, 4, 4, 2
LEVELS = 5
R = 128
BF = jnp.bfloat16
F32 = jnp.float32
FIRST = (0, 5, 9, 12, 14)
N_CAP = 15
H_FIRST = (0, 4, 7, 9)
N_H = 10
VMEM_LIMIT = 16 * 1024 * 1024
LEAF_VMEM_LIMIT = 52 * 1024 * 1024


def move(block, where):
    route = []
    for z in range(Z):
        for x in range(X):
            for y in range(Y):
                for c in range(C):
                    z1, x1, y1, c1 = where(z, x, y, c)
                    here = ((z * X + x) * Y + y) * C + c
                    there = ((z1 % Z * X + x1 % X) * Y + y1 % Y) * C + c1 % C
                    route.append((here, there))
    return lax.ppermute(block, ("partner", "row"), route)


def after(block, *others):
    return lax.optimization_barrier((block, *others))[0]


def to_core(block):
    return move(block, lambda z, x, y, c: (z, x, y, 1 - c))


def to_y(block, d):
    return move(block, lambda z, x, y, c: (z, x, y + d, c))


def to_x(block, mask):
    return move(block, lambda z, x, y, c: (z, x ^ mask, y, c))


def to_z(block, mask):
    return move(block, lambda z, x, y, c: (z ^ mask, x, y, c))


def dot(a, b):
    return jnp.dot(a, b, preferred_element_type=F32)


def split(a):
    upper = a.astype(BF)
    return upper, (a - upper.astype(F32)).astype(BF)


def dot_16_32(a, b):
    upper, lower = split(b)
    return dot(a, upper) + dot(a, lower)


def dot_32_32(a, b):
    a_upper, a_lower = split(a)
    b_upper, b_lower = split(b)
    return dot(a_upper, b_upper) + (dot(a_upper, b_lower) + dot(a_lower, b_upper))


def kernel_call(body, out_shape, n_scalar, n_in, scratch=(), name=None):
    smem = pl.BlockSpec(memory_space=pltpu.SMEM)
    vmem = pl.BlockSpec(memory_space=pltpu.VMEM)
    outs = out_shape if isinstance(out_shape, (tuple, list)) else (out_shape,)
    out_specs = [vmem] * len(outs)
    return pl.pallas_call(
        body,
        out_shape=out_shape,
        in_specs=[smem] * n_scalar + [vmem] * n_in,
        out_specs=out_specs if isinstance(out_shape, (tuple, list)) else vmem,
        scratch_shapes=list(scratch),
        compiler_params=pltpu.CompilerParams(vmem_limit_bytes=VMEM_LIMIT),
        name=name,
    )


def side_bits(upper, own, sib):
    return jnp.where(upper, sib, own), jnp.where(upper, own, sib)


def live_rhs_body(scalar_ref, rhs_ref, mine_ref, theirs_ref):
    first, c = scalar_ref[0], scalar_ref[1]
    rows, half = mine_ref.shape
    live = first + lax.broadcasted_iota(jnp.int32, (rows, 1), 0) < scalar_ref[2]
    for ref, core in ((mine_ref, c), (theirs_ref, 1 - c)):
        part = rhs_ref[:, pl.ds(pl.multiple_of(core * half, half), half)]
        ref[...] = jnp.where(live, part, 0.0).astype(BF)


def chip_body(scalar_ref, mine_ref, other_ref, chip_ref):
    c = scalar_ref[1]
    rows = mine_ref.shape[0]
    for ref, core in ((mine_ref, c), (other_ref, 1 - c)):
        chip_ref[pl.ds(pl.multiple_of(core * rows, rows), rows), :] = ref[...]


def halves_body(before_ref, behind_ref, top_ref, bottom_ref):
    rows = top_ref.shape[0]
    top_ref[...] = before_ref[:rows]
    bottom_ref[...] = behind_ref[rows:]


def prepare_body(scalar_ref, u_ref, v_ref, u_rows_ref, vt_ref, mine_ref, theirs_ref, cap_ref):
    rows = u_ref.shape[1]
    first, c = scalar_ref[0], scalar_ref[1]
    live = first + lax.broadcasted_iota(jnp.int32, (rows, 1), 0) < scalar_ref[2]
    for l in range(LEVELS):
        u_rows_ref[:, l * R : (l + 1) * R] = jnp.where(live, u_ref[l].astype(F32), 0.0).astype(BF)
        vt_ref[l * R : (l + 1) * R, :] = v_ref[l].T
    for l in range(LEVELS):
        cap = dot(vt_ref[l * R : (l + 1) * R, :], u_rows_ref[:, : (l + 1) * R])
        for m in range(l + 1):
            cap_ref[FIRST[m] + l - m] = cap[:, m * R : (m + 1) * R]
    half = R // 2
    mine_ref[...] = cap_ref[:, pl.ds(pl.multiple_of(c * half, half), half), :]
    theirs_ref[...] = cap_ref[:, pl.ds(pl.multiple_of((1 - c) * half, half), half), :]


def cap_parts_body(scalar_ref, mine_ref, other_ref, own_ref, *send_refs):
    y = scalar_ref[3]
    part = own_ref.shape[1]

    def at(d):
        return pl.ds(pl.multiple_of(((y + d) & (Y - 1)) * part, part), part)

    own_ref[...] = mine_ref[:, at(0), :] + other_ref[:, at(0), :]
    for d, ref in enumerate(send_refs):
        ref[...] = (mine_ref[:, at(d + 1), :] + other_ref[:, at(d + 1), :]).astype(BF)


def cap_leaf_body(own_ref, r1_ref, r2_ref, r3_ref, leaf_ref):
    leaf_ref[...] = (own_ref[...] + r1_ref[...].astype(F32)) + (
        r2_ref[...].astype(F32) + r3_ref[...].astype(F32)
    )


def cap_x_body(leaf_ref, r1_ref, r2_ref, r3_ref, low_ref, quad_ref):
    n0, n1 = FIRST[1], FIRST[2]
    low_ref[0, :n0] = leaf_ref[:n0].astype(BF)
    low_ref[1, :n0] = r1_ref[:n0].astype(BF)
    low_ref[0, n0:] = (leaf_ref[n0:n1] + r1_ref[n0:n1]).astype(BF)
    low_ref[1, n0:] = (r2_ref[n0:n1] + r3_ref[n0:n1]).astype(BF)
    quad_ref[...] = (leaf_ref[n1:] + r1_ref[n1:]) + (r2_ref[n1:] + r3_ref[n1:])


def cap_z_body(quad_ref, z1_ref, z2_ref, z3_ref, mid_ref, last_ref):
    n0, n1 = FIRST[3] - FIRST[2], FIRST[4] - FIRST[2]
    mid_ref[0, :n0] = quad_ref[:n0].astype(BF)
    mid_ref[1, :n0] = z1_ref[:n0].astype(BF)
    mid_ref[0, n0:] = (quad_ref[n0:n1] + z1_ref[n0:n1]).astype(BF)
    mid_ref[1, n0:] = (z2_ref[n0:n1] + z3_ref[n0:n1]).astype(BF)
    last_ref[...] = (quad_ref[n1:] + z1_ref[n1:]) + (z2_ref[n1:] + z3_ref[n1:])


def cap_both_body(low_ref, mid_ref, own4_ref, sib4_ref, both_ref):
    for side, last_ref in enumerate((own4_ref, sib4_ref)):
        at = side * N_CAP
        both_ref[at : at + FIRST[2]] = low_ref[side]
        both_ref[at + FIRST[2] : at + FIRST[4]] = mid_ref[side]
        both_ref[at + FIRST[4]] = last_ref[0].astype(BF)


def cap_stack_body(scalar_ref, b0_ref, b1_ref, b2_ref, b3_ref, out_ref):
    part = b0_ref.shape[1]
    for d, ref in enumerate((b0_ref, b1_ref, b2_ref, b3_ref)):
        at = ((scalar_ref[3] + d) & (Y - 1)) * part
        out_ref[:, pl.ds(pl.multiple_of(at, part), part), :] = ref[...]


def elimination_body(scalar_ref, side_ref, mine_ref, other_ref, g_ref, h_ref, diag_ref, all_ref):
    c = scalar_ref[1]
    half = R // 2
    all_ref[:, pl.ds(pl.multiple_of(c * half, half), half), :] = mine_ref[...]
    all_ref[:, pl.ds(pl.multiple_of((1 - c) * half, half), half), :] = other_ref[...]
    rows = lax.broadcasted_iota(jnp.int32, (R, R), 0)
    cols = lax.broadcasted_iota(jnp.int32, (R, R), 1)
    eye = (rows == cols).astype(F32)
    for m in range(LEVELS):
        upper = side_ref[m] == 1
        first = FIRST[m]
        c0, c1 = side_bits(upper, all_ref[first], all_ref[N_CAP + first])
        diag_ref[m, 0] = c0
        diag_ref[m, 1] = c1
        if m == LEVELS - 1:
            break
        g = g_ref[m]
        g_hi, g_lo = split(g)
        gc0 = dot(g_hi, c0) + dot(g_lo, c0)
        m1 = jnp.where(upper, -gc0, g)
        m0 = jnp.where(upper, eye, 0.0) - dot_16_32(c1, m1)
        m0_hi, m0_lo = split(m0)
        m1_hi, m1_lo = split(m1)
        for l in range(m + 1, LEVELS):
            j = first + l - m
            a0, a1 = side_bits(upper, all_ref[j], all_ref[N_CAP + j])
            h = dot(a0, m0_hi) + dot(a0, m0_lo) + dot(a1, m1_hi) + dot(a1, m1_lo)
            hi, lo = split(h)
            at = (H_FIRST[m] + l - m - 1) * R
            h_ref[at : at + R, 0:R] = hi
            h_ref[at : at + R, R : 2 * R] = lo


def leaf_body(n, final, scalar_ref, a_own_ref, a_oth_ref, *refs):
    refs = list(refs)
    if final:
        blocks, refs = [tuple(refs[:2])], refs[2:]
        sums, (va_ref, vb_ref) = refs[:2], refs[2:4]
        y_refs, q_refs = refs[4:6], refs[6:]
    else:
        blocks, y_refs = [(ref,) for ref in refs[:n]], refs[n:]
        sums = y_refs
    step = pl.program_id(0)
    for k, parts in enumerate(blocks):

        @pl.when(step == k)
        def _(k=k, parts=parts):
            for a_ref, total, y_ref in zip((a_own_ref, a_oth_ref), sums, y_refs):
                depth = a_ref.shape[1] // len(parts)
                new = None
                for j, part in enumerate(parts):
                    term = dot(a_ref[:, j * depth : (j + 1) * depth], part[...])
                    new = term if new is None else new + term
                y_ref[...] = new if k == 0 and not final else total[...] + new

    if final:
        rows = y_refs[0].shape[0]
        y, c, size = scalar_ref[n], scalar_ref[n + 1], scalar_ref[n + 2]
        iota = lax.broadcasted_iota(jnp.int32, (rows, 1), 0)
        for y_ref, core in zip(y_refs, (c, 1 - c)):
            y_ref[...] = jnp.where((y * C + core) * rows + iota < size, y_ref[...], 0.0)
        for d, q_ref in enumerate(q_refs):
            at = pl.ds(pl.multiple_of(((y + d) & (Y - 1)) * R, R), R)
            q = None
            for y_ref, v_ref in zip(y_refs, (va_ref, vb_ref)):
                hi, lo = split(y_ref[:, at])
                new = dot(v_ref[...], jnp.concatenate([hi, lo], axis=1))
                q = new if q is None else q + new
            q_ref[...] = (q[:, :R] + q[:, R:]).astype(BF)


def leaf(scalars, chips, a_own, a_oth, blocks, rest=()):
    rows = a_own.shape[0]
    half = blocks[0].shape[1]
    n = len(chips)
    final = len(rest) > 0
    whole2 = lambda i, scalar_ref: (0, 0)
    a_spec = pl.BlockSpec((rows, C * rows), lambda i, scalar_ref: (0, scalar_ref[i]))
    operands = [*blocks, *rest]
    out_shape = [jax.ShapeDtypeStruct((rows, half), F32)] * 2
    if final:
        out_shape += [jax.ShapeDtypeStruct((LEVELS * R, R), BF)] * Y
    return pl.pallas_call(
        lambda *refs: leaf_body(n, final, *refs),
        out_shape=out_shape,
        grid_spec=pltpu.PrefetchScalarGridSpec(
            num_scalar_prefetch=1,
            grid=(n,),
            in_specs=[a_spec, a_spec] + [pl.BlockSpec(o.shape, whole2) for o in operands],
            out_specs=[pl.BlockSpec(o.shape, whole2) for o in out_shape],
        ),
        compiler_params=pltpu.CompilerParams(vmem_limit_bytes=LEAF_VMEM_LIMIT),
        name="leaf",
    )(jnp.concatenate([jnp.stack(chips), scalars]), a_own, a_oth, *operands)


def eliminate_body(q0_ref, q1_ref, q2_ref, q3_ref, h_ref, e_ref, upper_ref):
    q = (q0_ref[...].astype(F32) + q1_ref[...].astype(F32)) + (
        q2_ref[...].astype(F32) + q3_ref[...].astype(F32)
    )
    for m in range(LEVELS):
        e = q[:R].astype(BF)
        e_ref[m * R : (m + 1) * R, :] = e
        if m > 0:
            upper_ref[(m - 1) * R : m * R, :] = e
        if m < LEVELS - 1:
            at, n = H_FIRST[m] * R, (LEVELS - 1 - m) * R
            q = q[R:] - dot(h_ref[at : at + n, :], jnp.concatenate([e, e], axis=0))


def solve(c0, c1, upper, own, sib, g):
    s0, s1 = side_bits(upper, own, sib)
    inner = s0 - dot_16_32(c0, s1)
    t1 = dot_32_32(g, inner)
    t0 = s1 - dot_16_32(c1, t1)
    return jnp.where(upper, t1, t0)


def solve_two_body(levels, side_ref, diag_ref, g_ref, a_ref, r1_ref, r2_ref, r3_ref, t_ref):
    low, high = levels
    one = slice(0, R)
    two = slice(R, 2 * R)
    t = solve(
        diag_ref[low, 0],
        diag_ref[low, 1],
        side_ref[low] == 1,
        a_ref[one].astype(F32),
        r1_ref[one].astype(F32),
        g_ref[low],
    )
    t_ref[one] = t.astype(BF)
    t = solve(
        diag_ref[high, 0],
        diag_ref[high, 1],
        side_ref[high] == 1,
        a_ref[two].astype(F32) + r1_ref[two].astype(F32),
        r2_ref[one].astype(F32) + r3_ref[one].astype(F32),
        g_ref[high],
    )
    t_ref[two] = t.astype(BF)


def quad_body(e_ref, r1_ref, r2_ref, r3_ref, quad_ref, upper_ref):
    two = slice(2 * R, 5 * R)
    quad = e_ref[two].astype(F32) + r1_ref[two].astype(F32)
    quad = quad + (r2_ref[R:].astype(F32) + r3_ref[R:].astype(F32))
    quad = quad.astype(BF)
    quad_ref[...] = quad
    upper_ref[...] = quad[R:]


def own4_body(quad_ref, z1_ref, z2_ref, z3_ref, own_ref):
    own = quad_ref[2 * R :].astype(F32) + z1_ref[2 * R :].astype(F32)
    own_ref[...] = (own + (z2_ref[R:].astype(F32) + z3_ref[R:].astype(F32))).astype(BF)


def solve_last_body(side_ref, diag_ref, g_ref, a_ref, r_ref, t01_ref, t23_ref, t_ref):
    last = LEVELS - 1
    t = solve(
        diag_ref[last, 0],
        diag_ref[last, 1],
        side_ref[last] == 1,
        a_ref[...].astype(F32),
        r_ref[...].astype(F32),
        g_ref[last],
    )
    t_ref[: 2 * R] = t01_ref[...]
    t_ref[2 * R : 4 * R] = t23_ref[...]
    t_ref[4 * R :] = t.astype(BF)


def columns_body(y_ref, *refs):
    ins, out_ref = refs[:-1], refs[-1]
    for d in range(Y):
        at = pl.ds(pl.multiple_of(((y_ref[0] + d) & (Y - 1)) * R, R), R)
        row = 0
        for ref in ins[d::Y]:
            out_ref[row : row + ref.shape[0], at] = ref[...]
            row += ref.shape[0]


def gather_y(block):
    return [block, to_y(block, -1), to_y(block, 2), to_y(block, 1)]


def gather_columns(y, *ts):
    blocks = [b for t in ts for b in gather_y(t)]
    rows = sum(t.shape[0] for t in ts)
    return kernel_call(
        columns_body, jax.ShapeDtypeStruct((rows, Y * R), BF), 1, len(blocks), name="columns"
    )(y[None], *blocks)


def update_body(c_ref, y_own_ref, y_oth_ref, u_ref, t_own_ref, t_oth_ref, out_ref, held, sems):
    rows, half = y_own_ref.shape
    tiles = sems.shape[0]
    tile = rows // tiles
    c = c_ref[0]
    copies = []
    for i in range(tiles):
        at_row = pl.ds(i * tile, tile)
        for y_ref, t_ref, core in ((y_own_ref, t_own_ref, c), (y_oth_ref, t_oth_ref, 1 - c)):
            at = pl.ds(pl.multiple_of(core * half, half), half)
            held[at_row, at] = y_ref[at_row, :] - dot(u_ref[at_row, :], t_ref[...])
        copy = pltpu.make_async_copy(held.at[at_row], out_ref.at[at_row], sems.at[i])
        copy.start()
        copies.append(copy)
    for copy in copies:
        copy.wait()


def update(c, y_own, y_oth, u, t_own, t_oth):
    rows, half = y_own.shape
    vmem = pl.BlockSpec(memory_space=pltpu.VMEM)
    return pl.pallas_call(
        update_body,
        out_shape=jax.ShapeDtypeStruct((rows, 2 * half), F32),
        in_specs=[pl.BlockSpec(memory_space=pltpu.SMEM)] + [vmem] * 5,
        out_specs=pl.BlockSpec(memory_space=pl.ANY),
        scratch_shapes=[pltpu.VMEM((rows, 2 * half), F32), pltpu.SemaphoreType.DMA((4,))],
        compiler_params=pltpu.CompilerParams(vmem_limit_bytes=VMEM_LIMIT),
        name="update",
    )(c[None], y_own, y_oth, u, t_own, t_oth)


def shards(rhs, leaf_inverse, leaf_sizes, u_tilde, v_right, cap_factor):
    rows, columns = rhs.shape
    row = lax.axis_index("row").astype(jnp.int32)
    partner = lax.axis_index("partner").astype(jnp.int32)
    y, c = row >> 1, row & 1
    side = (partner >> jnp.arange(LEVELS, dtype=jnp.int32)) & 1
    scalars = jnp.stack([row * rows, c, leaf_sizes[0], y])
    g = cap_factor[:, 0]
    struct = jax.ShapeDtypeStruct

    a_oth = to_core(leaf_inverse)
    part_shape = struct((rows, columns // C), BF)
    mine, theirs = kernel_call(live_rhs_body, (part_shape, part_shape), 1, 1, name="live_rhs")(
        scalars, rhs
    )
    other = to_core(theirs)

    half, part = R // 2, R // C // Y
    half_struct = struct((N_CAP, half, R), F32)
    u_rows, vt, cap_mine, cap_theirs = kernel_call(
        prepare_body,
        (
            struct((rows, LEVELS * R), BF),
            struct((LEVELS * R, rows), BF),
            half_struct,
            half_struct,
        ),
        1,
        2,
        scratch=[pltpu.VMEM((N_CAP, R, R), F32)],
        name="prepare",
    )(scalars, u_tilde, v_right)
    part_struct = struct((N_CAP, part, R), BF)
    own, s1, s2, s3 = kernel_call(
        cap_parts_body,
        (struct((N_CAP, part, R), F32), part_struct, part_struct, part_struct),
        1,
        2,
        name="cap_parts",
    )(scalars, cap_mine, to_core(cap_theirs))
    part1, part2, part3 = to_y(s1, 1), to_y(s2, 2), to_y(s3, 3)

    vt_oth = to_core(vt)
    chip = kernel_call(
        chip_body, struct((C * rows, columns // C), BF), 1, 2, name="chip"
    )(scalars, after(mine, part1, part2, part3, a_oth, vt_oth), other)
    before, behind = to_y(chip, 1), to_y(chip, -1)
    cap_leaf = kernel_call(cap_leaf_body, struct((N_CAP, part, R), F32), 0, 4, name="cap_leaf")(
        own, part1, part2, part3
    )
    low, cap_quad = kernel_call(
        cap_x_body,
        (struct((2, FIRST[2], part, R), BF), struct((N_CAP - FIRST[2], part, R), F32)),
        0,
        4,
        name="cap_x",
    )(cap_leaf, to_x(cap_leaf, 1), to_x(cap_leaf, 2), to_x(cap_leaf, 3))
    mid, last = kernel_call(
        cap_z_body,
        (struct((2, FIRST[4] - FIRST[2], part, R), BF), struct((1, part, R), F32)),
        0,
        4,
        name="cap_z",
    )(cap_quad, to_z(cap_quad, 1), to_z(cap_quad, 2), to_z(cap_quad, 3))
    both = kernel_call(
        cap_both_body, struct((2 * N_CAP, part, R), BF), 0, 4, name="cap_both"
    )(low, mid, last, to_z(last, 4))
    top, bottom = kernel_call(
        halves_body, (part_shape, part_shape), 0, 2, name="halves"
    )(after(before, both), behind)
    far_top, far_bottom = to_y(top, 1), to_y(bottom, -1)
    places = jnp.stack([y, c, leaf_sizes[0]])
    along = [(y + d) & (Y - 1) for d in range(Y)]
    sums = leaf(
        places, [along[0], along[3], along[1]], leaf_inverse, a_oth, [chip, before, behind]
    )
    both = after(both, top)
    cap_rows = kernel_call(
        cap_stack_body, struct((2 * N_CAP, half, R), BF), 1, 4, name="cap_stack"
    )(scalars, *gather_y(both))
    h, diag = kernel_call(
        elimination_body,
        (struct((N_H * R, 2 * R), BF), struct((LEVELS, 2, R, R), BF)),
        2,
        3,
        scratch=[pltpu.VMEM((2 * N_CAP, R, R), BF)],
        name="elimination",
    )(scalars, side, cap_rows, to_core(cap_rows), g)

    places = after(places, cap_rows)
    y_own, y_oth, *q = leaf(
        places, [along[2]], leaf_inverse, a_oth, [far_top, far_bottom], [*sums, vt, vt_oth]
    )
    y_other = to_core(y_oth)

    e, e_up = kernel_call(
        eliminate_body,
        (struct((LEVELS * R, R), BF), struct(((LEVELS - 1) * R, R), BF)),
        0,
        5,
        name="eliminate",
    )(q[0], to_y(q[1], 1), to_y(q[2], 2), to_y(q[3], 3), after(h, y_other))
    two = struct((2 * R, R), BF)
    r1, r2, r3 = to_x(e, 1), to_x(e_up, 2), to_x(e_up, 3)
    quad, quad_up = kernel_call(
        quad_body, (struct((3 * R, R), BF), struct((2 * R, R), BF)), 0, 4, name="quad"
    )(e, r1, r2, r3)
    z1, z2, z3 = to_z(quad, 1), to_z(quad_up, 2), to_z(quad_up, 3)
    t01 = kernel_call(
        lambda *refs: solve_two_body((0, 1), *refs), two, 1, 6, name="solve_0_1"
    )(side, diag, g, after(e, quad), r1, r2, r3)
    own4 = kernel_call(own4_body, struct((R, R), BF), 0, 4, name="own4")(quad, z1, z2, z3)
    sib4 = to_z(own4, 4)
    t23 = kernel_call(
        lambda *refs: solve_two_body((2, 3), *refs), two, 1, 6, name="solve_2_3"
    )(side, diag, g, after(quad, own4), z1, z2, z3)
    t = kernel_call(solve_last_body, struct((LEVELS * R, R), BF), 1, 6, name="solve_4")(
        side, diag, g, own4, sib4, t01, t23
    )
    t_own = gather_columns(y, t)
    t_oth = to_core(t_own)
    return update(c, y_own, y_other, u_rows, t_own, t_oth)


def solution(mesh):
    return jax.shard_map(
        shards,
        mesh=mesh,
        in_specs=(
            P(("partner", "row"), None),
            P(("partner", "row"), None),
            P("partner"),
            P(None, ("partner", "row"), None),
            P(None, ("partner", "row"), None),
            P(None, "partner", None, None),
        ),
        out_specs=P(("partner", "row"), None),
        check_vma=False,
    )
```

time: 736 us -> 137 us (0.19); the launches traced: 726 us -> 137 us
  waiting for transfers between devices: 615 us -> 36.7 us
  matrix products: 43.5 us -> 0 us
  Pallas kernels: 0 us -> 30.2 us
  starting transfers between devices: 33.6 us -> 61.1 us
  between operations: 14.5 us -> 1.14 us
    psum x5 -> x0, waiting for transfers between devices: 354 us -> none  [shards(): proj, own_cap = lax.psum((proj_local, cap_local[level]), 'row')]
    ppermute x15 -> x37, waiting for transfers between devices: 206 us -> 36.7 us  [move(): return lax.ppermute(block, ('partner', 'row'), route)]
    all_gather x1 -> x0, waiting for transfers between devices: 55.3 us -> none  [shards(): lax.all_gather(rhs_b, 'row', axis=0, tiled=True)]
    dot_general x37 -> x0, matrix products: 43.5 us -> none  [the longest x1 8.25 us: shards(): jnp.dot(leaf_inverse, lax.all_gather(rhs_b, 'row', axis=0, tiled=True), p...]
    pallas_call x0 -> x21, Pallas kernels: none -> 30.2 us  [the longest x2 15.1 us: leaf(): pl.pallas_call(lambda *refs: leaf_body(n, final, *refs), out_shape=out_sh...]
    ppermute x15 -> x37, starting transfers between devices: 33.4 us -> 61.1 us  [move(): return lax.ppermute(block, ('partner', 'row'), route)]
  transfers between devices with their start and end apart: 21 -> 37, of which waited for: 21 -> 19; matrix products, arithmetic and copies ran while one was open for 0% -> 0% of each run, Pallas kernels for 0% -> 12%
where the time goes in v1:
time: 137 us
  starting transfers between devices  61.1 us (45%)
  waiting for transfers between devices  36.7 us (27%)
  Pallas kernels  30.2 us (22%)
  local copies, waits for them, and re-layouts  7.32 us (5%)
    ppermute x37, starting transfers between devices, move(): return lax.ppermute(block, ('partner', 'row'), route)  61.1 us
    ppermute x37, waiting for transfers between devices, move(): return lax.ppermute(block, ('partner', 'row'), route)  36.7 us
    pallas_call x2, Pallas kernels, leaf(): pl.pallas_call(lambda *refs: leaf_body(n, final, *refs), out_shape=out_sh...  15.1 us
    unnamed x30, local copies, waits for them, and re-layouts  7.23 us
  transfers between devices with their start and end apart: 37, of which 19 were waited for; matrix products, arithmetic and copies ran while one was open for 0% of the time, Pallas kernels for 12%

profile of v1, /device:TPU:1, one launch (start us, length us, event | category | flops | bytes accessed | tf_op | source)
XLA Modules:
  0.0 136.6 jit_solution(1388454092214299585)
XLA Ops:
  0.0 3.2 %collective-permute-start.11 = (bf16[512,4096]{1,0:T(8,128)(2,1)}, bf16[512,4096]{1,0:T(8,128)(2,1)}, u32[]{:S(2)}, u32[]{:S(2)}) collective-permute-start(bf16[512,4096]{1,0:T(8,128)(2,1)} %refs_1_.3), channel_id=1, source_target_pairs={{0,1},{1,0},{2,3},{3,2},{4,5},{5,4},{6,7},{7,6},{8,9},{9,8},{10,11... | collective-permute-start | bytes 12582920 | tf_op jit(solution)/shard_map/ppermute | solution.py:31
  12.4 2.2 %collective-permute-start.2 = (bf16[15,16,128]{2,1,0:T(8,128)(2,1)S(1)}, bf16[15,16,128]{2,1,0:T(8,128)(2,1)S(1)}, u32[]{:S(2)}, u32[]{:S(2)}) collective-permute-start(bf16[15,16,128]{2,1,0:T(8,128)(2,1)S(1)} %get-tuple-element.46), channel_id=1, source_target_pairs={{0,4},{1,5},{2,6},{3,7},{4,0},{5,1},{6,2},{7,3},{8,12},{9,13},{10,... | collective-permute-start | bytes 184328 | tf_op jit(solution)/shard_map/ppermute | solution.py:31
  14.5 2.8 %collective-permute-done.1.r1_ref = bf16[15,16,128]{2,1,0:T(8,128)(2,1)S(1)} collective-permute-done((bf16[15,16,128]{2,1,0:T(8,128)(2,1)S(1)}, bf16[15,16,128]{2,1,0:T(8,128)(2,1)S(1)}, u32[]{:S(2)}, u32[]{:S(2)}) %collective-permute-start.1) | collective-permute-done | bytes 61472 | tf_op jit(solution)/shard_map/ppermute | solution.py:31
  18.0 2.4 %collective-permute-done.3.r3_ref = bf16[15,16,128]{2,1,0:T(8,128)(2,1)S(1)} collective-permute-done((bf16[15,16,128]{2,1,0:T(8,128)(2,1)S(1)}, bf16[15,16,128]{2,1,0:T(8,128)(2,1)S(1)}, u32[]{:S(2)}, u32[]{:S(2)}) %collective-permute-start.3) | collective-permute-done | bytes 61472 | tf_op jit(solution)/shard_map/ppermute | solution.py:31
  21.2 2.7 %collective-permute-start.15 = (bf16[1024,512]{1,0:T(8,128)(2,1)S(1)}, bf16[1024,512]{1,0:T(8,128)(2,1)S(1)}, u32[]{:S(2)}, u32[]{:S(2)}) collective-permute-start(bf16[1024,512]{1,0:T(8,128)(2,1)S(1)} %chip.1.refs_3_), channel_id=1, source_target_pairs={{0,6},{1,7},{2,0},{3,1},{4,2},{5,3},{6,4},{7,5},{8,14},{9,15},{10,... | collective-permute-start | bytes 3145736 | tf_op jit(solution)/shard_map/ppermute | solution.py:31
  25.5 2.3 %collective-permute-start.6 = (f32[15,16,128]{2,1,0:T(8,128)S(1)}, f32[15,16,128]{2,1,0:T(8,128)S(1)}, u32[]{:S(2)}, u32[]{:S(2)}) collective-permute-start(f32[15,16,128]{2,1,0:T(8,128)S(1)} %cap_leaf.1.leaf_ref), channel_id=1, source_target_pairs={{0,24},{1,25},{2,26},{3,27},{4,28},{5,29},{6,30},{7,31},{8,16},{9,... | collective-permute-start | bytes 368648 | tf_op jit(solution)/shard_map/ppermute | solution.py:31
  32.5 3.0 %collective-permute-start.8 = (f32[6,16,128]{2,1,0:T(8,128)S(1)}, f32[6,16,128]{2,1,0:T(8,128)S(1)}, u32[]{:S(2)}, u32[]{:S(2)}) collective-permute-start(f32[6,16,128]{2,1,0:T(8,128)S(1)} %get-tuple-element.49.quad_ref), channel_id=1, source_target_pairs={{0,64},{1,65},{2,66},{3,67},{4,68},{5,69},{6,70},{7,71},{8,72},{9,... | collective-permute-start | bytes 147464 | tf_op jit(solution)/shard_map/ppermute | solution.py:31
  35.5 2.3 %collective-permute-done.8.z2_ref = f32[6,16,128]{2,1,0:T(8,128)S(1)} collective-permute-done((f32[6,16,128]{2,1,0:T(8,128)S(1)}, f32[6,16,128]{2,1,0:T(8,128)S(1)}, u32[]{:S(2)}, u32[]{:S(2)}) %collective-permute-start.8) | collective-permute-done | bytes 49184 | tf_op jit(solution)/shard_map/ppermute | solution.py:31
  37.8 2.4 %collective-permute-done.9.z3_ref = f32[6,16,128]{2,1,0:T(8,128)S(1)} collective-permute-done((f32[6,16,128]{2,1,0:T(8,128)S(1)}, f32[6,16,128]{2,1,0:T(8,128)S(1)}, u32[]{:S(2)}, u32[]{:S(2)}) %collective-permute-start.9) | collective-permute-done | bytes 49184 | tf_op jit(solution)/shard_map/ppermute | solution.py:31
  40.3 4.3 %collective-permute-start.10 = (f32[1,16,128]{2,1,0:T(8,128)S(1)}, f32[1,16,128]{2,1,0:T(8,128)S(1)}, u32[]{:S(2)}, u32[]{:S(2)}) collective-permute-start(f32[1,16,128]{2,1,0:T(8,128)S(1)} %get-tuple-element.51.own4_ref), channel_id=1, source_target_pairs={{0,128},{1,129},{2,130},{3,131},{4,132},{5,133},{6,134},{7,135},{8... | collective-permute-start | bytes 24584 | tf_op jit(solution)/shard_map/ppermute | solution.py:31
  44.6 2.2 %collective-permute-done.10.sib4_ref = f32[1,16,128]{2,1,0:T(8,128)S(1)} collective-permute-done((f32[1,16,128]{2,1,0:T(8,128)S(1)}, f32[1,16,128]{2,1,0:T(8,128)S(1)}, u32[]{:S(2)}, u32[]{:S(2)}) %collective-permute-start.10) | collective-permute-done | bytes 8224 | tf_op jit(solution)/shard_map/ppermute | solution.py:31
  47.9 2.7 %collective-permute-start.20 = (bf16[512,512]{1,0:T(8,128)(2,1)}, bf16[512,512]{1,0:T(8,128)(2,1)}, u32[]{:S(2)}, u32[]{:S(2)}) collective-permute-start(bf16[512,512]{1,0:T(8,128)(2,1)} %get-tuple-element.60), channel_id=1, source_target_pairs={{0,6},{1,7},{2,0},{3,1},{4,2},{5,3},{6,4},{7,5},{8,14},{9,15},{10,... | collective-permute-start | bytes 1572872 | tf_op jit(solution)/shard_map/ppermute | solution.py:31
  52.3 8.1 %leaf.2 = (f32[512,512]{1,0:T(8,128)S(1)}, f32[512,512]{1,0:T(8,128)}) custom-call(s32[6]{0:T(128)S(1)} %concatenate.8.refs_0_, bf16[512,4096]{1,0:T(8,128)(2,1)} %refs_1_.3, bf16[512,4096]{1,0:T(8,128)(2,1)} %collective-permute-done.11.refs_2_, bf16[1024,512]{1,0:T(8,128)(2,1)} %copy-done.1, bf16[1024,512]{1,0:T(8,128)(2,1)} %copy-done.2, ...), custom_call_target="tpu_custom_call" | custom-call | tf_op jit(solution)/shard_map/leaf/pallas_call | solution.py:265
  62.5 7.0 %leaf.3 = (f32[512,512]{1,0:T(8,128)}, f32[512,512]{1,0:T(8,128)}, bf16[640,128]{1,0:T(8,128)(2,1)S(1)}, bf16[640,128]{1,0:T(8,128)(2,1)}, bf16[640,128]{1,0:T(8,128)(2,1)}, /*index=5*/bf16[640,128]{1,0:T(8,128)(2,1)}) custom-call(s32[4]{0:T(128)S(1)} %pad_add_fusion.2.refs_0_, bf16[512,4096]{1,0:T(8,128)(2,1)} %refs_1_.3, ...), custom_call_target="tpu_custom_call" | custom-call | tf_op jit(solution)/shard_map/leaf/pallas_call | solution.py:265
  70.1 8.6 %collective-permute-start.21 = (f32[512,512]{1,0:T(8,128)}, f32[512,512]{1,0:T(8,128)S(1)}, u32[]{:S(2)}, u32[]{:S(2)}) collective-permute-start(f32[512,512]{1,0:T(8,128)} %get-tuple-element.64), channel_id=1, source_target_pairs={{0,1},{1,0},{2,3},{3,2},{4,5},{5,4},{6,7},{7,6},{8,9},{9,8},{10,11... | collective-permute-start | bytes 3145736 | tf_op jit(solution)/shard_map/ppermute | solution.py:31
  82.6 2.1 %collective-permute-start.25 = (bf16[640,128]{1,0:T(8,128)(2,1)}, bf16[640,128]{1,0:T(8,128)(2,1)}, u32[]{:S(2)}, u32[]{:S(2)}) collective-permute-start(bf16[640,128]{1,0:T(8,128)(2,1)} %get-tuple-element.70), channel_id=1, source_target_pairs={{0,6},{1,7},{2,0},{3,1},{4,2},{5,3},{6,4},{7,5},{8,14},{9,15},{10,... | collective-permute-start | bytes 491528 | tf_op jit(solution)/shard_map/ppermute | solution.py:31
  84.7 2.4 %elimination.1 = (bf16[1280,256]{1,0:T(8,128)(2,1)S(1)}, bf16[5,2,128,128]{3,2,1,0:T(8,128)(2,1)S(1)}) custom-call(s32[4]{0:T(128)S(1)} %pad_add_fusion.1.scalar_ref, s32[5]{0:T(128)S(1)} %shift-right-arithmetic_and_fusion.side_ref.refs_0_, bf16[30,64,128]{2,1,0:T(8,128)(2,1)S(1)} %cap_stack.1.mine_ref, ...), custom_call_target="tpu_custom_call" | custom-call | tf_op jit(solution)/shard_map/elimination/pallas_call | solution.py:488
  87.1 3.4 %collective-permute-done.24.q2_ref = bf16[640,128]{1,0:T(8,128)(2,1)} collective-permute-done((bf16[640,128]{1,0:T(8,128)(2,1)}, bf16[640,128]{1,0:T(8,128)(2,1)}, u32[]{:S(2)}, u32[]{:S(2)}) %collective-permute-start.24) | collective-permute-done | bytes 163872 | tf_op jit(solution)/shard_map/ppermute | solution.py:31
  97.1 3.8 %collective-permute-done.27.r2_ref.refs_5_ = bf16[512,128]{1,0:T(8,128)(2,1)S(1)} collective-permute-done((bf16[512,128]{1,0:T(8,128)(2,1)S(1)}, bf16[512,128]{1,0:T(8,128)(2,1)S(1)}, u32[]{:S(2)}, u32[]{:S(2)}) %collective-permute-start.27) | collective-permute-done | bytes 131104 | tf_op jit(solution)/shard_map/ppermute | solution.py:31
  100.9 2.4 %collective-permute-done.28.r3_ref.refs_6_ = bf16[512,128]{1,0:T(8,128)(2,1)S(1)} collective-permute-done((bf16[512,128]{1,0:T(8,128)(2,1)S(1)}, bf16[512,128]{1,0:T(8,128)(2,1)S(1)}, u32[]{:S(2)}, u32[]{:S(2)}) %collective-permute-start.28) | collective-permute-done | bytes 131104 | tf_op jit(solution)/shard_map/ppermute | solution.py:31
  103.5 3.4 %collective-permute-start.31 = (bf16[256,128]{1,0:T(8,128)(2,1)S(1)}, bf16[256,128]{1,0:T(8,128)(2,1)S(1)}, u32[]{:S(2)}, u32[]{:S(2)}) collective-permute-start(bf16[256,128]{1,0:T(8,128)(2,1)S(1)} %get-tuple-element.76), channel_id=1, source_target_pairs={{0,96},{1,97},{2,98},{3,99},{4,100},{5,101},{6,102},{7,103},{8,104... | collective-permute-start | bytes 196616 | tf_op jit(solution)/shard_map/ppermute | solution.py:31
  109.5 5.2 %collective-permute-start.32 = (bf16[128,128]{1,0:T(8,128)(2,1)S(1)}, bf16[128,128]{1,0:T(8,128)(2,1)S(1)}, u32[]{:S(2)}, u32[]{:S(2)}) collective-permute-start(bf16[128,128]{1,0:T(8,128)(2,1)S(1)} %own4.1.a_ref), channel_id=1, source_target_pairs={{0,128},{1,129},{2,130},{3,131},{4,132},{5,133},{6,134},{7,135},{8... | collective-permute-start | bytes 98312 | tf_op jit(solution)/shard_map/ppermute | solution.py:31
  120.6 3.3 %collective-permute-done.33.refs_1_ = bf16[640,128]{1,0:T(8,128)(2,1)S(1)} collective-permute-done((bf16[640,128]{1,0:T(8,128)(2,1)S(1)}, bf16[640,128]{1,0:T(8,128)(2,1)S(1)}, u32[]{:S(2)}, u32[]{:S(2)}) %collective-permute-start.33) | collective-permute-done | bytes 163872 | tf_op jit(solution)/shard_map/ppermute | solution.py:31
  127.2 5.6 %collective-permute-start.36 = (bf16[640,512]{1,0:T(8,128)(2,1)S(1)}, bf16[640,512]{1,0:T(8,128)(2,1)S(1)}, u32[]{:S(2)}, u32[]{:S(2)}) collective-permute-start(bf16[640,512]{1,0:T(8,128)(2,1)S(1)} %columns.1.t_own_ref), channel_id=1, source_target_pairs={{0,1},{1,0},{2,3},{3,2},{4,5},{5,4},{6,7},{7,6},{8,9},{9,8},{10,11... | collective-permute-start | bytes 1966088 | tf_op jit(solution)/shard_map/ppermute | solution.py:31
  (106 shorter events, 47.7 us)
Async XLA Ops:
  0.0 20.4 %collective-permute-start.11 = (bf16[512,4096]{1,0:T(8,128)(2,1)}, bf16[512,4096]{1,0:T(8,128)(2,1)}, u32[]{:S(2)}, u32[]{:S(2)}) collective-permute-start(bf16[512,4096]{1,0:T(8,128)(2,1)} %refs_1_.3), channel_id=1, source_target_pairs={{0,1},{1,0},{2,3},{3,2},{4,5},{5,4},{6,7},{7,6},{8,9},{9,8},{10,11... | collective-permute-start | bytes 12582920 | tf_op jit(solution)/shard_map/ppermute | solution.py:31
  8.2 12.2 %collective-permute-start.12 = (bf16[640,512]{1,0:T(8,128)(2,1)S(1)}, bf16[640,512]{1,0:T(8,128)(2,1)S(1)}, u32[]{:S(2)}, u32[]{:S(2)}) collective-permute-start(bf16[640,512]{1,0:T(8,128)(2,1)S(1)} %get-tuple-element.53.refs_7_), channel_id=1, source_target_pairs={{0,1},{1,0},{2,3},{3,2},{4,5},{5,4},{6,7},{7,6},{8,9},{9,8},{10,11... | collective-permute-start | bytes 1966088 | tf_op jit(solution)/shard_map/ppermute | solution.py:31
  11.1 9.4 %collective-permute-start.13 = (bf16[512,512]{1,0:T(8,128)(2,1)S(1)}, bf16[512,512]{1,0:T(8,128)(2,1)S(1)}, u32[]{:S(2)}, u32[]{:S(2)}) collective-permute-start(bf16[512,512]{1,0:T(8,128)(2,1)S(1)} %get-tuple-element.55), channel_id=1, source_target_pairs={{0,1},{1,0},{2,3},{3,2},{4,5},{5,4},{6,7},{7,6},{8,9},{9,8},{10,11... | collective-permute-start | bytes 1572872 | tf_op jit(solution)/shard_map/ppermute | solution.py:31
  21.1 25.7 %collective-permute-start.14 = (bf16[1024,512]{1,0:T(8,128)(2,1)S(1)}, bf16[1024,512]{1,0:T(8,128)(2,1)S(1)}, u32[]{:S(2)}, u32[]{:S(2)}) collective-permute-start(bf16[1024,512]{1,0:T(8,128)(2,1)S(1)} %chip.1.refs_3_), channel_id=1, source_target_pairs={{0,2},{1,3},{2,4},{3,5},{4,6},{5,7},{6,0},{7,1},{8,10},{9,11},{10,... | collective-permute-start | bytes 3145736 | tf_op jit(solution)/shard_map/ppermute | solution.py:31
  21.2 25.7 %collective-permute-start.15 = (bf16[1024,512]{1,0:T(8,128)(2,1)S(1)}, bf16[1024,512]{1,0:T(8,128)(2,1)S(1)}, u32[]{:S(2)}, u32[]{:S(2)}) collective-permute-start(bf16[1024,512]{1,0:T(8,128)(2,1)S(1)} %chip.1.refs_3_), channel_id=1, source_target_pairs={{0,6},{1,7},{2,0},{3,1},{4,2},{5,3},{6,4},{7,5},{8,14},{9,15},{10,... | collective-permute-start | bytes 3145736 | tf_op jit(solution)/shard_map/ppermute | solution.py:31
  40.3 6.5 %collective-permute-start.10 = (f32[1,16,128]{2,1,0:T(8,128)S(1)}, f32[1,16,128]{2,1,0:T(8,128)S(1)}, u32[]{:S(2)}, u32[]{:S(2)}) collective-permute-start(f32[1,16,128]{2,1,0:T(8,128)S(1)} %get-tuple-element.51.own4_ref), channel_id=1, source_target_pairs={{0,128},{1,129},{2,130},{3,131},{4,132},{5,133},{6,134},{7,135},{8... | collective-permute-start | bytes 24584 | tf_op jit(solution)/shard_map/ppermute | solution.py:31
  47.9 14.5 %collective-permute-start.19 = (bf16[512,512]{1,0:T(8,128)(2,1)}, bf16[512,512]{1,0:T(8,128)(2,1)}, u32[]{:S(2)}, u32[]{:S(2)}) collective-permute-start(bf16[512,512]{1,0:T(8,128)(2,1)} %get-tuple-element.57), channel_id=1, source_target_pairs={{0,2},{1,3},{2,4},{3,5},{4,6},{5,7},{6,0},{7,1},{8,10},{9,11},{10,... | collective-permute-start | bytes 1572872 | tf_op jit(solution)/shard_map/ppermute | solution.py:31
  47.9 14.5 %collective-permute-start.20 = (bf16[512,512]{1,0:T(8,128)(2,1)}, bf16[512,512]{1,0:T(8,128)(2,1)}, u32[]{:S(2)}, u32[]{:S(2)}) collective-permute-start(bf16[512,512]{1,0:T(8,128)(2,1)} %get-tuple-element.60), channel_id=1, source_target_pairs={{0,6},{1,7},{2,0},{3,1},{4,2},{5,3},{6,4},{7,5},{8,14},{9,15},{10,... | collective-permute-start | bytes 1572872 | tf_op jit(solution)/shard_map/ppermute | solution.py:31
  50.6 10.8 %collective-permute-start.16 = (bf16[30,16,128]{2,1,0:T(8,128)(2,1)S(1)}, bf16[30,16,128]{2,1,0:T(8,128)(2,1)S(1)}, u32[]{:S(2)}, u32[]{:S(2)}) collective-permute-start(bf16[30,16,128]{2,1,0:T(8,128)(2,1)S(1)} %cap_both.1.b0_ref), channel_id=1, source_target_pairs={{0,6},{1,7},{2,0},{3,1},{4,2},{5,3},{6,4},{7,5},{8,14},{9,15},{10,... | collective-permute-start | bytes 368648 | tf_op jit(solution)/shard_map/ppermute | solution.py:31
  50.7 10.7 %collective-permute-start.17 = (bf16[30,16,128]{2,1,0:T(8,128)(2,1)S(1)}, bf16[30,16,128]{2,1,0:T(8,128)(2,1)S(1)}, u32[]{:S(2)}, u32[]{:S(2)}) collective-permute-start(bf16[30,16,128]{2,1,0:T(8,128)(2,1)S(1)} %cap_both.1.b0_ref), channel_id=1, source_target_pairs={{0,4},{1,5},{2,6},{3,7},{4,0},{5,1},{6,2},{7,3},{8,12},{9,13},{10,... | collective-permute-start | bytes 368648 | tf_op jit(solution)/shard_map/ppermute | solution.py:31
  51.2 10.2 %collective-permute-start.18 = (bf16[30,16,128]{2,1,0:T(8,128)(2,1)S(1)}, bf16[30,16,128]{2,1,0:T(8,128)(2,1)}, u32[]{:S(2)}, u32[]{:S(2)}) collective-permute-start(bf16[30,16,128]{2,1,0:T(8,128)(2,1)S(1)} %cap_both.1.b0_ref), channel_id=1, source_target_pairs={{0,2},{1,3},{2,4},{3,5},{4,6},{5,7},{6,0},{7,1},{8,10},{9,11},{10,... | collective-permute-start | bytes 368648 | tf_op jit(solution)/shard_map/ppermute | solution.py:31
  70.1 17.0 %collective-permute-start.21 = (f32[512,512]{1,0:T(8,128)}, f32[512,512]{1,0:T(8,128)S(1)}, u32[]{:S(2)}, u32[]{:S(2)}) collective-permute-start(f32[512,512]{1,0:T(8,128)} %get-tuple-element.64), channel_id=1, source_target_pairs={{0,1},{1,0},{2,3},{3,2},{4,5},{5,4},{6,7},{7,6},{8,9},{9,8},{10,11... | collective-permute-start | bytes 3145736 | tf_op jit(solution)/shard_map/ppermute | solution.py:31
  78.7 5.9 %collective-permute-start.22 = (bf16[30,64,128]{2,1,0:T(8,128)(2,1)S(1)}, bf16[30,64,128]{2,1,0:T(8,128)(2,1)S(1)}, u32[]{:S(2)}, u32[]{:S(2)}) collective-permute-start(bf16[30,64,128]{2,1,0:T(8,128)(2,1)S(1)} %cap_stack.1.mine_ref), channel_id=1, source_target_pairs={{0,1},{1,0},{2,3},{3,2},{4,5},{5,4},{6,7},{7,6},{8,9},{9,8},{10,11... | collective-permute-start | bytes 1474568 | tf_op jit(solution)/shard_map/ppermute | solution.py:31
  78.7 8.4 %collective-permute-start.23 = (bf16[640,128]{1,0:T(8,128)(2,1)}, bf16[640,128]{1,0:T(8,128)(2,1)}, u32[]{:S(2)}, u32[]{:S(2)}) collective-permute-start(bf16[640,128]{1,0:T(8,128)(2,1)} %get-tuple-element.68), channel_id=1, source_target_pairs={{0,2},{1,3},{2,4},{3,5},{4,6},{5,7},{6,0},{7,1},{8,10},{9,11},{10,... | collective-permute-start | bytes 491528 | tf_op jit(solution)/shard_map/ppermute | solution.py:31
  80.6 9.9 %collective-permute-start.24 = (bf16[640,128]{1,0:T(8,128)(2,1)}, bf16[640,128]{1,0:T(8,128)(2,1)}, u32[]{:S(2)}, u32[]{:S(2)}) collective-permute-start(bf16[640,128]{1,0:T(8,128)(2,1)} %get-tuple-element.69), channel_id=1, source_target_pairs={{0,4},{1,5},{2,6},{3,7},{4,0},{5,1},{6,2},{7,3},{8,12},{9,13},{10,... | collective-permute-start | bytes 491528 | tf_op jit(solution)/shard_map/ppermute | solution.py:31
  82.6 7.9 %collective-permute-start.25 = (bf16[640,128]{1,0:T(8,128)(2,1)}, bf16[640,128]{1,0:T(8,128)(2,1)}, u32[]{:S(2)}, u32[]{:S(2)}) collective-permute-start(bf16[640,128]{1,0:T(8,128)(2,1)} %get-tuple-element.70), channel_id=1, source_target_pairs={{0,6},{1,7},{2,0},{3,1},{4,2},{5,3},{6,4},{7,5},{8,14},{9,15},{10,... | collective-permute-start | bytes 491528 | tf_op jit(solution)/shard_map/ppermute | solution.py:31
  93.1 10.1 %collective-permute-start.26 = (bf16[640,128]{1,0:T(8,128)(2,1)S(1)}, bf16[640,128]{1,0:T(8,128)(2,1)S(1)}, u32[]{:S(2)}, u32[]{:S(2)}) collective-permute-start(bf16[640,128]{1,0:T(8,128)(2,1)S(1)} %get-tuple-element.77.e_ref.refs_3_), channel_id=1, source_target_pairs={{0,8},{1,9},{2,10},{3,11},{4,12},{5,13},{6,14},{7,15},{8,0},{9,1},... | collective-permute-start | bytes 491528 | tf_op jit(solution)/shard_map/ppermute | solution.py:31
  93.2 7.6 %collective-permute-start.27 = (bf16[512,128]{1,0:T(8,128)(2,1)S(1)}, bf16[512,128]{1,0:T(8,128)(2,1)S(1)}, u32[]{:S(2)}, u32[]{:S(2)}) collective-permute-start(bf16[512,128]{1,0:T(8,128)(2,1)S(1)} %get-tuple-element.74), channel_id=1, source_target_pairs={{0,16},{1,17},{2,18},{3,19},{4,20},{5,21},{6,22},{7,23},{8,24},{9,... | collective-permute-start | bytes 393224 | tf_op jit(solution)/shard_map/ppermute | solution.py:31
  95.2 8.1 %collective-permute-start.28 = (bf16[512,128]{1,0:T(8,128)(2,1)S(1)}, bf16[512,128]{1,0:T(8,128)(2,1)S(1)}, u32[]{:S(2)}, u32[]{:S(2)}) collective-permute-start(bf16[512,128]{1,0:T(8,128)(2,1)S(1)} %get-tuple-element.74), channel_id=1, source_target_pairs={{0,24},{1,25},{2,26},{3,27},{4,28},{5,29},{6,30},{7,31},{8,16},{9,... | collective-permute-start | bytes 393224 | tf_op jit(solution)/shard_map/ppermute | solution.py:31
  103.3 6.2 %collective-permute-start.29 = (bf16[384,128]{1,0:T(8,128)(2,1)S(1)}, bf16[384,128]{1,0:T(8,128)(2,1)S(1)}, u32[]{:S(2)}, u32[]{:S(2)}) collective-permute-start(bf16[384,128]{1,0:T(8,128)(2,1)S(1)} %get-tuple-element.78.quad_ref.refs_3_), channel_id=1, source_target_pairs={{0,32},{1,33},{2,34},{3,35},{4,36},{5,37},{6,38},{7,39},{8,40},{9,... | collective-permute-start | bytes 294920 | tf_op jit(solution)/shard_map/ppermute | solution.py:31
  103.5 6.0 %collective-permute-start.31 = (bf16[256,128]{1,0:T(8,128)(2,1)S(1)}, bf16[256,128]{1,0:T(8,128)(2,1)S(1)}, u32[]{:S(2)}, u32[]{:S(2)}) collective-permute-start(bf16[256,128]{1,0:T(8,128)(2,1)S(1)} %get-tuple-element.76), channel_id=1, source_target_pairs={{0,96},{1,97},{2,98},{3,99},{4,100},{5,101},{6,102},{7,103},{8,104... | collective-permute-start | bytes 196616 | tf_op jit(solution)/shard_map/ppermute | solution.py:31
  109.5 7.7 %collective-permute-start.32 = (bf16[128,128]{1,0:T(8,128)(2,1)S(1)}, bf16[128,128]{1,0:T(8,128)(2,1)S(1)}, u32[]{:S(2)}, u32[]{:S(2)}) collective-permute-start(bf16[128,128]{1,0:T(8,128)(2,1)S(1)} %own4.1.a_ref), channel_id=1, source_target_pairs={{0,128},{1,129},{2,130},{3,131},{4,132},{5,133},{6,134},{7,135},{8... | collective-permute-start | bytes 98312 | tf_op jit(solution)/shard_map/ppermute | solution.py:31
  119.9 7.1 %collective-permute-start.35 = (bf16[640,128]{1,0:T(8,128)(2,1)S(1)}, bf16[640,128]{1,0:T(8,128)(2,1)S(1)}, u32[]{:S(2)}, u32[]{:S(2)}) collective-permute-start(bf16[640,128]{1,0:T(8,128)(2,1)S(1)} %solve_4.1.refs_0_), channel_id=1, source_target_pairs={{0,2},{1,3},{2,4},{3,5},{4,6},{5,7},{6,0},{7,1},{8,10},{9,11},{10,... | collective-permute-start | bytes 491528 | tf_op jit(solution)/shard_map/ppermute | solution.py:31
  127.2 7.4 %collective-permute-start.36 = (bf16[640,512]{1,0:T(8,128)(2,1)S(1)}, bf16[640,512]{1,0:T(8,128)(2,1)S(1)}, u32[]{:S(2)}, u32[]{:S(2)}) collective-permute-start(bf16[640,512]{1,0:T(8,128)(2,1)S(1)} %columns.1.t_own_ref), channel_id=1, source_target_pairs={{0,1},{1,0},{2,3},{3,2},{4,5},{5,4},{6,7},{7,6},{8,9},{9,8},{10,11... | collective-permute-start | bytes 1966088 | tf_op jit(solution)/shard_map/ppermute | solution.py:31
  (28 other events, 318.2 us)

commit v2 on v1

--- a/solution.py
+++ b/solution.py
@@ -15,7 +15,6 @@
 H_FIRST = (0, 4, 7, 9)
 N_H = 10
 VMEM_LIMIT = 16 * 1024 * 1024
-LEAF_VMEM_LIMIT = 52 * 1024 * 1024
 
 
 def move(block, where):
@@ -33,6 +32,10 @@
 
 def after(block, *others):
     return lax.optimization_barrier((block, *others))[0]
+
+
+def in_hbm(block):
+    return pltpu.with_memory_space_constraint(block, pltpu.HBM)
 
 
 def to_core(block):
@@ -91,13 +94,40 @@
     return jnp.where(upper, sib, own), jnp.where(upper, own, sib)
 
 
-def live_rhs_body(scalar_ref, rhs_ref, mine_ref, theirs_ref):
+def live_rhs_body(scalar_ref, rhs_hbm, mine_ref, theirs_ref, rhs_ref, sems):
     first, c = scalar_ref[0], scalar_ref[1]
     rows, half = mine_ref.shape
-    live = first + lax.broadcasted_iota(jnp.int32, (rows, 1), 0) < scalar_ref[2]
-    for ref, core in ((mine_ref, c), (theirs_ref, 1 - c)):
-        part = rhs_ref[:, pl.ds(pl.multiple_of(core * half, half), half)]
-        ref[...] = jnp.where(live, part, 0.0).astype(BF)
+    tiles = sems.shape[0]
+    tile = rows // tiles
+    spans = [pl.ds(i * tile, tile) for i in range(tiles)]
+    loads = [
+        pltpu.make_async_copy(rhs_hbm.at[at], rhs_ref.at[at], sems.at[i])
+        for i, at in enumerate(spans)
+    ]
+    for load in loads:
+        load.start()
+    iota = lax.broadcasted_iota(jnp.int32, (tile, 1), 0)
+    for i, (load, at) in enumerate(zip(loads, spans)):
+        load.wait()
+        live = first + i * tile + iota < scalar_ref[2]
+        for ref, core in ((mine_ref, c), (theirs_ref, 1 - c)):
+            part = rhs_ref[at, pl.ds(pl.multiple_of(core * half, half), half)]
+            ref[at, :] = jnp.where(live, part, 0.0).astype(BF)
+
+
+def live_rhs(scalars, rhs):
+    rows, columns = rhs.shape
+    vmem = pl.BlockSpec(memory_space=pltpu.VMEM)
+    out = jax.ShapeDtypeStruct((rows, columns // C), BF)
+    return pl.pallas_call(
+        live_rhs_body,
+        out_shape=(out, out),
+        in_specs=[pl.BlockSpec(memory_space=pltpu.SMEM), pl.BlockSpec(memory_space=pltpu.HBM)],
+        out_specs=(vmem, vmem),
+        scratch_shapes=[pltpu.VMEM(rhs.shape, F32), pltpu.SemaphoreType.DMA((4,))],
+        compiler_params=pltpu.CompilerParams(vmem_limit_bytes=VMEM_LIMIT),
+        name="live_rhs",
+    )(scalars, rhs)
 
 
 def chip_body(scalar_ref, mine_ref, other_ref, chip_ref):
@@ -113,20 +143,67 @@
     bottom_ref[...] = behind_ref[rows:]
 
 
-def prepare_body(scalar_ref, u_ref, v_ref, u_rows_ref, vt_ref, mine_ref, theirs_ref, cap_ref):
+def prepare_body(
+    scalar_ref,
+    u_hbm,
+    v_hbm,
+    vt_ref,
+    mine_ref,
+    theirs_ref,
+    u_ref,
+    v_ref,
+    rows_ref,
+    cap_ref,
+    sems,
+):
+    loads = [
+        pltpu.make_async_copy(u_hbm, u_ref, sems.at[0]),
+        pltpu.make_async_copy(v_hbm, v_ref, sems.at[1]),
+    ]
+    for load in loads:
+        load.start()
     rows = u_ref.shape[1]
     first, c = scalar_ref[0], scalar_ref[1]
     live = first + lax.broadcasted_iota(jnp.int32, (rows, 1), 0) < scalar_ref[2]
+    loads[0].wait()
     for l in range(LEVELS):
-        u_rows_ref[:, l * R : (l + 1) * R] = jnp.where(live, u_ref[l].astype(F32), 0.0).astype(BF)
+        rows_ref[:, l * R : (l + 1) * R] = jnp.where(live, u_ref[l].astype(F32), 0.0).astype(BF)
+    loads[1].wait()
+    for l in range(LEVELS):
         vt_ref[l * R : (l + 1) * R, :] = v_ref[l].T
     for l in range(LEVELS):
-        cap = dot(vt_ref[l * R : (l + 1) * R, :], u_rows_ref[:, : (l + 1) * R])
+        cap = dot(vt_ref[l * R : (l + 1) * R, :], rows_ref[:, : (l + 1) * R])
         for m in range(l + 1):
             cap_ref[FIRST[m] + l - m] = cap[:, m * R : (m + 1) * R]
     half = R // 2
     mine_ref[...] = cap_ref[:, pl.ds(pl.multiple_of(c * half, half), half), :]
     theirs_ref[...] = cap_ref[:, pl.ds(pl.multiple_of((1 - c) * half, half), half), :]
+
+
+def prepare(scalars, u, v):
+    levels, rows, _ = u.shape
+    half = jax.ShapeDtypeStruct((N_CAP, R // 2, R), F32)
+    hbm = pl.BlockSpec(memory_space=pltpu.HBM)
+    vmem = pl.BlockSpec(memory_space=pltpu.VMEM)
+    return pl.pallas_call(
+        prepare_body,
+        out_shape=(
+            jax.ShapeDtypeStruct((levels * R, rows), BF),
+            half,
+            half,
+        ),
+        in_specs=[pl.BlockSpec(memory_space=pltpu.SMEM), hbm, hbm],
+        out_specs=(vmem, vmem, vmem),
+        scratch_shapes=[
+            pltpu.VMEM(u.shape, BF),
+            pltpu.VMEM(v.shape, BF),
+            pltpu.VMEM((rows, levels * R), BF),
+            pltpu.VMEM((N_CAP, R, R), F32),
+            pltpu.SemaphoreType.DMA((2,)),
+        ],
+        compiler_params=pltpu.CompilerParams(vmem_limit_bytes=VMEM_LIMIT),
+        name="prepare",
+    )(scalars, u, v)
 
 
 def cap_parts_body(scalar_ref, mine_ref, other_ref, own_ref, *send_refs):
@@ -213,67 +290,78 @@
             h_ref[at : at + R, R : 2 * R] = lo
 
 
-def leaf_body(n, final, scalar_ref, a_own_ref, a_oth_ref, *refs):
-    refs = list(refs)
-    if final:
-        blocks, refs = [tuple(refs[:2])], refs[2:]
-        sums, (va_ref, vb_ref) = refs[:2], refs[2:4]
-        y_refs, q_refs = refs[4:6], refs[6:]
-    else:
-        blocks, y_refs = [(ref,) for ref in refs[:n]], refs[n:]
-        sums = y_refs
-    step = pl.program_id(0)
-    for k, parts in enumerate(blocks):
-
-        @pl.when(step == k)
-        def _(k=k, parts=parts):
-            for a_ref, total, y_ref in zip((a_own_ref, a_oth_ref), sums, y_refs):
-                depth = a_ref.shape[1] // len(parts)
-                new = None
-                for j, part in enumerate(parts):
-                    term = dot(a_ref[:, j * depth : (j + 1) * depth], part[...])
-                    new = term if new is None else new + term
-                y_ref[...] = new if k == 0 and not final else total[...] + new
-
-    if final:
-        rows = y_refs[0].shape[0]
-        y, c, size = scalar_ref[n], scalar_ref[n + 1], scalar_ref[n + 2]
-        iota = lax.broadcasted_iota(jnp.int32, (rows, 1), 0)
-        for y_ref, core in zip(y_refs, (c, 1 - c)):
-            y_ref[...] = jnp.where((y * C + core) * rows + iota < size, y_ref[...], 0.0)
-        for d, q_ref in enumerate(q_refs):
-            at = pl.ds(pl.multiple_of(((y + d) & (Y - 1)) * R, R), R)
-            q = None
-            for y_ref, v_ref in zip(y_refs, (va_ref, vb_ref)):
-                hi, lo = split(y_ref[:, at])
-                new = dot(v_ref[...], jnp.concatenate([hi, lo], axis=1))
-                q = new if q is None else q + new
-            q_ref[...] = (q[:, :R] + q[:, R:]).astype(BF)
-
-
-def leaf(scalars, chips, a_own, a_oth, blocks, rest=()):
+def leaf_body(
+    chip_ref, a0_hbm, a1_hbm, b0_ref, b1_ref, b2_ref, sum0, sum1, far0, far1, buffers, sems
+):
+    depth = b0_ref.shape[0]
+    loads = []
+    for k in range(Y):
+        at = pl.ds(pl.multiple_of(chip_ref[k] * depth, depth), depth)
+        for i, (a_hbm, far) in enumerate(((a0_hbm, far0), (a1_hbm, far1))):
+            to = far if k == Y - 1 else buffers.at[k, i]
+            loads.append(pltpu.make_async_copy(a_hbm.at[:, at], to, sems.at[k, i]))
+    for load in loads:
+        load.start()
+    for k, block in enumerate((b0_ref, b1_ref, b2_ref)):
+        for i, total in enumerate((sum0, sum1)):
+            loads[2 * k + i].wait()
+            new = dot(buffers[k, i], block[...])
+            total[...] = new if k == 0 else total[...] + new
+    for load in loads[2 * (Y - 1) :]:
+        load.wait()
+
+
+def leaf(chips, a_own, a_oth, blocks):
     rows = a_own.shape[0]
-    half = blocks[0].shape[1]
-    n = len(chips)
-    final = len(rest) > 0
-    whole2 = lambda i, scalar_ref: (0, 0)
-    a_spec = pl.BlockSpec((rows, C * rows), lambda i, scalar_ref: (0, scalar_ref[i]))
-    operands = [*blocks, *rest]
+    depth, half = blocks[0].shape
+    vmem = pl.BlockSpec(memory_space=pltpu.VMEM)
+    hbm = pl.BlockSpec(memory_space=pltpu.HBM)
     out_shape = [jax.ShapeDtypeStruct((rows, half), F32)] * 2
-    if final:
-        out_shape += [jax.ShapeDtypeStruct((LEVELS * R, R), BF)] * Y
+    out_shape += [jax.ShapeDtypeStruct((rows, depth), BF)] * 2
     return pl.pallas_call(
-        lambda *refs: leaf_body(n, final, *refs),
+        leaf_body,
         out_shape=out_shape,
-        grid_spec=pltpu.PrefetchScalarGridSpec(
-            num_scalar_prefetch=1,
-            grid=(n,),
-            in_specs=[a_spec, a_spec] + [pl.BlockSpec(o.shape, whole2) for o in operands],
-            out_specs=[pl.BlockSpec(o.shape, whole2) for o in out_shape],
-        ),
-        compiler_params=pltpu.CompilerParams(vmem_limit_bytes=LEAF_VMEM_LIMIT),
+        in_specs=[pl.BlockSpec(memory_space=pltpu.SMEM), hbm, hbm] + [vmem] * 3,
+        out_specs=[vmem] * 4,
+        scratch_shapes=[
+            pltpu.VMEM((Y - 1, 2, rows, depth), BF),
+            pltpu.SemaphoreType.DMA((Y, 2)),
+        ],
+        compiler_params=pltpu.CompilerParams(vmem_limit_bytes=VMEM_LIMIT),
         name="leaf",
-    )(jnp.concatenate([jnp.stack(chips), scalars]), a_own, a_oth, *operands)
+    )(jnp.stack(chips), a_own, a_oth, *blocks)
+
+
+def project(block, y_refs, v_refs):
+    at = pl.ds(pl.multiple_of((block & (Y - 1)) * R, R), R)
+    q = None
+    for y_ref, v_ref in zip(y_refs, v_refs):
+        hi, lo = split(y_ref[:, at])
+        new = dot(v_ref[...], jnp.concatenate([hi, lo], axis=1))
+        q = new if q is None else q + new
+    return (q[:, :R] + q[:, R:]).astype(BF)
+
+
+def leaf_end_body(
+    scalar_ref, a0_ref, a1_ref, top_ref, bottom_ref, sum0_ref, sum1_ref, va_ref, vb_ref, *out_refs
+):
+    y_refs, q_refs = out_refs[:2], out_refs[2:]
+    rows = y_refs[0].shape[0]
+    y, c, size = scalar_ref[0], scalar_ref[1], scalar_ref[2]
+    iota = lax.broadcasted_iota(jnp.int32, (rows, 1), 0)
+    far = jnp.concatenate([top_ref[...], bottom_ref[...]], axis=0)
+    for a_ref, sum_ref, y_ref, core in zip(
+        (a0_ref, a1_ref), (sum0_ref, sum1_ref), y_refs, (c, 1 - c)
+    ):
+        new = dot(a_ref[...], far)
+        live = (y * C + core) * rows + iota < size
+        y_ref[...] = jnp.where(live, sum_ref[...] + new, 0.0)
+    for d, q_ref in enumerate(q_refs):
+        q_ref[...] = project(y + d + 1, y_refs, (va_ref, vb_ref))
+
+
+def project_own_body(place_ref, y0_ref, y1_ref, va_ref, vb_ref, q_ref):
+    q_ref[...] = project(place_ref[0], (y0_ref, y1_ref), (va_ref, vb_ref))
 
 
 def eliminate_body(q0_ref, q1_ref, q2_ref, q3_ref, h_ref, e_ref, upper_ref):
@@ -351,47 +439,70 @@
     t_ref[4 * R :] = t.astype(BF)
 
 
-def columns_body(y_ref, *refs):
-    ins, out_ref = refs[:-1], refs[-1]
-    for d in range(Y):
-        at = pl.ds(pl.multiple_of(((y_ref[0] + d) & (Y - 1)) * R, R), R)
-        row = 0
-        for ref in ins[d::Y]:
-            out_ref[row : row + ref.shape[0], at] = ref[...]
-            row += ref.shape[0]
+def columns_body(y_ref, b0_ref, b1_ref, b2_ref, b3_ref, out_ref):
+    for d, ref in enumerate((b0_ref, b1_ref, b2_ref, b3_ref)):
+        at = ((y_ref[0] + d) & (Y - 1)) * R
+        out_ref[:, pl.ds(pl.multiple_of(at, R), R)] = ref[...]
 
 
 def gather_y(block):
     return [block, to_y(block, -1), to_y(block, 2), to_y(block, 1)]
 
 
-def gather_columns(y, *ts):
-    blocks = [b for t in ts for b in gather_y(t)]
-    rows = sum(t.shape[0] for t in ts)
-    return kernel_call(
-        columns_body, jax.ShapeDtypeStruct((rows, Y * R), BF), 1, len(blocks), name="columns"
-    )(y[None], *blocks)
-
-
-def update_body(c_ref, y_own_ref, y_oth_ref, u_ref, t_own_ref, t_oth_ref, out_ref, held, sems):
-    rows, half = y_own_ref.shape
+def put_columns(y, blocks):
+    out = jax.ShapeDtypeStruct((blocks[0].shape[0], Y * R), BF)
+    return kernel_call(columns_body, out, 1, Y, name="columns")(y[None], *blocks)
+
+
+def bring_body(*refs):
+    n = (len(refs) - 1) // 2
+    sems = refs[-1]
+    copies = [
+        pltpu.make_async_copy(refs[i], refs[n + i], sems.at[i]) for i in range(n)
+    ]
+    for copy in copies:
+        copy.start()
+    for copy in copies:
+        copy.wait()
+
+
+def bring(*arrays):
+    n = len(arrays)
+    size = sum(a.size * a.dtype.itemsize for a in arrays)
+    return pl.pallas_call(
+        bring_body,
+        out_shape=[jax.ShapeDtypeStruct(a.shape, a.dtype) for a in arrays],
+        in_specs=[pl.BlockSpec(memory_space=pltpu.HBM)] * n,
+        out_specs=[pl.BlockSpec(memory_space=pltpu.VMEM)] * n,
+        scratch_shapes=[pltpu.SemaphoreType.DMA((n,))],
+        compiler_params=pltpu.CompilerParams(vmem_limit_bytes=VMEM_LIMIT),
+        cost_estimate=pl.CostEstimate(flops=0, bytes_accessed=2 * size, transcendentals=0),
+        name="bring",
+    )(*[in_hbm(a) for a in arrays])
+
+
+def update_body(scalar_ref, y0_ref, y1_ref, u_ref, t0_ref, t1_ref, out_hbm, held, sems):
+    rows, half = y0_ref.shape
     tiles = sems.shape[0]
     tile = rows // tiles
-    c = c_ref[0]
+    first, c, size = scalar_ref[0], scalar_ref[1], scalar_ref[2]
+    iota = lax.broadcasted_iota(jnp.int32, (tile, 1), 0)
     copies = []
     for i in range(tiles):
         at_row = pl.ds(i * tile, tile)
-        for y_ref, t_ref, core in ((y_own_ref, t_own_ref, c), (y_oth_ref, t_oth_ref, 1 - c)):
+        u = jnp.concatenate([u_ref[l, at_row, :] for l in range(LEVELS)], axis=1)
+        live = first + i * tile + iota < size
+        for y_ref, t_ref, core in ((y0_ref, t0_ref, c), (y1_ref, t1_ref, 1 - c)):
             at = pl.ds(pl.multiple_of(core * half, half), half)
-            held[at_row, at] = y_ref[at_row, :] - dot(u_ref[at_row, :], t_ref[...])
-        copy = pltpu.make_async_copy(held.at[at_row], out_ref.at[at_row], sems.at[i])
+            held[at_row, at] = y_ref[at_row, :] - jnp.where(live, dot(u, t_ref[...]), 0.0)
+        copy = pltpu.make_async_copy(held.at[at_row], out_hbm.at[at_row], sems.at[i])
         copy.start()
         copies.append(copy)
     for copy in copies:
         copy.wait()
 
 
-def update(c, y_own, y_oth, u, t_own, t_oth):
+def update(scalars, y_own, y_oth, u, t_own, t_oth):
     rows, half = y_own.shape
     vmem = pl.BlockSpec(memory_space=pltpu.VMEM)
     return pl.pallas_call(
@@ -402,7 +513,7 @@
         scratch_shapes=[pltpu.VMEM((rows, 2 * half), F32), pltpu.SemaphoreType.DMA((4,))],
         compiler_params=pltpu.CompilerParams(vmem_limit_bytes=VMEM_LIMIT),
         name="update",
-    )(c[None], y_own, y_oth, u, t_own, t_oth)
+    )(scalars, y_own, y_oth, u, t_own, t_oth)
 
 
 def shards(rhs, leaf_inverse, leaf_sizes, u_tilde, v_right, cap_factor):
@@ -417,26 +528,11 @@
 
     a_oth = to_core(leaf_inverse)
     part_shape = struct((rows, columns // C), BF)
-    mine, theirs = kernel_call(live_rhs_body, (part_shape, part_shape), 1, 1, name="live_rhs")(
-        scalars, rhs
-    )
+    mine, theirs = live_rhs(scalars, in_hbm(rhs))
     other = to_core(theirs)
 
     half, part = R // 2, R // C // Y
-    half_struct = struct((N_CAP, half, R), F32)
-    u_rows, vt, cap_mine, cap_theirs = kernel_call(
-        prepare_body,
-        (
-            struct((rows, LEVELS * R), BF),
-            struct((LEVELS * R, rows), BF),
-            half_struct,
-            half_struct,
-        ),
-        1,
-        2,
-        scratch=[pltpu.VMEM((N_CAP, R, R), F32)],
-        name="prepare",
-    )(scalars, u_tilde, v_right)
+    vt, cap_mine, cap_theirs = prepare(scalars, in_hbm(u_tilde), in_hbm(v_right))
     part_struct = struct((N_CAP, part, R), BF)
     own, s1, s2, s3 = kernel_call(
         cap_parts_body,
@@ -450,8 +546,8 @@
     vt_oth = to_core(vt)
     chip = kernel_call(
         chip_body, struct((C * rows, columns // C), BF), 1, 2, name="chip"
-    )(scalars, after(mine, part1, part2, part3, a_oth, vt_oth), other)
-    before, behind = to_y(chip, 1), to_y(chip, -1)
+    )(scalars, after(mine, part1, a_oth, vt_oth), other)
+    before, behind = to_y(chip, 1), to_y(after(chip, part2, part3), -1)
     cap_leaf = kernel_call(cap_leaf_body, struct((N_CAP, part, R), F32), 0, 4, name="cap_leaf")(
         own, part1, part2, part3
     )
@@ -478,8 +574,11 @@
     far_top, far_bottom = to_y(top, 1), to_y(bottom, -1)
     places = jnp.stack([y, c, leaf_sizes[0]])
     along = [(y + d) & (Y - 1) for d in range(Y)]
-    sums = leaf(
-        places, [along[0], along[3], along[1]], leaf_inverse, a_oth, [chip, before, behind]
+    sum_own, sum_oth, far_own, far_oth = leaf(
+        [along[0], along[3], along[1], along[2]],
+        in_hbm(leaf_inverse),
+        in_hbm(a_oth),
+        [chip, before, behind],
     )
     both = after(both, top)
     cap_rows = kernel_call(
@@ -495,9 +594,16 @@
     )(scalars, side, cap_rows, to_core(cap_rows), g)
 
     places = after(places, cap_rows)
-    y_own, y_oth, *q = leaf(
-        places, [along[2]], leaf_inverse, a_oth, [far_top, far_bottom], [*sums, vt, vt_oth]
-    )
+    y_own, y_oth, *q = kernel_call(
+        leaf_end_body,
+        [struct((rows, columns // C), F32)] * 2 + [struct((LEVELS * R, R), BF)] * (Y - 1),
+        1,
+        8,
+        name="leaf_end",
+    )(places, far_own, far_oth, far_top, far_bottom, sum_own, sum_oth, vt, vt_oth)
+    q_own = kernel_call(
+        project_own_body, struct((LEVELS * R, R), BF), 1, 4, name="project_own"
+    )(places, y_own, y_oth, vt, vt_oth)
     y_other = to_core(y_oth)
 
     e, e_up = kernel_call(
@@ -506,7 +612,7 @@
         0,
         5,
         name="eliminate",
-    )(q[0], to_y(q[1], 1), to_y(q[2], 2), to_y(q[3], 3), after(h, y_other))
+    )(q_own, to_y(q[0], 1), to_y(q[1], 2), to_y(q[2], 3), after(h, y_other))
     two = struct((2 * R, R), BF)
     r1, r2, r3 = to_x(e, 1), to_x(e_up, 2), to_x(e_up, 3)
     quad, quad_up = kernel_call(
@@ -516,7 +622,9 @@
     t01 = kernel_call(
         lambda *refs: solve_two_body((0, 1), *refs), two, 1, 6, name="solve_0_1"
     )(side, diag, g, after(e, quad), r1, r2, r3)
-    own4 = kernel_call(own4_body, struct((R, R), BF), 0, 4, name="own4")(quad, z1, z2, z3)
+    own4 = kernel_call(own4_body, struct((R, R), BF), 0, 4, name="own4")(
+        after(quad, t01), z1, z2, z3
+    )
     sib4 = to_z(own4, 4)
     t23 = kernel_call(
         lambda *refs: solve_two_body((2, 3), *refs), two, 1, 6, name="solve_2_3"
@@ -524,9 +632,9 @@
     t = kernel_call(solve_last_body, struct((LEVELS * R, R), BF), 1, 6, name="solve_4")(
         side, diag, g, own4, sib4, t01, t23
     )
-    t_own = gather_columns(y, t)
+    t_own = put_columns(y, gather_y(t))
     t_oth = to_core(t_own)
-    return update(c, y_own, y_other, u_rows, t_own, t_oth)
+    return update(scalars, *bring(y_own, y_other, u_tilde), t_own, t_oth)
 
 
 def solution(mesh):

time: 137 us -> 130 us (0.949)
  local copies, waits for them, and re-layouts: 7.32 us -> 0.03 us
  Pallas kernels: 30.2 us -> 31.9 us
  starting transfers between devices: 61.1 us -> 59.5 us
    unnamed x30 -> x16, local copies, waits for them, and re-layouts: 7.23 us -> 0.03 us
    ppermute x37, starting transfers between devices: 61.1 us -> 59.5 us  [move(): return lax.ppermute(block, ('partner', 'row'), route)]
    pallas_call x5 -> x7, Pallas kernels: 17.1 us -> 18.2 us  [the longest x1 5.63 us: leaf(): pl.pallas_call(leaf_body, out_shape=out_shape, in_specs=[pl.BlockSpec(mem...]
  transfers between devices with their start and end apart: 37 -> 37, of which waited for: 19 -> 20; matrix products, arithmetic and copies ran while one was open for 0% -> 0% of each run, Pallas kernels for 12% -> 16%
where the time goes in v2:
time: 130 us
  starting transfers between devices  59.5 us (46%)
  waiting for transfers between devices  36.7 us (28%)
  Pallas kernels  31.9 us (25%)
    ppermute x37, starting transfers between devices, move(): return lax.ppermute(block, ('partner', 'row'), route)  59.5 us
    ppermute x37, waiting for transfers between devices, move(): return lax.ppermute(block, ('partner', 'row'), route)  36.7 us
    pallas_call x1, Pallas kernels, leaf(): pl.pallas_call(leaf_body, out_shape=out_shape, in_specs=[pl.BlockSpec(mem...  5.63 us
    pallas_call x1, Pallas kernels, shards(): kernel_call(leaf_end_body, [struct((rows, columns // C), F32)] * 2 + [str...  4.38 us
    pallas_call x1, Pallas kernels, shards(): kernel_call(elimination_body, (struct((N_H * R, 2 * R), BF), struct((LEVE...  2.92 us
  transfers between devices with their start and end apart: 37, of which 20 were waited for; matrix products, arithmetic and copies ran while one was open for 0% of the time, Pallas kernels for 16%

profile of v2, /device:TPU:1, one launch (start us, length us, event | category | flops | bytes accessed | tf_op | source)
XLA Modules:
  0.0 129.5 jit_solution(7773601769086030368)
XLA Ops:
  0.0 3.2 %collective-permute-start.11 = (bf16[512,4096]{1,0:T(8,128)(2,1)}, bf16[512,4096]{1,0:T(8,128)(2,1)}, u32[]{:S(2)}, u32[]{:S(2)}) collective-permute-start(bf16[512,4096]{1,0:T(8,128)(2,1)} %a0_hbm.1), channel_id=1, source_target_pairs={{0,1},{1,0},{2,3},{3,2},{4,5},{5,4},{6,7},{7,6},{8,9},{9,8},{10,11... | collective-permute-start | bytes 12582920 | tf_op jit(solution)/shard_map/ppermute | solution.py:30
  4.0 2.4 %prepare.1 = (bf16[640,512]{1,0:T(8,128)(2,1)S(1)}, f32[15,64,128]{2,1,0:T(8,128)S(1)}, f32[15,64,128]{2,1,0:T(8,128)S(1)}) custom-call(s32[4]{0:T(128)S(1)} %pad_add_fusion.scalar_ref, bf16[5,512,128]{2,1,0:T(8,128)(2,1)} %refs_2_.1, bf16[5,512,128]{2,1,0:T(8,128)(2,1)} %v_hbm.1), custom_call_target="tpu_custom_call" | custom-call | tf_op jit(solution)/shard_map/prepare/pallas_call | solution.py:188
  9.3 2.3 %collective-permute-done.other_ref = f32[15,64,128]{2,1,0:T(8,128)S(1)} collective-permute-done((f32[15,64,128]{2,1,0:T(8,128)S(1)}, f32[15,64,128]{2,1,0:T(8,128)S(1)}, u32[]{:S(2)}, u32[]{:S(2)}) %collective-permute-start) | collective-permute-done | bytes 491552 | tf_op jit(solution)/shard_map/ppermute | solution.py:30
  12.4 2.2 %collective-permute-start.2 = (bf16[15,16,128]{2,1,0:T(8,128)(2,1)S(1)}, bf16[15,16,128]{2,1,0:T(8,128)(2,1)S(1)}, u32[]{:S(2)}, u32[]{:S(2)}) collective-permute-start(bf16[15,16,128]{2,1,0:T(8,128)(2,1)S(1)} %get-tuple-element.51), channel_id=1, source_target_pairs={{0,4},{1,5},{2,6},{3,7},{4,0},{5,1},{6,2},{7,3},{8,12},{9,13},{10,... | collective-permute-start | bytes 184328 | tf_op jit(solution)/shard_map/ppermute | solution.py:30
  14.5 2.8 %collective-permute-done.1.r1_ref = bf16[15,16,128]{2,1,0:T(8,128)(2,1)S(1)} collective-permute-done((bf16[15,16,128]{2,1,0:T(8,128)(2,1)S(1)}, bf16[15,16,128]{2,1,0:T(8,128)(2,1)S(1)}, u32[]{:S(2)}, u32[]{:S(2)}) %collective-permute-start.1) | collective-permute-done | bytes 61472 | tf_op jit(solution)/shard_map/ppermute | solution.py:30
  28.9 4.1 %collective-permute-start.9 = (f32[6,16,128]{2,1,0:T(8,128)S(1)}, f32[6,16,128]{2,1,0:T(8,128)S(1)}, u32[]{:S(2)}, u32[]{:S(2)}) collective-permute-start(f32[6,16,128]{2,1,0:T(8,128)S(1)} %get-tuple-element.54.quad_ref), channel_id=1, source_target_pairs={{0,96},{1,97},{2,98},{3,99},{4,100},{5,101},{6,102},{7,103},{8,104... | collective-permute-start | bytes 147464 | tf_op jit(solution)/shard_map/ppermute | solution.py:30
  34.5 2.7 %collective-permute-done.8.z2_ref = f32[6,16,128]{2,1,0:T(8,128)S(1)} collective-permute-done((f32[6,16,128]{2,1,0:T(8,128)S(1)}, f32[6,16,128]{2,1,0:T(8,128)S(1)}, u32[]{:S(2)}, u32[]{:S(2)}) %collective-permute-start.8) | collective-permute-done | bytes 49184 | tf_op jit(solution)/shard_map/ppermute | solution.py:30
  37.2 4.6 %collective-permute-start.10 = (f32[1,16,128]{2,1,0:T(8,128)S(1)}, f32[1,16,128]{2,1,0:T(8,128)S(1)}, u32[]{:S(2)}, u32[]{:S(2)}) collective-permute-start(f32[1,16,128]{2,1,0:T(8,128)S(1)} %get-tuple-element.56.own4_ref), channel_id=1, source_target_pairs={{0,128},{1,129},{2,130},{3,131},{4,132},{5,133},{6,134},{7,135},{8... | collective-permute-start | bytes 24584 | tf_op jit(solution)/shard_map/ppermute | solution.py:30
  46.3 3.2 %collective-permute-start.17 = (bf16[30,16,128]{2,1,0:T(8,128)(2,1)S(1)}, bf16[30,16,128]{2,1,0:T(8,128)(2,1)S(1)}, u32[]{:S(2)}, u32[]{:S(2)}) collective-permute-start(bf16[30,16,128]{2,1,0:T(8,128)(2,1)S(1)} %cap_both.1.b0_ref), channel_id=1, source_target_pairs={{0,4},{1,5},{2,6},{3,7},{4,0},{5,1},{6,2},{7,3},{8,12},{9,13},{10,... | collective-permute-start | bytes 368648 | tf_op jit(solution)/shard_map/ppermute | solution.py:30
  49.7 5.6 %leaf.1 = (f32[512,512]{1,0:T(8,128)S(1)}, f32[512,512]{1,0:T(8,128)S(1)}, bf16[512,1024]{1,0:T(8,128)(2,1)S(1)}, bf16[512,1024]{1,0:T(8,128)(2,1)S(1)}) custom-call(s32[4]{0:T(128)S(1)} %pad_add_fusion.2.chip_ref, bf16[512,4096]{1,0:T(8,128)(2,1)} %a0_hbm.1, bf16[512,4096]{1,0:T(8,128)(2,1)} %collective-permute-done.11.a1_hbm, ...), custom_call_target="tpu_custom_call" | custom-call | tf_op jit(solution)/shard_map/leaf/pallas_call | solution.py:321
  55.4 3.4 %collective-permute-done.18.b3_ref = bf16[30,16,128]{2,1,0:T(8,128)(2,1)S(1)} collective-permute-done((bf16[30,16,128]{2,1,0:T(8,128)(2,1)S(1)}, bf16[30,16,128]{2,1,0:T(8,128)(2,1)S(1)}, u32[]{:S(2)}, u32[]{:S(2)}) %collective-permute-start.18) | collective-permute-done | bytes 122912 | tf_op jit(solution)/shard_map/ppermute | solution.py:30
  59.8 4.4 %leaf_end.1 = (f32[512,512]{1,0:T(8,128)S(1)}, f32[512,512]{1,0:T(8,128)}, bf16[640,128]{1,0:T(8,128)(2,1)}, bf16[640,128]{1,0:T(8,128)(2,1)}, bf16[640,128]{1,0:T(8,128)(2,1)}) custom-call(s32[3]{0:T(128)S(1)} %pad_add_fusion.1.scalar_ref.place_ref, bf16[512,1024]{1,0:T(8,128)(2,1)S(1)} %get-tuple-element.66.a0_ref, ...), custom_call_target="tpu_custom_call" | custom-call | tf_op jit(solution)/shard_map/leaf_end/pallas_call | solution.py:597
  64.2 8.0 %collective-permute-start.21 = (f32[512,512]{1,0:T(8,128)}, f32[512,512]{1,0:T(8,128)}, u32[]{:S(2)}, u32[]{:S(2)}) collective-permute-start(f32[512,512]{1,0:T(8,128)} %get-tuple-element.72.y1_ref), channel_id=1, source_target_pairs={{0,1},{1,0},{2,3},{3,2},{4,5},{5,4},{6,7},{7,6},{8,9},{9,8},{10,11... | collective-permute-start | bytes 3145736 | tf_op jit(solution)/shard_map/ppermute | solution.py:30
  77.0 2.9 %elimination.1 = (bf16[1280,256]{1,0:T(8,128)(2,1)S(1)}, bf16[5,2,128,128]{3,2,1,0:T(8,128)(2,1)S(1)}) custom-call(s32[4]{0:T(128)S(1)} %pad_add_fusion.scalar_ref, s32[5]{0:T(128)S(1)} %shift-right-arithmetic_and_fusion.side_ref.refs_0_, bf16[30,64,128]{2,1,0:T(8,128)(2,1)S(1)} %cap_stack.1.mine_ref, ...), custom_call_target="tpu_custom_call" | custom-call | tf_op jit(solution)/shard_map/elimination/pallas_call | solution.py:587
  80.0 2.6 %collective-permute-done.23.q1_ref = bf16[640,128]{1,0:T(8,128)(2,1)S(1)} collective-permute-done((bf16[640,128]{1,0:T(8,128)(2,1)}, bf16[640,128]{1,0:T(8,128)(2,1)S(1)}, u32[]{:S(2)}, u32[]{:S(2)}) %collective-permute-start.23) | collective-permute-done | bytes 163872 | tf_op jit(solution)/shard_map/ppermute | solution.py:30
  89.7 3.4 %collective-permute-done.27.r2_ref.refs_5_ = bf16[512,128]{1,0:T(8,128)(2,1)S(1)} collective-permute-done((bf16[512,128]{1,0:T(8,128)(2,1)S(1)}, bf16[512,128]{1,0:T(8,128)(2,1)S(1)}, u32[]{:S(2)}, u32[]{:S(2)}) %collective-permute-start.27) | collective-permute-done | bytes 131104 | tf_op jit(solution)/shard_map/ppermute | solution.py:30
  94.9 2.8 %collective-permute-start.31 = (bf16[256,128]{1,0:T(8,128)(2,1)S(1)}, bf16[256,128]{1,0:T(8,128)(2,1)S(1)}, u32[]{:S(2)}, u32[]{:S(2)}) collective-permute-start(bf16[256,128]{1,0:T(8,128)(2,1)S(1)} %get-tuple-element.87), channel_id=1, source_target_pairs={{0,96},{1,97},{2,98},{3,99},{4,100},{5,101},{6,102},{7,103},{8,104... | collective-permute-start | bytes 196616 | tf_op jit(solution)/shard_map/ppermute | solution.py:30
  100.3 2.8 %collective-permute-done.30.z2_ref.refs_5_ = bf16[256,128]{1,0:T(8,128)(2,1)S(1)} collective-permute-done((bf16[256,128]{1,0:T(8,128)(2,1)S(1)}, bf16[256,128]{1,0:T(8,128)(2,1)S(1)}, u32[]{:S(2)}, u32[]{:S(2)}) %collective-permute-start.30) | collective-permute-done | bytes 65568 | tf_op jit(solution)/shard_map/ppermute | solution.py:30
  103.2 4.6 %collective-permute-start.32 = (bf16[128,128]{1,0:T(8,128)(2,1)S(1)}, bf16[128,128]{1,0:T(8,128)(2,1)S(1)}, u32[]{:S(2)}, u32[]{:S(2)}) collective-permute-start(bf16[128,128]{1,0:T(8,128)(2,1)S(1)} %own4.1.a_ref), channel_id=1, source_target_pairs={{0,128},{1,129},{2,130},{3,131},{4,132},{5,133},{6,134},{7,135},{8... | collective-permute-start | bytes 98312 | tf_op jit(solution)/shard_map/ppermute | solution.py:30
  111.0 3.2 %collective-permute-start.35 = (bf16[640,128]{1,0:T(8,128)(2,1)S(1)}, bf16[640,128]{1,0:T(8,128)(2,1)S(1)}, u32[]{:S(2)}, u32[]{:S(2)}) collective-permute-start(bf16[640,128]{1,0:T(8,128)(2,1)S(1)} %solve_4.1.b0_ref), channel_id=1, source_target_pairs={{0,2},{1,3},{2,4},{3,5},{4,6},{5,7},{6,0},{7,1},{8,10},{9,11},{10,... | collective-permute-start | bytes 491528 | tf_op jit(solution)/shard_map/ppermute | solution.py:30
  114.1 2.2 %collective-permute-start.34 = (bf16[640,128]{1,0:T(8,128)(2,1)S(1)}, bf16[640,128]{1,0:T(8,128)(2,1)S(1)}, u32[]{:S(2)}, u32[]{:S(2)}) collective-permute-start(bf16[640,128]{1,0:T(8,128)(2,1)S(1)} %solve_4.1.b0_ref), channel_id=1, source_target_pairs={{0,4},{1,5},{2,6},{3,7},{4,0},{5,1},{6,2},{7,3},{8,12},{9,13},{10,... | collective-permute-start | bytes 491528 | tf_op jit(solution)/shard_map/ppermute | solution.py:30
  117.9 3.1 %collective-permute-done.34.b2_ref = bf16[640,128]{1,0:T(8,128)(2,1)S(1)} collective-permute-done((bf16[640,128]{1,0:T(8,128)(2,1)S(1)}, bf16[640,128]{1,0:T(8,128)(2,1)S(1)}, u32[]{:S(2)}, u32[]{:S(2)}) %collective-permute-start.34) | collective-permute-done | bytes 163872 | tf_op jit(solution)/shard_map/ppermute | solution.py:30
  121.4 3.9 %collective-permute-start.36 = (bf16[640,512]{1,0:T(8,128)(2,1)S(1)}, bf16[640,512]{1,0:T(8,128)(2,1)S(1)}, u32[]{:S(2)}, u32[]{:S(2)}) collective-permute-start(bf16[640,512]{1,0:T(8,128)(2,1)S(1)} %columns.1.t0_ref), channel_id=1, source_target_pairs={{0,1},{1,0},{2,3},{3,2},{4,5},{5,4},{6,7},{7,6},{8,9},{9,8},{10,11... | collective-permute-start | bytes 1966088 | tf_op jit(solution)/shard_map/ppermute | solution.py:30
  127.0 2.4 %update.1 = f32[512,1024]{1,0:T(8,128)} custom-call(s32[4]{0:T(128)S(1)} %pad_add_fusion.scalar_ref, f32[512,512]{1,0:T(8,128)S(1)} %get-tuple-element.73.y0_ref, f32[512,512]{1,0:T(8,128)S(1)} %get-tuple-element.74.y1_ref, bf16[5,512,128]{2,1,0:T(8,128)(2,1)S(1)} %get-tuple-element.75.u_ref, bf16[640,512]{1,0:T(8,128)(2,1)S(1)} %columns.1.t0_ref, ...), custom_call_target="tpu_custom_call" | custom-call | tf_op jit(solution)/shard_map/update/pallas_call | solution.py:508
  (93 shorter events, 45.6 us)
Async XLA Ops:
  0.0 17.4 %collective-permute-start.11 = (bf16[512,4096]{1,0:T(8,128)(2,1)}, bf16[512,4096]{1,0:T(8,128)(2,1)}, u32[]{:S(2)}, u32[]{:S(2)}) collective-permute-start(bf16[512,4096]{1,0:T(8,128)(2,1)} %a0_hbm.1), channel_id=1, source_target_pairs={{0,1},{1,0},{2,3},{3,2},{4,5},{5,4},{6,7},{7,6},{8,9},{9,8},{10,11... | collective-permute-start | bytes 12582920 | tf_op jit(solution)/shard_map/ppermute | solution.py:30
  6.4 10.9 %collective-permute-start.12 = (bf16[640,512]{1,0:T(8,128)(2,1)S(1)}, bf16[640,512]{1,0:T(8,128)(2,1)S(1)}, u32[]{:S(2)}, u32[]{:S(2)}) collective-permute-start(bf16[640,512]{1,0:T(8,128)(2,1)S(1)} %get-tuple-element.58.va_ref), channel_id=1, source_target_pairs={{0,1},{1,0},{2,3},{3,2},{4,5},{5,4},{6,7},{7,6},{8,9},{9,8},{10,11... | collective-permute-start | bytes 1966088 | tf_op jit(solution)/shard_map/ppermute | solution.py:30
  9.1 8.2 %collective-permute-start.13 = (bf16[512,512]{1,0:T(8,128)(2,1)S(1)}, bf16[512,512]{1,0:T(8,128)(2,1)S(1)}, u32[]{:S(2)}, u32[]{:S(2)}) collective-permute-start(bf16[512,512]{1,0:T(8,128)(2,1)S(1)} %get-tuple-element.60), channel_id=1, source_target_pairs={{0,1},{1,0},{2,3},{3,2},{4,5},{5,4},{6,7},{7,6},{8,9},{9,8},{10,11... | collective-permute-start | bytes 1572872 | tf_op jit(solution)/shard_map/ppermute | solution.py:30
  12.4 7.2 %collective-permute-start.2 = (bf16[15,16,128]{2,1,0:T(8,128)(2,1)S(1)}, bf16[15,16,128]{2,1,0:T(8,128)(2,1)S(1)}, u32[]{:S(2)}, u32[]{:S(2)}) collective-permute-start(bf16[15,16,128]{2,1,0:T(8,128)(2,1)S(1)} %get-tuple-element.51), channel_id=1, source_target_pairs={{0,4},{1,5},{2,6},{3,7},{4,0},{5,1},{6,2},{7,3},{8,12},{9,13},{10,... | collective-permute-start | bytes 184328 | tf_op jit(solution)/shard_map/ppermute | solution.py:30
  18.0 25.8 %collective-permute-start.14 = (bf16[1024,512]{1,0:T(8,128)(2,1)S(1)}, bf16[1024,512]{1,0:T(8,128)(2,1)S(1)}, u32[]{:S(2)}, u32[]{:S(2)}) collective-permute-start(bf16[1024,512]{1,0:T(8,128)(2,1)S(1)} %chip.1.b0_ref), channel_id=1, source_target_pairs={{0,2},{1,3},{2,4},{3,5},{4,6},{5,7},{6,0},{7,1},{8,10},{9,11},{10,... | collective-permute-start | bytes 3145736 | tf_op jit(solution)/shard_map/ppermute | solution.py:30
  20.4 23.4 %collective-permute-start.15 = (bf16[1024,512]{1,0:T(8,128)(2,1)S(1)}, bf16[1024,512]{1,0:T(8,128)(2,1)S(1)}, u32[]{:S(2)}, u32[]{:S(2)}) collective-permute-start(bf16[1024,512]{1,0:T(8,128)(2,1)S(1)} %chip.1.b0_ref), channel_id=1, source_target_pairs={{0,6},{1,7},{2,0},{3,1},{4,2},{5,3},{6,4},{7,5},{8,14},{9,15},{10,... | collective-permute-start | bytes 3145736 | tf_op jit(solution)/shard_map/ppermute | solution.py:30
  28.9 5.6 %collective-permute-start.9 = (f32[6,16,128]{2,1,0:T(8,128)S(1)}, f32[6,16,128]{2,1,0:T(8,128)S(1)}, u32[]{:S(2)}, u32[]{:S(2)}) collective-permute-start(f32[6,16,128]{2,1,0:T(8,128)S(1)} %get-tuple-element.54.quad_ref), channel_id=1, source_target_pairs={{0,96},{1,97},{2,98},{3,99},{4,100},{5,101},{6,102},{7,103},{8,104... | collective-permute-start | bytes 147464 | tf_op jit(solution)/shard_map/ppermute | solution.py:30
  37.2 6.6 %collective-permute-start.10 = (f32[1,16,128]{2,1,0:T(8,128)S(1)}, f32[1,16,128]{2,1,0:T(8,128)S(1)}, u32[]{:S(2)}, u32[]{:S(2)}) collective-permute-start(f32[1,16,128]{2,1,0:T(8,128)S(1)} %get-tuple-element.56.own4_ref), channel_id=1, source_target_pairs={{0,128},{1,129},{2,130},{3,131},{4,132},{5,133},{6,134},{7,135},{8... | collective-permute-start | bytes 24584 | tf_op jit(solution)/shard_map/ppermute | solution.py:30
  44.8 14.9 %collective-permute-start.20 = (bf16[512,512]{1,0:T(8,128)(2,1)}, bf16[512,512]{1,0:T(8,128)(2,1)}, u32[]{:S(2)}, u32[]{:S(2)}) collective-permute-start(bf16[512,512]{1,0:T(8,128)(2,1)} %get-tuple-element.68), channel_id=1, source_target_pairs={{0,6},{1,7},{2,0},{3,1},{4,2},{5,3},{6,4},{7,5},{8,14},{9,15},{10,... | collective-permute-start | bytes 1572872 | tf_op jit(solution)/shard_map/ppermute | solution.py:30
  45.7 14.1 %collective-permute-start.19 = (bf16[512,512]{1,0:T(8,128)(2,1)}, bf16[512,512]{1,0:T(8,128)(2,1)}, u32[]{:S(2)}, u32[]{:S(2)}) collective-permute-start(bf16[512,512]{1,0:T(8,128)(2,1)} %get-tuple-element.63), channel_id=1, source_target_pairs={{0,2},{1,3},{2,4},{3,5},{4,6},{5,7},{6,0},{7,1},{8,10},{9,11},{10,... | collective-permute-start | bytes 1572872 | tf_op jit(solution)/shard_map/ppermute | solution.py:30
  46.3 12.4 %collective-permute-start.18 = (bf16[30,16,128]{2,1,0:T(8,128)(2,1)S(1)}, bf16[30,16,128]{2,1,0:T(8,128)(2,1)S(1)}, u32[]{:S(2)}, u32[]{:S(2)}) collective-permute-start(bf16[30,16,128]{2,1,0:T(8,128)(2,1)S(1)} %cap_both.1.b0_ref), channel_id=1, source_target_pairs={{0,2},{1,3},{2,4},{3,5},{4,6},{5,7},{6,0},{7,1},{8,10},{9,11},{10,... | collective-permute-start | bytes 368648 | tf_op jit(solution)/shard_map/ppermute | solution.py:30
  46.3 12.4 %collective-permute-start.17 = (bf16[30,16,128]{2,1,0:T(8,128)(2,1)S(1)}, bf16[30,16,128]{2,1,0:T(8,128)(2,1)S(1)}, u32[]{:S(2)}, u32[]{:S(2)}) collective-permute-start(bf16[30,16,128]{2,1,0:T(8,128)(2,1)S(1)} %cap_both.1.b0_ref), channel_id=1, source_target_pairs={{0,4},{1,5},{2,6},{3,7},{4,0},{5,1},{6,2},{7,3},{8,12},{9,13},{10,... | collective-permute-start | bytes 368648 | tf_op jit(solution)/shard_map/ppermute | solution.py:30
  49.5 9.2 %collective-permute-start.16 = (bf16[30,16,128]{2,1,0:T(8,128)(2,1)S(1)}, bf16[30,16,128]{2,1,0:T(8,128)(2,1)}, u32[]{:S(2)}, u32[]{:S(2)}) collective-permute-start(bf16[30,16,128]{2,1,0:T(8,128)(2,1)S(1)} %cap_both.1.b0_ref), channel_id=1, source_target_pairs={{0,6},{1,7},{2,0},{3,1},{4,2},{5,3},{6,4},{7,5},{8,14},{9,15},{10,... | collective-permute-start | bytes 368648 | tf_op jit(solution)/shard_map/ppermute | solution.py:30
  64.2 15.8 %collective-permute-start.21 = (f32[512,512]{1,0:T(8,128)}, f32[512,512]{1,0:T(8,128)}, u32[]{:S(2)}, u32[]{:S(2)}) collective-permute-start(f32[512,512]{1,0:T(8,128)} %get-tuple-element.72.y1_ref), channel_id=1, source_target_pairs={{0,1},{1,0},{2,3},{3,2},{4,5},{5,4},{6,7},{7,6},{8,9},{9,8},{10,11... | collective-permute-start | bytes 3145736 | tf_op jit(solution)/shard_map/ppermute | solution.py:30
  72.2 10.3 %collective-permute-start.23 = (bf16[640,128]{1,0:T(8,128)(2,1)}, bf16[640,128]{1,0:T(8,128)(2,1)S(1)}, u32[]{:S(2)}, u32[]{:S(2)}) collective-permute-start(bf16[640,128]{1,0:T(8,128)(2,1)} %get-tuple-element.77), channel_id=1, source_target_pairs={{0,2},{1,3},{2,4},{3,5},{4,6},{5,7},{6,0},{7,1},{8,10},{9,11},{10,... | collective-permute-start | bytes 491528 | tf_op jit(solution)/shard_map/ppermute | solution.py:30
  72.2 10.3 %collective-permute-start.24 = (bf16[640,128]{1,0:T(8,128)(2,1)}, bf16[640,128]{1,0:T(8,128)(2,1)S(1)}, u32[]{:S(2)}, u32[]{:S(2)}) collective-permute-start(bf16[640,128]{1,0:T(8,128)(2,1)} %get-tuple-element.78), channel_id=1, source_target_pairs={{0,4},{1,5},{2,6},{3,7},{4,0},{5,1},{6,2},{7,3},{8,12},{9,13},{10,... | collective-permute-start | bytes 491528 | tf_op jit(solution)/shard_map/ppermute | solution.py:30
  73.5 9.4 %collective-permute-start.25 = (bf16[640,128]{1,0:T(8,128)(2,1)}, bf16[640,128]{1,0:T(8,128)(2,1)}, u32[]{:S(2)}, u32[]{:S(2)}) collective-permute-start(bf16[640,128]{1,0:T(8,128)(2,1)} %get-tuple-element.79), channel_id=1, source_target_pairs={{0,6},{1,7},{2,0},{3,1},{4,2},{5,3},{6,4},{7,5},{8,14},{9,15},{10,... | collective-permute-start | bytes 491528 | tf_op jit(solution)/shard_map/ppermute | solution.py:30
  84.5 8.6 %collective-permute-start.26 = (bf16[640,128]{1,0:T(8,128)(2,1)S(1)}, bf16[640,128]{1,0:T(8,128)(2,1)S(1)}, u32[]{:S(2)}, u32[]{:S(2)}) collective-permute-start(bf16[640,128]{1,0:T(8,128)(2,1)S(1)} %get-tuple-element.85.e_ref.refs_3_), channel_id=1, source_target_pairs={{0,8},{1,9},{2,10},{3,11},{4,12},{5,13},{6,14},{7,15},{8,0},{9,1},... | collective-permute-start | bytes 491528 | tf_op jit(solution)/shard_map/ppermute | solution.py:30
  86.4 6.7 %collective-permute-start.27 = (bf16[512,128]{1,0:T(8,128)(2,1)S(1)}, bf16[512,128]{1,0:T(8,128)(2,1)S(1)}, u32[]{:S(2)}, u32[]{:S(2)}) collective-permute-start(bf16[512,128]{1,0:T(8,128)(2,1)S(1)} %get-tuple-element.83), channel_id=1, source_target_pairs={{0,16},{1,17},{2,18},{3,19},{4,20},{5,21},{6,22},{7,23},{8,24},{9,... | collective-permute-start | bytes 393224 | tf_op jit(solution)/shard_map/ppermute | solution.py:30
  93.2 10.0 %collective-permute-start.29 = (bf16[384,128]{1,0:T(8,128)(2,1)S(1)}, bf16[384,128]{1,0:T(8,128)(2,1)S(1)}, u32[]{:S(2)}, u32[]{:S(2)}) collective-permute-start(bf16[384,128]{1,0:T(8,128)(2,1)S(1)} %get-tuple-element.88.quad_ref.refs_3_), channel_id=1, source_target_pairs={{0,32},{1,33},{2,34},{3,35},{4,36},{5,37},{6,38},{7,39},{8,40},{9,... | collective-permute-start | bytes 294920 | tf_op jit(solution)/shard_map/ppermute | solution.py:30
  103.2 6.8 %collective-permute-start.32 = (bf16[128,128]{1,0:T(8,128)(2,1)S(1)}, bf16[128,128]{1,0:T(8,128)(2,1)S(1)}, u32[]{:S(2)}, u32[]{:S(2)}) collective-permute-start(bf16[128,128]{1,0:T(8,128)(2,1)S(1)} %own4.1.a_ref), channel_id=1, source_target_pairs={{0,128},{1,129},{2,130},{3,131},{4,132},{5,133},{6,134},{7,135},{8... | collective-permute-start | bytes 98312 | tf_op jit(solution)/shard_map/ppermute | solution.py:30
  111.0 6.9 %collective-permute-start.35 = (bf16[640,128]{1,0:T(8,128)(2,1)S(1)}, bf16[640,128]{1,0:T(8,128)(2,1)S(1)}, u32[]{:S(2)}, u32[]{:S(2)}) collective-permute-start(bf16[640,128]{1,0:T(8,128)(2,1)S(1)} %solve_4.1.b0_ref), channel_id=1, source_target_pairs={{0,2},{1,3},{2,4},{3,5},{4,6},{5,7},{6,0},{7,1},{8,10},{9,11},{10,... | collective-permute-start | bytes 491528 | tf_op jit(solution)/shard_map/ppermute | solution.py:30
  114.1 6.9 %collective-permute-start.34 = (bf16[640,128]{1,0:T(8,128)(2,1)S(1)}, bf16[640,128]{1,0:T(8,128)(2,1)S(1)}, u32[]{:S(2)}, u32[]{:S(2)}) collective-permute-start(bf16[640,128]{1,0:T(8,128)(2,1)S(1)} %solve_4.1.b0_ref), channel_id=1, source_target_pairs={{0,4},{1,5},{2,6},{3,7},{4,0},{5,1},{6,2},{7,3},{8,12},{9,13},{10,... | collective-permute-start | bytes 491528 | tf_op jit(solution)/shard_map/ppermute | solution.py:30
  121.4 5.6 %collective-permute-start.36 = (bf16[640,512]{1,0:T(8,128)(2,1)S(1)}, bf16[640,512]{1,0:T(8,128)(2,1)S(1)}, u32[]{:S(2)}, u32[]{:S(2)}) collective-permute-start(bf16[640,512]{1,0:T(8,128)(2,1)S(1)} %columns.1.t0_ref), channel_id=1, source_target_pairs={{0,1},{1,0},{2,3},{3,2},{4,5},{5,4},{6,7},{7,6},{8,9},{9,8},{10,11... | collective-permute-start | bytes 1966088 | tf_op jit(solution)/shard_map/ppermute | solution.py:30
  (21 other events, 242.8 us)

commit v3 on v2

--- a/solution.py
+++ b/solution.py
@@ -230,24 +230,22 @@
     low_ref[1, :n0] = r1_ref[:n0].astype(BF)
     low_ref[0, n0:] = (leaf_ref[n0:n1] + r1_ref[n0:n1]).astype(BF)
     low_ref[1, n0:] = (r2_ref[n0:n1] + r3_ref[n0:n1]).astype(BF)
-    quad_ref[...] = (leaf_ref[n1:] + r1_ref[n1:]) + (r2_ref[n1:] + r3_ref[n1:])
-
-
-def cap_z_body(quad_ref, z1_ref, z2_ref, z3_ref, mid_ref, last_ref):
+    quad = ((leaf_ref[n1:] + r1_ref[n1:]) + (r2_ref[n1:] + r3_ref[n1:])).astype(BF)
+    for z in range(Z):
+        quad_ref[z] = quad
+
+
+def cap_both_body(z_ref, low_ref, quads_ref, both_ref):
     n0, n1 = FIRST[3] - FIRST[2], FIRST[4] - FIRST[2]
-    mid_ref[0, :n0] = quad_ref[:n0].astype(BF)
-    mid_ref[1, :n0] = z1_ref[:n0].astype(BF)
-    mid_ref[0, n0:] = (quad_ref[n0:n1] + z1_ref[n0:n1]).astype(BF)
-    mid_ref[1, n0:] = (z2_ref[n0:n1] + z3_ref[n0:n1]).astype(BF)
-    last_ref[...] = (quad_ref[n1:] + z1_ref[n1:]) + (z2_ref[n1:] + z3_ref[n1:])
-
-
-def cap_both_body(low_ref, mid_ref, own4_ref, sib4_ref, both_ref):
-    for side, last_ref in enumerate((own4_ref, sib4_ref)):
+    quads = [quads_ref[z_ref[0] ^ k].astype(F32) for k in range(Z)]
+    pairs = [quads[k][n0:] + quads[k + 1][n0:] for k in range(0, Z, 2)]
+    fours = [pairs[k][n1 - n0 :] + pairs[k + 1][n1 - n0 :] for k in (0, 2)]
+    for side in range(2):
         at = side * N_CAP
         both_ref[at : at + FIRST[2]] = low_ref[side]
-        both_ref[at + FIRST[2] : at + FIRST[4]] = mid_ref[side]
-        both_ref[at + FIRST[4]] = last_ref[0].astype(BF)
+        both_ref[at + FIRST[2] : at + FIRST[3]] = quads[side][:n0].astype(BF)
+        both_ref[at + FIRST[3] : at + FIRST[4]] = pairs[side][: n1 - n0].astype(BF)
+        both_ref[at + FIRST[4] : at + N_CAP] = fours[side].astype(BF)
 
 
 def cap_stack_body(scalar_ref, b0_ref, b1_ref, b2_ref, b3_ref, out_ref):
@@ -526,7 +524,6 @@
     g = cap_factor[:, 0]
     struct = jax.ShapeDtypeStruct
 
-    a_oth = to_core(leaf_inverse)
     part_shape = struct((rows, columns // C), BF)
     mine, theirs = live_rhs(scalars, in_hbm(rhs))
     other = to_core(theirs)
@@ -543,31 +540,33 @@
     )(scalars, cap_mine, to_core(cap_theirs))
     part1, part2, part3 = to_y(s1, 1), to_y(s2, 2), to_y(s3, 3)
 
-    vt_oth = to_core(vt)
+    a_oth = to_core(after(leaf_inverse, own))
+    vt_oth = to_core(after(vt, own))
     chip = kernel_call(
         chip_body, struct((C * rows, columns // C), BF), 1, 2, name="chip"
-    )(scalars, after(mine, part1, a_oth, vt_oth), other)
-    before, behind = to_y(chip, 1), to_y(after(chip, part2, part3), -1)
+    )(scalars, after(mine, part1, vt_oth), other)
+    before, behind = to_y(chip, 1), to_y(after(chip, part2, part3, a_oth), -1)
     cap_leaf = kernel_call(cap_leaf_body, struct((N_CAP, part, R), F32), 0, 4, name="cap_leaf")(
         own, part1, part2, part3
     )
+    n_high = N_CAP - FIRST[2]
     low, cap_quad = kernel_call(
         cap_x_body,
-        (struct((2, FIRST[2], part, R), BF), struct((N_CAP - FIRST[2], part, R), F32)),
+        (struct((2, FIRST[2], part, R), BF), struct((Z, n_high, part, R), BF)),
         0,
         4,
         name="cap_x",
     )(cap_leaf, to_x(cap_leaf, 1), to_x(cap_leaf, 2), to_x(cap_leaf, 3))
-    mid, last = kernel_call(
-        cap_z_body,
-        (struct((2, FIRST[4] - FIRST[2], part, R), BF), struct((1, part, R), F32)),
+    cap_quads = lax.all_to_all(
+        cap_quad,
+        "partner",
         0,
-        4,
-        name="cap_z",
-    )(cap_quad, to_z(cap_quad, 1), to_z(cap_quad, 2), to_z(cap_quad, 3))
+        0,
+        axis_index_groups=[[z * X + x for z in range(Z)] for x in range(X)],
+    )
     both = kernel_call(
-        cap_both_body, struct((2 * N_CAP, part, R), BF), 0, 4, name="cap_both"
-    )(low, mid, last, to_z(last, 4))
+        cap_both_body, struct((2 * N_CAP, part, R), BF), 1, 2, name="cap_both"
+    )((partner >> 2)[None], low, cap_quads)
     top, bottom = kernel_call(
         halves_body, (part_shape, part_shape), 0, 2, name="halves"
     )(after(before, both), behind)

time: 130 us -> 129 us (level)
  waiting for transfers between devices: 36.7 us -> 39.1 us
  Pallas kernels: 31.9 us -> 29.9 us
    ppermute x37 -> x33, starting transfers between devices: 59.5 us -> 50.4 us  [move(): return lax.ppermute(block, ('partner', 'row'), route)]
    all_to_all x0 -> x1, waiting for transfers between devices: none -> 8.63 us  [shards(): lax.all_to_all(cap_quad, 'partner', 0, 0, axis_index_groups=[[z * X + x f...]
    all_to_all x0 -> x1, starting transfers between devices: none -> 7.94 us  [shards(): lax.all_to_all(cap_quad, 'partner', 0, 0, axis_index_groups=[[z * X + x f...]
    ppermute x37 -> x33, waiting for transfers between devices: 36.7 us -> 30.5 us  [move(): return lax.ppermute(block, ('partner', 'row'), route)]
  transfers between devices with their start and end apart: 37 -> 34, of which waited for: 20 -> 19; matrix products, arithmetic and copies ran while one was open for 0% -> 0% of each run, Pallas kernels for 16% -> 14%
where the time goes in v3:
time: 129 us
  starting transfers between devices  58.4 us (45%)
  waiting for transfers between devices  39.1 us (30%)
  Pallas kernels  29.9 us (23%)
    ppermute x33, starting transfers between devices, move(): return lax.ppermute(block, ('partner', 'row'), route)  50.4 us
    ppermute x33, waiting for transfers between devices, move(): return lax.ppermute(block, ('partner', 'row'), route)  30.5 us
    all_to_all x1, waiting for transfers between devices, shards(): lax.all_to_all(cap_quad, 'partner', 0, 0, axis_index_groups=[[z * X + x f...  8.63 us
    all_to_all x1, starting transfers between devices, shards(): lax.all_to_all(cap_quad, 'partner', 0, 0, axis_index_groups=[[z * X + x f...  7.94 us
    pallas_call x1, Pallas kernels, leaf(): pl.pallas_call(leaf_body, out_shape=out_shape, in_specs=[pl.BlockSpec(mem...  5.68 us
    pallas_call x1, Pallas kernels, shards(): kernel_call(leaf_end_body, [struct((rows, columns // C), F32)] * 2 + [str...  3.68 us
  transfers between devices with their start and end apart: 34, of which 19 were waited for; matrix products, arithmetic and copies ran while one was open for 0% of the time, Pallas kernels for 14%

profile of v3, /device:TPU:1, one launch (start us, length us, event | category | flops | bytes accessed | tf_op | source)
XLA Modules:
  0.0 128.8 jit_solution(9770680368740413510)
XLA Ops:
  0.7 2.4 %prepare.1 = (bf16[640,512]{1,0:T(8,128)(2,1)S(1)}, f32[15,64,128]{2,1,0:T(8,128)S(1)}, f32[15,64,128]{2,1,0:T(8,128)S(1)}) custom-call(s32[4]{0:T(128)S(1)} %pad_add_fusion.scalar_ref, bf16[5,512,128]{2,1,0:T(8,128)(2,1)} %refs_2_.1, bf16[5,512,128]{2,1,0:T(8,128)(2,1)} %v_hbm.1), custom_call_target="tpu_custom_call" | custom-call | tf_op jit(solution)/shard_map/prepare/pallas_call | solution.py:188
  3.2 3.3 %collective-permute-start = (f32[15,64,128]{2,1,0:T(8,128)S(1)}, f32[15,64,128]{2,1,0:T(8,128)S(1)}, u32[]{:S(2)}, u32[]{:S(2)}) collective-permute-start(f32[15,64,128]{2,1,0:T(8,128)S(1)} %get-tuple-element.48), channel_id=1, source_target_pairs={{0,1},{1,0},{2,3},{3,2},{4,5},{5,4},{6,7},{7,6},{8,9},{9,8},{10,11... | collective-permute-start | bytes 1474568 | tf_op jit(solution)/shard_map/ppermute | solution.py:30
  9.2 2.1 %live_rhs.1 = (bf16[512,512]{1,0:T(8,128)(2,1)S(1)}, bf16[512,512]{1,0:T(8,128)(2,1)S(1)}) custom-call(s32[4]{0:T(128)S(1)} %pad_add_fusion.scalar_ref, f32[512,1024]{1,0:T(8,128)} %rhs_hbm.1), custom_call_target="tpu_custom_call" | custom-call | tf_op jit(solution)/shard_map/live_rhs/pallas_call | solution.py:122
  11.8 2.2 %collective-permute-start.2 = (bf16[15,16,128]{2,1,0:T(8,128)(2,1)S(1)}, bf16[15,16,128]{2,1,0:T(8,128)(2,1)S(1)}, u32[]{:S(2)}, u32[]{:S(2)}) collective-permute-start(bf16[15,16,128]{2,1,0:T(8,128)(2,1)S(1)} %get-tuple-element.51), channel_id=1, source_target_pairs={{0,4},{1,5},{2,6},{3,7},{4,0},{5,1},{6,2},{7,3},{8,12},{9,13},{10,... | collective-permute-start | bytes 184328 | tf_op jit(solution)/shard_map/ppermute | solution.py:30
  14.0 3.2 %collective-permute-done.1.r1_ref = bf16[15,16,128]{2,1,0:T(8,128)(2,1)S(1)} collective-permute-done((bf16[15,16,128]{2,1,0:T(8,128)(2,1)S(1)}, bf16[15,16,128]{2,1,0:T(8,128)(2,1)S(1)}, u32[]{:S(2)}, u32[]{:S(2)}) %collective-permute-start.1) | collective-permute-done | bytes 61472 | tf_op jit(solution)/shard_map/ppermute | solution.py:30
  29.5 7.9 %all-to-all-start = ((bf16[8,6,16,128]{3,2,1,0:T(8,128)(2,1)}), bf16[8,6,16,128]{3,2,1,0:T(8,128)(2,1)S(1)}, u32[]{:S(2)}, u32[]{:S(2)}) async-start(bf16[8,6,16,128]{3,2,1,0:T(8,128)(2,1)} %get-tuple-element.54), calls=%async_computation | async-start | bytes 393216 | tf_op jit(solution)/shard_map/all_to_all | solution.py:560
  37.4 8.6 %all-to-all-done.quads_ref = bf16[8,6,16,128]{3,2,1,0:T(8,128)(2,1)S(1)} async-done(((bf16[8,6,16,128]{3,2,1,0:T(8,128)(2,1)}), bf16[8,6,16,128]{3,2,1,0:T(8,128)(2,1)S(1)}, u32[]{:S(2)}, u32[]{:S(2)}) %all-to-all-start) | async-done | bytes 196640 | tf_op jit(solution)/shard_map/all_to_all | solution.py:560
  48.6 2.4 %collective-permute-start.13 = (bf16[30,16,128]{2,1,0:T(8,128)(2,1)S(1)}, bf16[30,16,128]{2,1,0:T(8,128)(2,1)}, u32[]{:S(2)}, u32[]{:S(2)}) collective-permute-start(bf16[30,16,128]{2,1,0:T(8,128)(2,1)S(1)} %cap_both.1.b0_ref), channel_id=1, source_target_pairs={{0,4},{1,5},{2,6},{3,7},{4,0},{5,1},{6,2},{7,3},{8,12},{9,13},{10,... | collective-permute-start | bytes 368648 | tf_op jit(solution)/shard_map/ppermute | solution.py:30
  51.5 5.7 %leaf.1 = (f32[512,512]{1,0:T(8,128)S(1)}, f32[512,512]{1,0:T(8,128)S(1)}, bf16[512,1024]{1,0:T(8,128)(2,1)S(1)}, bf16[512,1024]{1,0:T(8,128)(2,1)S(1)}) custom-call(s32[4]{0:T(128)S(1)} %pad_add_fusion.2.chip_ref, bf16[512,4096]{1,0:T(8,128)(2,1)} %a0_hbm.1, bf16[512,4096]{1,0:T(8,128)(2,1)} %copy-done.6, bf16[1024,512]{1,0:T(8,128)(2,1)S(1)} %chip.1.b0_ref, ...), custom_call_target="tpu_custom_call" | custom-call | tf_op jit(solution)/shard_map/leaf/pallas_call | solution.py:319
  57.1 2.8 %collective-permute-done.14.b3_ref = bf16[30,16,128]{2,1,0:T(8,128)(2,1)S(1)} collective-permute-done((bf16[30,16,128]{2,1,0:T(8,128)(2,1)S(1)}, bf16[30,16,128]{2,1,0:T(8,128)(2,1)S(1)}, u32[]{:S(2)}, u32[]{:S(2)}) %collective-permute-start.14) | collective-permute-done | bytes 122912 | tf_op jit(solution)/shard_map/ppermute | solution.py:30
  61.6 3.7 %leaf_end.1 = (f32[512,512]{1,0:T(8,128)S(1)}, f32[512,512]{1,0:T(8,128)S(1)}, bf16[640,128]{1,0:T(8,128)(2,1)S(1)}, bf16[640,128]{1,0:T(8,128)(2,1)S(1)}, bf16[640,128]{1,0:T(8,128)(2,1)S(1)}) custom-call(s32[3]{0:T(128)S(1)} %pad_add_fusion.1.scalar_ref.place_ref, bf16[512,1024]{1,0:T(8,128)(2,1)S(1)} %get-tuple-element.66.a0_ref, ...), custom_call_target="tpu_custom_call" | custom-call | tf_op jit(solution)/shard_map/leaf_end/pallas_call | solution.py:596
  65.3 7.8 %collective-permute-start.17 = (f32[512,512]{1,0:T(8,128)S(1)}, f32[512,512]{1,0:T(8,128)S(1)}, u32[]{:S(2)}, u32[]{:S(2)}) collective-permute-start(f32[512,512]{1,0:T(8,128)S(1)} %get-tuple-element.72.y1_ref), channel_id=1, source_target_pairs={{0,1},{1,0},{2,3},{3,2},{4,5},{5,4},{6,7},{7,6},{8,9},{9,8},{10,11... | collective-permute-start | bytes 3145736 | tf_op jit(solution)/shard_map/ppermute | solution.py:30
  78.2 2.4 %elimination.1 = (bf16[1280,256]{1,0:T(8,128)(2,1)S(1)}, bf16[5,2,128,128]{3,2,1,0:T(8,128)(2,1)S(1)}) custom-call(s32[4]{0:T(128)S(1)} %pad_add_fusion.scalar_ref, s32[5]{0:T(128)S(1)} %shift-right-arithmetic_and_fusion.side_ref.refs_0_, bf16[30,64,128]{2,1,0:T(8,128)(2,1)S(1)} %cap_stack.1.mine_ref, ...), custom_call_target="tpu_custom_call" | custom-call | tf_op jit(solution)/shard_map/elimination/pallas_call | solution.py:586
  80.6 2.2 %collective-permute-done.20.q2_ref = bf16[640,128]{1,0:T(8,128)(2,1)S(1)} collective-permute-done((bf16[640,128]{1,0:T(8,128)(2,1)S(1)}, bf16[640,128]{1,0:T(8,128)(2,1)S(1)}, u32[]{:S(2)}, u32[]{:S(2)}) %collective-permute-start.20) | collective-permute-done | bytes 163872 | tf_op jit(solution)/shard_map/ppermute | solution.py:30
  87.6 2.4 %collective-permute-done.24.r3_ref.refs_6_ = bf16[512,128]{1,0:T(8,128)(2,1)S(1)} collective-permute-done((bf16[512,128]{1,0:T(8,128)(2,1)S(1)}, bf16[512,128]{1,0:T(8,128)(2,1)S(1)}, u32[]{:S(2)}, u32[]{:S(2)}) %collective-permute-start.24) | collective-permute-done | bytes 131104 | tf_op jit(solution)/shard_map/ppermute | solution.py:30
  90.0 3.4 %collective-permute-done.23.r2_ref.refs_5_ = bf16[512,128]{1,0:T(8,128)(2,1)S(1)} collective-permute-done((bf16[512,128]{1,0:T(8,128)(2,1)S(1)}, bf16[512,128]{1,0:T(8,128)(2,1)S(1)}, u32[]{:S(2)}, u32[]{:S(2)}) %collective-permute-start.23) | collective-permute-done | bytes 131104 | tf_op jit(solution)/shard_map/ppermute | solution.py:30
  93.8 2.5 %collective-permute-start.27 = (bf16[256,128]{1,0:T(8,128)(2,1)S(1)}, bf16[256,128]{1,0:T(8,128)(2,1)S(1)}, u32[]{:S(2)}, u32[]{:S(2)}) collective-permute-start(bf16[256,128]{1,0:T(8,128)(2,1)S(1)} %get-tuple-element.87), channel_id=1, source_target_pairs={{0,96},{1,97},{2,98},{3,99},{4,100},{5,101},{6,102},{7,103},{8,104... | collective-permute-start | bytes 196616 | tf_op jit(solution)/shard_map/ppermute | solution.py:30
  98.9 2.4 %collective-permute-done.26.z2_ref.refs_5_ = bf16[256,128]{1,0:T(8,128)(2,1)S(1)} collective-permute-done((bf16[256,128]{1,0:T(8,128)(2,1)S(1)}, bf16[256,128]{1,0:T(8,128)(2,1)S(1)}, u32[]{:S(2)}, u32[]{:S(2)}) %collective-permute-start.26) | collective-permute-done | bytes 65568 | tf_op jit(solution)/shard_map/ppermute | solution.py:30
  101.4 5.0 %collective-permute-start.28 = (bf16[128,128]{1,0:T(8,128)(2,1)S(1)}, bf16[128,128]{1,0:T(8,128)(2,1)S(1)}, u32[]{:S(2)}, u32[]{:S(2)}) collective-permute-start(bf16[128,128]{1,0:T(8,128)(2,1)S(1)} %own4.1.a_ref), channel_id=1, source_target_pairs={{0,128},{1,129},{2,130},{3,131},{4,132},{5,133},{6,134},{7,135},{8... | collective-permute-start | bytes 98312 | tf_op jit(solution)/shard_map/ppermute | solution.py:30
  109.2 3.4 %collective-permute-start.31 = (bf16[640,128]{1,0:T(8,128)(2,1)S(1)}, bf16[640,128]{1,0:T(8,128)(2,1)S(1)}, u32[]{:S(2)}, u32[]{:S(2)}) collective-permute-start(bf16[640,128]{1,0:T(8,128)(2,1)S(1)} %solve_4.1.b0_ref), channel_id=1, source_target_pairs={{0,2},{1,3},{2,4},{3,5},{4,6},{5,7},{6,0},{7,1},{8,10},{9,11},{10,... | collective-permute-start | bytes 491528 | tf_op jit(solution)/shard_map/ppermute | solution.py:30
  112.6 2.8 %collective-permute-start.30 = (bf16[640,128]{1,0:T(8,128)(2,1)S(1)}, bf16[640,128]{1,0:T(8,128)(2,1)S(1)}, u32[]{:S(2)}, u32[]{:S(2)}) collective-permute-start(bf16[640,128]{1,0:T(8,128)(2,1)S(1)} %solve_4.1.b0_ref), channel_id=1, source_target_pairs={{0,4},{1,5},{2,6},{3,7},{4,0},{5,1},{6,2},{7,3},{8,12},{9,13},{10,... | collective-permute-start | bytes 491528 | tf_op jit(solution)/shard_map/ppermute | solution.py:30
  117.0 3.0 %collective-permute-done.30.b2_ref = bf16[640,128]{1,0:T(8,128)(2,1)S(1)} collective-permute-done((bf16[640,128]{1,0:T(8,128)(2,1)S(1)}, bf16[640,128]{1,0:T(8,128)(2,1)S(1)}, u32[]{:S(2)}, u32[]{:S(2)}) %collective-permute-start.30) | collective-permute-done | bytes 163872 | tf_op jit(solution)/shard_map/ppermute | solution.py:30
  120.3 4.2 %collective-permute-start.32 = (bf16[640,512]{1,0:T(8,128)(2,1)S(1)}, bf16[640,512]{1,0:T(8,128)(2,1)S(1)}, u32[]{:S(2)}, u32[]{:S(2)}) collective-permute-start(bf16[640,512]{1,0:T(8,128)(2,1)S(1)} %columns.1.t0_ref), channel_id=1, source_target_pairs={{0,1},{1,0},{2,3},{3,2},{4,5},{5,4},{6,7},{7,6},{8,9},{9,8},{10,11... | collective-permute-start | bytes 1966088 | tf_op jit(solution)/shard_map/ppermute | solution.py:30
  126.2 2.4 %update.1 = f32[512,1024]{1,0:T(8,128)} custom-call(s32[4]{0:T(128)S(1)} %pad_add_fusion.scalar_ref, f32[512,512]{1,0:T(8,128)S(1)} %get-tuple-element.73.y0_ref, f32[512,512]{1,0:T(8,128)S(1)} %get-tuple-element.74.y1_ref, bf16[5,512,128]{2,1,0:T(8,128)(2,1)S(1)} %get-tuple-element.75.u_ref, bf16[640,512]{1,0:T(8,128)(2,1)S(1)} %columns.1.t0_ref, ...), custom_call_target="tpu_custom_call" | custom-call | tf_op jit(solution)/shard_map/update/pallas_call | solution.py:506
  (86 shorter events, 39.3 us)
Async XLA Ops:
  8.6 11.6 %collective-permute-start.10 = (bf16[512,4096]{1,0:T(8,128)(2,1)}, bf16[512,4096]{1,0:T(8,128)(2,1)S(1)}, u32[]{:S(2)}, u32[]{:S(2)}) collective-permute-start(bf16[512,4096]{1,0:T(8,128)(2,1)} %a0_hbm.1), channel_id=1, source_target_pairs={{0,1},{1,0},{2,3},{3,2},{4,5},{5,4},{6,7},{7,6},{8,9},{9,8},{10,11... | collective-permute-start | bytes 12582920 | tf_op jit(solution)/shard_map/ppermute | solution.py:30
  9.1 8.1 %collective-permute-start.7 = (bf16[640,512]{1,0:T(8,128)(2,1)S(1)}, bf16[640,512]{1,0:T(8,128)(2,1)S(1)}, u32[]{:S(2)}, u32[]{:S(2)}) collective-permute-start(bf16[640,512]{1,0:T(8,128)(2,1)S(1)} %get-tuple-element.57.va_ref), channel_id=1, source_target_pairs={{0,1},{1,0},{2,3},{3,2},{4,5},{5,4},{6,7},{7,6},{8,9},{9,8},{10,11... | collective-permute-start | bytes 1966088 | tf_op jit(solution)/shard_map/ppermute | solution.py:30
  11.3 5.8 %collective-permute-start.8 = (bf16[512,512]{1,0:T(8,128)(2,1)S(1)}, bf16[512,512]{1,0:T(8,128)(2,1)S(1)}, u32[]{:S(2)}, u32[]{:S(2)}) collective-permute-start(bf16[512,512]{1,0:T(8,128)(2,1)S(1)} %get-tuple-element.59), channel_id=1, source_target_pairs={{0,1},{1,0},{2,3},{3,2},{4,5},{5,4},{6,7},{7,6},{8,9},{9,8},{10,11... | collective-permute-start | bytes 1572872 | tf_op jit(solution)/shard_map/ppermute | solution.py:30
  11.8 5.4 %collective-permute-start.1 = (bf16[15,16,128]{2,1,0:T(8,128)(2,1)S(1)}, bf16[15,16,128]{2,1,0:T(8,128)(2,1)S(1)}, u32[]{:S(2)}, u32[]{:S(2)}) collective-permute-start(bf16[15,16,128]{2,1,0:T(8,128)(2,1)S(1)} %get-tuple-element.50), channel_id=1, source_target_pairs={{0,2},{1,3},{2,4},{3,5},{4,6},{5,7},{6,0},{7,1},{8,10},{9,11},{10,... | collective-permute-start | bytes 184328 | tf_op jit(solution)/shard_map/ppermute | solution.py:30
  11.8 7.5 %collective-permute-start.2 = (bf16[15,16,128]{2,1,0:T(8,128)(2,1)S(1)}, bf16[15,16,128]{2,1,0:T(8,128)(2,1)S(1)}, u32[]{:S(2)}, u32[]{:S(2)}) collective-permute-start(bf16[15,16,128]{2,1,0:T(8,128)(2,1)S(1)} %get-tuple-element.51), channel_id=1, source_target_pairs={{0,4},{1,5},{2,6},{3,7},{4,0},{5,1},{6,2},{7,3},{8,12},{9,13},{10,... | collective-permute-start | bytes 184328 | tf_op jit(solution)/shard_map/ppermute | solution.py:30
  17.8 28.3 %collective-permute-start.9 = (bf16[1024,512]{1,0:T(8,128)(2,1)S(1)}, bf16[1024,512]{1,0:T(8,128)(2,1)S(1)}, u32[]{:S(2)}, u32[]{:S(2)}) collective-permute-start(bf16[1024,512]{1,0:T(8,128)(2,1)S(1)} %chip.1.b0_ref), channel_id=1, source_target_pairs={{0,2},{1,3},{2,4},{3,5},{4,6},{5,7},{6,0},{7,1},{8,10},{9,11},{10,... | collective-permute-start | bytes 3145736 | tf_op jit(solution)/shard_map/ppermute | solution.py:30
  20.3 25.9 %collective-permute-start.11 = (bf16[1024,512]{1,0:T(8,128)(2,1)S(1)}, bf16[1024,512]{1,0:T(8,128)(2,1)S(1)}, u32[]{:S(2)}, u32[]{:S(2)}) collective-permute-start(bf16[1024,512]{1,0:T(8,128)(2,1)S(1)} %chip.1.b0_ref), channel_id=1, source_target_pairs={{0,6},{1,7},{2,0},{3,1},{4,2},{5,3},{6,4},{7,5},{8,14},{9,15},{10,... | collective-permute-start | bytes 3145736 | tf_op jit(solution)/shard_map/ppermute | solution.py:30
  29.5 16.6 %all-to-all-start = ((bf16[8,6,16,128]{3,2,1,0:T(8,128)(2,1)}), bf16[8,6,16,128]{3,2,1,0:T(8,128)(2,1)S(1)}, u32[]{:S(2)}, u32[]{:S(2)}) async-start(bf16[8,6,16,128]{3,2,1,0:T(8,128)(2,1)} %get-tuple-element.54), calls=%async_computation | async-start | bytes 393216 | tf_op jit(solution)/shard_map/all_to_all | solution.py:560
  47.1 14.4 %collective-permute-start.16 = (bf16[512,512]{1,0:T(8,128)(2,1)}, bf16[512,512]{1,0:T(8,128)(2,1)}, u32[]{:S(2)}, u32[]{:S(2)}) collective-permute-start(bf16[512,512]{1,0:T(8,128)(2,1)} %get-tuple-element.68), channel_id=1, source_target_pairs={{0,6},{1,7},{2,0},{3,1},{4,2},{5,3},{6,4},{7,5},{8,14},{9,15},{10,... | collective-permute-start | bytes 1572872 | tf_op jit(solution)/shard_map/ppermute | solution.py:30
  47.2 14.4 %collective-permute-start.15 = (bf16[512,512]{1,0:T(8,128)(2,1)}, bf16[512,512]{1,0:T(8,128)(2,1)}, u32[]{:S(2)}, u32[]{:S(2)}) collective-permute-start(bf16[512,512]{1,0:T(8,128)(2,1)} %get-tuple-element.63), channel_id=1, source_target_pairs={{0,2},{1,3},{2,4},{3,5},{4,6},{5,7},{6,0},{7,1},{8,10},{9,11},{10,... | collective-permute-start | bytes 1572872 | tf_op jit(solution)/shard_map/ppermute | solution.py:30
  48.6 11.3 %collective-permute-start.14 = (bf16[30,16,128]{2,1,0:T(8,128)(2,1)S(1)}, bf16[30,16,128]{2,1,0:T(8,128)(2,1)S(1)}, u32[]{:S(2)}, u32[]{:S(2)}) collective-permute-start(bf16[30,16,128]{2,1,0:T(8,128)(2,1)S(1)} %cap_both.1.b0_ref), channel_id=1, source_target_pairs={{0,2},{1,3},{2,4},{3,5},{4,6},{5,7},{6,0},{7,1},{8,10},{9,11},{10,... | collective-permute-start | bytes 368648 | tf_op jit(solution)/shard_map/ppermute | solution.py:30
  48.6 11.9 %collective-permute-start.13 = (bf16[30,16,128]{2,1,0:T(8,128)(2,1)S(1)}, bf16[30,16,128]{2,1,0:T(8,128)(2,1)}, u32[]{:S(2)}, u32[]{:S(2)}) collective-permute-start(bf16[30,16,128]{2,1,0:T(8,128)(2,1)S(1)} %cap_both.1.b0_ref), channel_id=1, source_target_pairs={{0,4},{1,5},{2,6},{3,7},{4,0},{5,1},{6,2},{7,3},{8,12},{9,13},{10,... | collective-permute-start | bytes 368648 | tf_op jit(solution)/shard_map/ppermute | solution.py:30
  51.1 9.5 %collective-permute-start.12 = (bf16[30,16,128]{2,1,0:T(8,128)(2,1)S(1)}, bf16[30,16,128]{2,1,0:T(8,128)(2,1)}, u32[]{:S(2)}, u32[]{:S(2)}) collective-permute-start(bf16[30,16,128]{2,1,0:T(8,128)(2,1)S(1)} %cap_both.1.b0_ref), channel_id=1, source_target_pairs={{0,6},{1,7},{2,0},{3,1},{4,2},{5,3},{6,4},{7,5},{8,14},{9,15},{10,... | collective-permute-start | bytes 368648 | tf_op jit(solution)/shard_map/ppermute | solution.py:30
  65.3 15.3 %collective-permute-start.17 = (f32[512,512]{1,0:T(8,128)S(1)}, f32[512,512]{1,0:T(8,128)S(1)}, u32[]{:S(2)}, u32[]{:S(2)}) collective-permute-start(f32[512,512]{1,0:T(8,128)S(1)} %get-tuple-element.72.y1_ref), channel_id=1, source_target_pairs={{0,1},{1,0},{2,3},{3,2},{4,5},{5,4},{6,7},{7,6},{8,9},{9,8},{10,11... | collective-permute-start | bytes 3145736 | tf_op jit(solution)/shard_map/ppermute | solution.py:30
  73.2 7.4 %collective-permute-start.19 = (bf16[640,128]{1,0:T(8,128)(2,1)S(1)}, bf16[640,128]{1,0:T(8,128)(2,1)S(1)}, u32[]{:S(2)}, u32[]{:S(2)}) collective-permute-start(bf16[640,128]{1,0:T(8,128)(2,1)S(1)} %get-tuple-element.77), channel_id=1, source_target_pairs={{0,2},{1,3},{2,4},{3,5},{4,6},{5,7},{6,0},{7,1},{8,10},{9,11},{10,... | collective-permute-start | bytes 491528 | tf_op jit(solution)/shard_map/ppermute | solution.py:30
  73.2 9.6 %collective-permute-start.20 = (bf16[640,128]{1,0:T(8,128)(2,1)S(1)}, bf16[640,128]{1,0:T(8,128)(2,1)S(1)}, u32[]{:S(2)}, u32[]{:S(2)}) collective-permute-start(bf16[640,128]{1,0:T(8,128)(2,1)S(1)} %get-tuple-element.78), channel_id=1, source_target_pairs={{0,4},{1,5},{2,6},{3,7},{4,0},{5,1},{6,2},{7,3},{8,12},{9,13},{10,... | collective-permute-start | bytes 491528 | tf_op jit(solution)/shard_map/ppermute | solution.py:30
  75.0 8.6 %collective-permute-start.21 = (bf16[640,128]{1,0:T(8,128)(2,1)S(1)}, bf16[640,128]{1,0:T(8,128)(2,1)S(1)}, u32[]{:S(2)}, u32[]{:S(2)}) collective-permute-start(bf16[640,128]{1,0:T(8,128)(2,1)S(1)} %get-tuple-element.79), channel_id=1, source_target_pairs={{0,6},{1,7},{2,0},{3,1},{4,2},{5,3},{6,4},{7,5},{8,14},{9,15},{10,... | collective-permute-start | bytes 491528 | tf_op jit(solution)/shard_map/ppermute | solution.py:30
  84.3 9.2 %collective-permute-start.22 = (bf16[640,128]{1,0:T(8,128)(2,1)S(1)}, bf16[640,128]{1,0:T(8,128)(2,1)S(1)}, u32[]{:S(2)}, u32[]{:S(2)}) collective-permute-start(bf16[640,128]{1,0:T(8,128)(2,1)S(1)} %get-tuple-element.85.e_ref.refs_3_), channel_id=1, source_target_pairs={{0,8},{1,9},{2,10},{3,11},{4,12},{5,13},{6,14},{7,15},{8,0},{9,1},... | collective-permute-start | bytes 491528 | tf_op jit(solution)/shard_map/ppermute | solution.py:30
  86.8 6.6 %collective-permute-start.23 = (bf16[512,128]{1,0:T(8,128)(2,1)S(1)}, bf16[512,128]{1,0:T(8,128)(2,1)S(1)}, u32[]{:S(2)}, u32[]{:S(2)}) collective-permute-start(bf16[512,128]{1,0:T(8,128)(2,1)S(1)} %get-tuple-element.83), channel_id=1, source_target_pairs={{0,16},{1,17},{2,18},{3,19},{4,20},{5,21},{6,22},{7,23},{8,24},{9,... | collective-permute-start | bytes 393224 | tf_op jit(solution)/shard_map/ppermute | solution.py:30
  93.5 7.9 %collective-permute-start.25 = (bf16[384,128]{1,0:T(8,128)(2,1)S(1)}, bf16[384,128]{1,0:T(8,128)(2,1)S(1)}, u32[]{:S(2)}, u32[]{:S(2)}) collective-permute-start(bf16[384,128]{1,0:T(8,128)(2,1)S(1)} %get-tuple-element.88.quad_ref.refs_3_), channel_id=1, source_target_pairs={{0,32},{1,33},{2,34},{3,35},{4,36},{5,37},{6,38},{7,39},{8,40},{9,... | collective-permute-start | bytes 294920 | tf_op jit(solution)/shard_map/ppermute | solution.py:30
  101.4 6.8 %collective-permute-start.28 = (bf16[128,128]{1,0:T(8,128)(2,1)S(1)}, bf16[128,128]{1,0:T(8,128)(2,1)S(1)}, u32[]{:S(2)}, u32[]{:S(2)}) collective-permute-start(bf16[128,128]{1,0:T(8,128)(2,1)S(1)} %own4.1.a_ref), channel_id=1, source_target_pairs={{0,128},{1,129},{2,130},{3,131},{4,132},{5,133},{6,134},{7,135},{8... | collective-permute-start | bytes 98312 | tf_op jit(solution)/shard_map/ppermute | solution.py:30
  109.2 7.8 %collective-permute-start.31 = (bf16[640,128]{1,0:T(8,128)(2,1)S(1)}, bf16[640,128]{1,0:T(8,128)(2,1)S(1)}, u32[]{:S(2)}, u32[]{:S(2)}) collective-permute-start(bf16[640,128]{1,0:T(8,128)(2,1)S(1)} %solve_4.1.b0_ref), channel_id=1, source_target_pairs={{0,2},{1,3},{2,4},{3,5},{4,6},{5,7},{6,0},{7,1},{8,10},{9,11},{10,... | collective-permute-start | bytes 491528 | tf_op jit(solution)/shard_map/ppermute | solution.py:30
  112.6 7.4 %collective-permute-start.30 = (bf16[640,128]{1,0:T(8,128)(2,1)S(1)}, bf16[640,128]{1,0:T(8,128)(2,1)S(1)}, u32[]{:S(2)}, u32[]{:S(2)}) collective-permute-start(bf16[640,128]{1,0:T(8,128)(2,1)S(1)} %solve_4.1.b0_ref), channel_id=1, source_target_pairs={{0,4},{1,5},{2,6},{3,7},{4,0},{5,1},{6,2},{7,3},{8,12},{9,13},{10,... | collective-permute-start | bytes 491528 | tf_op jit(solution)/shard_map/ppermute | solution.py:30
  120.3 6.0 %collective-permute-start.32 = (bf16[640,512]{1,0:T(8,128)(2,1)S(1)}, bf16[640,512]{1,0:T(8,128)(2,1)S(1)}, u32[]{:S(2)}, u32[]{:S(2)}) collective-permute-start(bf16[640,512]{1,0:T(8,128)(2,1)S(1)} %columns.1.t0_ref), channel_id=1, source_target_pairs={{0,1},{1,0},{2,3},{3,2},{4,5},{5,4},{6,7},{7,6},{8,9},{9,8},{10,11... | collective-permute-start | bytes 1966088 | tf_op jit(solution)/shard_map/ppermute | solution.py:30
  (18 other events, 194.7 us)

commit v4 on v2

--- a/solution.py
+++ b/solution.py
@@ -74,7 +74,13 @@
     return dot(a_upper, b_upper) + (dot(a_upper, b_lower) + dot(a_lower, b_upper))
 
 
-def kernel_call(body, out_shape, n_scalar, n_in, scratch=(), name=None):
+def cost(microseconds):
+    return pl.CostEstimate(
+        flops=int(microseconds * 1.1e9), bytes_accessed=int(microseconds * 1e6), transcendentals=0
+    )
+
+
+def kernel_call(body, out_shape, n_scalar, n_in, scratch=(), name=None, us=None):
     smem = pl.BlockSpec(memory_space=pltpu.SMEM)
     vmem = pl.BlockSpec(memory_space=pltpu.VMEM)
     outs = out_shape if isinstance(out_shape, (tuple, list)) else (out_shape,)
@@ -86,6 +92,7 @@
         out_specs=out_specs if isinstance(out_shape, (tuple, list)) else vmem,
         scratch_shapes=list(scratch),
         compiler_params=pltpu.CompilerParams(vmem_limit_bytes=VMEM_LIMIT),
+        cost_estimate=None if us is None else cost(us),
         name=name,
     )
 
@@ -218,28 +225,36 @@
         ref[...] = (mine_ref[:, at(d + 1), :] + other_ref[:, at(d + 1), :]).astype(BF)
 
 
-def cap_leaf_body(own_ref, r1_ref, r2_ref, r3_ref, leaf_ref):
-    leaf_ref[...] = (own_ref[...] + r1_ref[...].astype(F32)) + (
+def cap_leaf_body(own_ref, r1_ref, r2_ref, r3_ref, leaf_ref, send_ref, upper_ref):
+    leaf = (own_ref[...] + r1_ref[...].astype(F32)) + (
         r2_ref[...].astype(F32) + r3_ref[...].astype(F32)
     )
-
-
-def cap_x_body(leaf_ref, r1_ref, r2_ref, r3_ref, low_ref, quad_ref):
+    leaf_ref[...] = leaf
+    send_ref[...] = leaf.astype(BF)
+    upper_ref[...] = leaf[FIRST[1] :].astype(BF)
+
+
+def cap_x_body(leaf_ref, r1_ref, r2_ref, r3_ref, low_ref, quad_ref, send_ref, upper_ref):
     n0, n1 = FIRST[1], FIRST[2]
     low_ref[0, :n0] = leaf_ref[:n0].astype(BF)
-    low_ref[1, :n0] = r1_ref[:n0].astype(BF)
-    low_ref[0, n0:] = (leaf_ref[n0:n1] + r1_ref[n0:n1]).astype(BF)
-    low_ref[1, n0:] = (r2_ref[n0:n1] + r3_ref[n0:n1]).astype(BF)
-    quad_ref[...] = (leaf_ref[n1:] + r1_ref[n1:]) + (r2_ref[n1:] + r3_ref[n1:])
+    low_ref[1, :n0] = r1_ref[:n0]
+    low_ref[0, n0:] = (leaf_ref[n0:n1] + r1_ref[n0:n1].astype(F32)).astype(BF)
+    other = r2_ref[...].astype(F32) + r3_ref[...].astype(F32)
+    low_ref[1, n0:] = other[: n1 - n0].astype(BF)
+    quad = (leaf_ref[n1:] + r1_ref[n1:].astype(F32)) + other[n1 - n0 :]
+    quad_ref[...] = quad
+    send_ref[...] = quad.astype(BF)
+    upper_ref[...] = quad[FIRST[3] - n1 :].astype(BF)
 
 
 def cap_z_body(quad_ref, z1_ref, z2_ref, z3_ref, mid_ref, last_ref):
     n0, n1 = FIRST[3] - FIRST[2], FIRST[4] - FIRST[2]
+    other = z2_ref[...].astype(F32) + z3_ref[...].astype(F32)
     mid_ref[0, :n0] = quad_ref[:n0].astype(BF)
-    mid_ref[1, :n0] = z1_ref[:n0].astype(BF)
-    mid_ref[0, n0:] = (quad_ref[n0:n1] + z1_ref[n0:n1]).astype(BF)
-    mid_ref[1, n0:] = (z2_ref[n0:n1] + z3_ref[n0:n1]).astype(BF)
-    last_ref[...] = (quad_ref[n1:] + z1_ref[n1:]) + (z2_ref[n1:] + z3_ref[n1:])
+    mid_ref[1, :n0] = z1_ref[:n0]
+    mid_ref[0, n0:] = (quad_ref[n0:n1] + z1_ref[n0:n1].astype(F32)).astype(BF)
+    mid_ref[1, n0:] = other[: n1 - n0].astype(BF)
+    last_ref[...] = (quad_ref[n1:] + z1_ref[n1:].astype(F32)) + other[n1 - n0 :]
 
 
 def cap_both_body(low_ref, mid_ref, own4_ref, sib4_ref, both_ref):
@@ -332,14 +347,17 @@
     )(jnp.stack(chips), a_own, a_oth, *blocks)
 
 
-def project(block, y_refs, v_refs):
-    at = pl.ds(pl.multiple_of((block & (Y - 1)) * R, R), R)
+def project(blocks, y_refs, v_refs, q_refs):
     q = None
     for y_ref, v_ref in zip(y_refs, v_refs):
-        hi, lo = split(y_ref[:, at])
-        new = dot(v_ref[...], jnp.concatenate([hi, lo], axis=1))
+        parts = []
+        for block in blocks:
+            at = pl.ds(pl.multiple_of((block & (Y - 1)) * R, R), R)
+            parts.append(y_ref[:, at].astype(BF))
+        new = dot(v_ref[...], parts[0] if len(parts) == 1 else jnp.concatenate(parts, axis=1))
         q = new if q is None else q + new
-    return (q[:, :R] + q[:, R:]).astype(BF)
+    for k, q_ref in enumerate(q_refs):
+        q_ref[...] = q[:, k * R : (k + 1) * R].astype(BF)
 
 
 def leaf_end_body(
@@ -356,12 +374,11 @@
         new = dot(a_ref[...], far)
         live = (y * C + core) * rows + iota < size
         y_ref[...] = jnp.where(live, sum_ref[...] + new, 0.0)
-    for d, q_ref in enumerate(q_refs):
-        q_ref[...] = project(y + d + 1, y_refs, (va_ref, vb_ref))
+    project([y + d + 1 for d in range(len(q_refs))], y_refs, (va_ref, vb_ref), q_refs)
 
 
 def project_own_body(place_ref, y0_ref, y1_ref, va_ref, vb_ref, q_ref):
-    q_ref[...] = project(place_ref[0], (y0_ref, y1_ref), (va_ref, vb_ref))
+    project([place_ref[0]], (y0_ref, y1_ref), (va_ref, vb_ref), [q_ref])
 
 
 def eliminate_body(q0_ref, q1_ref, q2_ref, q3_ref, h_ref, e_ref, upper_ref):
@@ -526,7 +543,6 @@
     g = cap_factor[:, 0]
     struct = jax.ShapeDtypeStruct
 
-    a_oth = to_core(leaf_inverse)
     part_shape = struct((rows, columns // C), BF)
     mine, theirs = live_rhs(scalars, in_hbm(rhs))
     other = to_core(theirs)
@@ -543,28 +559,37 @@
     )(scalars, cap_mine, to_core(cap_theirs))
     part1, part2, part3 = to_y(s1, 1), to_y(s2, 2), to_y(s3, 3)
 
-    vt_oth = to_core(vt)
+    a_oth = to_core(after(leaf_inverse, own))
+    vt_oth = to_core(after(vt, own))
     chip = kernel_call(
         chip_body, struct((C * rows, columns // C), BF), 1, 2, name="chip"
-    )(scalars, after(mine, part1, a_oth, vt_oth), other)
-    before, behind = to_y(chip, 1), to_y(after(chip, part2, part3), -1)
-    cap_leaf = kernel_call(cap_leaf_body, struct((N_CAP, part, R), F32), 0, 4, name="cap_leaf")(
-        own, part1, part2, part3
-    )
-    low, cap_quad = kernel_call(
+    )(scalars, after(mine, part1, vt_oth), other)
+    before, behind = to_y(chip, 1), to_y(after(chip, part2, part3, a_oth), -1)
+    def blocks(n, kind):
+        return struct((n, part, R), kind)
+
+    n1, n2, n3 = N_CAP - FIRST[1], N_CAP - FIRST[2], N_CAP - FIRST[3]
+    cap_leaf, leaf_send, leaf_up = kernel_call(
+        cap_leaf_body,
+        (blocks(N_CAP, F32), blocks(N_CAP, BF), blocks(n1, BF)),
+        0,
+        4,
+        name="cap_leaf",
+    )(own, part1, part2, part3)
+    low, cap_quad, quad_send, cap_quad_up = kernel_call(
         cap_x_body,
-        (struct((2, FIRST[2], part, R), BF), struct((N_CAP - FIRST[2], part, R), F32)),
+        (struct((2, FIRST[2], part, R), BF), blocks(n2, F32), blocks(n2, BF), blocks(n3, BF)),
         0,
         4,
         name="cap_x",
-    )(cap_leaf, to_x(cap_leaf, 1), to_x(cap_leaf, 2), to_x(cap_leaf, 3))
+    )(cap_leaf, to_x(leaf_send, 1), to_x(leaf_up, 2), to_x(leaf_up, 3))
     mid, last = kernel_call(
         cap_z_body,
-        (struct((2, FIRST[4] - FIRST[2], part, R), BF), struct((1, part, R), F32)),
+        (struct((2, FIRST[4] - FIRST[2], part, R), BF), blocks(1, F32)),
         0,
         4,
         name="cap_z",
-    )(cap_quad, to_z(cap_quad, 1), to_z(cap_quad, 2), to_z(cap_quad, 3))
+    )(cap_quad, to_z(quad_send, 1), to_z(cap_quad_up, 2), to_z(cap_quad_up, 3))
     both = kernel_call(
         cap_both_body, struct((2 * N_CAP, part, R), BF), 0, 4, name="cap_both"
     )(low, mid, last, to_z(last, 4))
@@ -591,6 +616,7 @@
         3,
         scratch=[pltpu.VMEM((2 * N_CAP, R, R), BF)],
         name="elimination",
+        us=2.5,
     )(scalars, side, cap_rows, to_core(cap_rows), g)
 
     places = after(places, cap_rows)
@@ -600,9 +626,10 @@
         1,
         8,
         name="leaf_end",
+        us=4.0,
     )(places, far_own, far_oth, far_top, far_bottom, sum_own, sum_oth, vt, vt_oth)
     q_own = kernel_call(
-        project_own_body, struct((LEVELS * R, R), BF), 1, 4, name="project_own"
+        project_own_body, struct((LEVELS * R, R), BF), 1, 4, name="project_own", us=1.2
     )(places, y_own, y_oth, vt, vt_oth)
     y_other = to_core(y_oth)
 

time: 130 us -> 129 us (level)
  Pallas kernels: 31.9 us -> 28.8 us
  local copies, waits for them, and re-layouts: 0.03 us -> 2.92 us
  waiting for transfers between devices: 36.7 us -> 35.1 us
    unnamed x16 -> x24, local copies, waits for them, and re-layouts: 0.03 us -> 2.92 us
    ppermute x37, waiting for transfers between devices: 36.7 us -> 35.1 us  [move(): return lax.ppermute(block, ('partner', 'row'), route)]
  transfers between devices with their start and end apart: 37 -> 37, of which waited for: 20 -> 19; matrix products, arithmetic and copies ran while one was open for 0% -> 0% of each run, Pallas kernels for 16% -> 13%
where the time goes in v4:
time: 129 us
  starting transfers between devices  60.4 us (47%)
  waiting for transfers between devices  35.1 us (27%)
  Pallas kernels  28.8 us (22%)
  local copies, waits for them, and re-layouts  2.92 us (2%)
    ppermute x37, starting transfers between devices, move(): return lax.ppermute(block, ('partner', 'row'), route)  60.4 us
    ppermute x37, waiting for transfers between devices, move(): return lax.ppermute(block, ('partner', 'row'), route)  35.1 us
    pallas_call x1, Pallas kernels, leaf(): pl.pallas_call(leaf_body, out_shape=out_shape, in_specs=[pl.BlockSpec(mem...  5.63 us
    pallas_call x1, Pallas kernels, shards(): kernel_call(leaf_end_body, [struct((rows, columns // C), F32)] * 2 + [str...  3.36 us
    unnamed x24, local copies, waits for them, and re-layouts  2.92 us
  transfers between devices with their start and end apart: 37, of which 19 were waited for; matrix products, arithmetic and copies ran while one was open for 0% of the time, Pallas kernels for 13%

profile of v4, /device:TPU:1, one launch (start us, length us, event | category | flops | bytes accessed | tf_op | source)
XLA Modules:
  0.0 128.6 jit_solution(17214655711952172857)
XLA Ops:
  0.7 2.4 %prepare.1 = (bf16[640,512]{1,0:T(8,128)(2,1)S(1)}, f32[15,64,128]{2,1,0:T(8,128)S(1)}, f32[15,64,128]{2,1,0:T(8,128)S(1)}) custom-call(s32[4]{0:T(128)S(1)} %pad_add_fusion.scalar_ref, bf16[5,512,128]{2,1,0:T(8,128)(2,1)} %refs_2_.1, bf16[5,512,128]{2,1,0:T(8,128)(2,1)} %v_hbm.1), custom_call_target="tpu_custom_call" | custom-call | tf_op jit(solution)/shard_map/prepare/pallas_call | solution.py:195
  3.2 3.3 %collective-permute-start = (f32[15,64,128]{2,1,0:T(8,128)S(1)}, f32[15,64,128]{2,1,0:T(8,128)S(1)}, u32[]{:S(2)}, u32[]{:S(2)}) collective-permute-start(f32[15,64,128]{2,1,0:T(8,128)S(1)} %get-tuple-element.55), channel_id=1, source_target_pairs={{0,1},{1,0},{2,3},{3,2},{4,5},{5,4},{6,7},{7,6},{8,9},{9,8},{10,11... | collective-permute-start | bytes 1474568 | tf_op jit(solution)/shard_map/ppermute | solution.py:30
  9.2 2.1 %live_rhs.1 = (bf16[512,512]{1,0:T(8,128)(2,1)S(1)}, bf16[512,512]{1,0:T(8,128)(2,1)S(1)}) custom-call(s32[4]{0:T(128)S(1)} %pad_add_fusion.scalar_ref, f32[512,1024]{1,0:T(8,128)} %rhs_hbm.1), custom_call_target="tpu_custom_call" | custom-call | tf_op jit(solution)/shard_map/live_rhs/pallas_call | solution.py:129
  11.8 2.2 %collective-permute-start.2 = (bf16[15,16,128]{2,1,0:T(8,128)(2,1)S(1)}, bf16[15,16,128]{2,1,0:T(8,128)(2,1)S(1)}, u32[]{:S(2)}, u32[]{:S(2)}) collective-permute-start(bf16[15,16,128]{2,1,0:T(8,128)(2,1)S(1)} %get-tuple-element.58), channel_id=1, source_target_pairs={{0,4},{1,5},{2,6},{3,7},{4,0},{5,1},{6,2},{7,3},{8,12},{9,13},{10,... | collective-permute-start | bytes 184328 | tf_op jit(solution)/shard_map/ppermute | solution.py:30
  14.0 3.2 %collective-permute-done.1.r1_ref = bf16[15,16,128]{2,1,0:T(8,128)(2,1)S(1)} collective-permute-done((bf16[15,16,128]{2,1,0:T(8,128)(2,1)S(1)}, bf16[15,16,128]{2,1,0:T(8,128)(2,1)S(1)}, u32[]{:S(2)}, u32[]{:S(2)}) %collective-permute-start.1) | collective-permute-done | bytes 61472 | tf_op jit(solution)/shard_map/ppermute | solution.py:30
  29.8 2.8 %collective-permute-start.9 = (bf16[3,16,128]{2,1,0:T(8,128)(2,1)S(1)}, bf16[3,16,128]{2,1,0:T(8,128)(2,1)S(1)}, u32[]{:S(2)}, u32[]{:S(2)}) collective-permute-start(bf16[3,16,128]{2,1,0:T(8,128)(2,1)S(1)} %get-tuple-element.66), channel_id=1, source_target_pairs={{0,96},{1,97},{2,98},{3,99},{4,100},{5,101},{6,102},{7,103},{8,104... | collective-permute-start | bytes 36872 | tf_op jit(solution)/shard_map/ppermute | solution.py:30
  34.2 2.2 %collective-permute-done.8.z2_ref = bf16[3,16,128]{2,1,0:T(8,128)(2,1)S(1)} collective-permute-done((bf16[3,16,128]{2,1,0:T(8,128)(2,1)S(1)}, bf16[3,16,128]{2,1,0:T(8,128)(2,1)S(1)}, u32[]{:S(2)}, u32[]{:S(2)}) %collective-permute-start.8) | collective-permute-done | bytes 12320 | tf_op jit(solution)/shard_map/ppermute | solution.py:30
  36.4 4.9 %collective-permute-start.10 = (f32[1,16,128]{2,1,0:T(8,128)S(1)}, f32[1,16,128]{2,1,0:T(8,128)S(1)}, u32[]{:S(2)}, u32[]{:S(2)}) collective-permute-start(f32[1,16,128]{2,1,0:T(8,128)S(1)} %get-tuple-element.68.own4_ref), channel_id=1, source_target_pairs={{0,128},{1,129},{2,130},{3,131},{4,132},{5,133},{6,134},{7,135},{8... | collective-permute-start | bytes 24584 | tf_op jit(solution)/shard_map/ppermute | solution.py:30
  44.0 1.9 %collective-permute-start.20 = (bf16[512,512]{1,0:T(8,128)(2,1)}, bf16[512,512]{1,0:T(8,128)(2,1)}, u32[]{:S(2)}, u32[]{:S(2)}) collective-permute-start(bf16[512,512]{1,0:T(8,128)(2,1)} %get-tuple-element.82), channel_id=1, source_target_pairs={{0,6},{1,7},{2,0},{3,1},{4,2},{5,3},{6,4},{7,5},{8,14},{9,15},{10,... | collective-permute-start | bytes 1572872 | tf_op jit(solution)/shard_map/ppermute | solution.py:30
  45.9 3.9 %collective-permute-start.17 = (bf16[30,16,128]{2,1,0:T(8,128)(2,1)S(1)}, bf16[30,16,128]{2,1,0:T(8,128)(2,1)S(1)}, u32[]{:S(2)}, u32[]{:S(2)}) collective-permute-start(bf16[30,16,128]{2,1,0:T(8,128)(2,1)S(1)} %cap_both.1.b0_ref), channel_id=1, source_target_pairs={{0,4},{1,5},{2,6},{3,7},{4,0},{5,1},{6,2},{7,3},{8,12},{9,13},{10,... | collective-permute-start | bytes 368648 | tf_op jit(solution)/shard_map/ppermute | solution.py:30
  49.9 5.6 %leaf.1 = (f32[512,512]{1,0:T(8,128)S(1)}, f32[512,512]{1,0:T(8,128)S(1)}, bf16[512,1024]{1,0:T(8,128)(2,1)S(1)}, bf16[512,1024]{1,0:T(8,128)(2,1)S(1)}) custom-call(s32[4]{0:T(128)S(1)} %pad_add_fusion.2.chip_ref, bf16[512,4096]{1,0:T(8,128)(2,1)} %a0_hbm.1, bf16[512,4096]{1,0:T(8,128)(2,1)} %copy-done.11, bf16[1024,512]{1,0:T(8,128)(2,1)S(1)} %chip.1.b0_ref, ...), custom_call_target="tpu_custom_call" | custom-call | tf_op jit(solution)/shard_map/leaf/pallas_call | solution.py:336
  55.6 4.1 %collective-permute-done.18.b3_ref = bf16[30,16,128]{2,1,0:T(8,128)(2,1)S(1)} collective-permute-done((bf16[30,16,128]{2,1,0:T(8,128)(2,1)S(1)}, bf16[30,16,128]{2,1,0:T(8,128)(2,1)S(1)}, u32[]{:S(2)}, u32[]{:S(2)}) %collective-permute-start.18) | collective-permute-done | bytes 122912 | tf_op jit(solution)/shard_map/ppermute | solution.py:30
  60.7 3.4 %leaf_end.1 = (f32[512,512]{1,0:T(8,128)S(1)}, f32[512,512]{1,0:T(8,128)S(1)}, bf16[640,128]{1,0:T(8,128)(2,1)S(1)}, bf16[640,128]{1,0:T(8,128)(2,1)S(1)}, bf16[640,128]{1,0:T(8,128)(2,1)S(1)}) custom-call(s32[3]{0:T(128)S(1)} %pad_add_fusion.1.scalar_ref.place_ref, bf16[512,1024]{1,0:T(8,128)(2,1)S(1)} %get-tuple-element.80.a0_ref, ...), custom_call_target="tpu_custom_call" | custom-call | flops 4400000000 | bytes 4000000 | tf_op jit(solution)/shard_map/leaf_end/pallas_call | solution.py:623
  64.8 7.3 %collective-permute-start.21 = (f32[512,512]{1,0:T(8,128)S(1)}, f32[512,512]{1,0:T(8,128)}, u32[]{:S(2)}, u32[]{:S(2)}) collective-permute-start(f32[512,512]{1,0:T(8,128)S(1)} %get-tuple-element.86.y1_ref), channel_id=1, source_target_pairs={{0,1},{1,0},{2,3},{3,2},{4,5},{5,4},{6,7},{7,6},{8,9},{9,8},{10,11... | collective-permute-start | bytes 3145736 | tf_op jit(solution)/shard_map/ppermute | solution.py:30
  78.1 2.4 %elimination.1 = (bf16[1280,256]{1,0:T(8,128)(2,1)S(1)}, bf16[5,2,128,128]{3,2,1,0:T(8,128)(2,1)S(1)}) custom-call(s32[4]{0:T(128)S(1)} %pad_add_fusion.scalar_ref, s32[5]{0:T(128)S(1)} %shift-right-arithmetic_and_fusion.side_ref.refs_0_, bf16[30,64,128]{2,1,0:T(8,128)(2,1)S(1)} %cap_stack.1.mine_ref, ...), custom_call_target="tpu_custom_call" | custom-call | flops 2750000128 | bytes 2500000 | tf_op jit(solution)/shard_map/elimination/pallas_call | solution.py:612
  88.7 3.5 %collective-permute-done.27.r2_ref.refs_5_ = bf16[512,128]{1,0:T(8,128)(2,1)S(1)} collective-permute-done((bf16[512,128]{1,0:T(8,128)(2,1)S(1)}, bf16[512,128]{1,0:T(8,128)(2,1)S(1)}, u32[]{:S(2)}, u32[]{:S(2)}) %collective-permute-start.27) | collective-permute-done | bytes 131104 | tf_op jit(solution)/shard_map/ppermute | solution.py:30
  94.0 2.8 %collective-permute-start.31 = (bf16[256,128]{1,0:T(8,128)(2,1)S(1)}, bf16[256,128]{1,0:T(8,128)(2,1)S(1)}, u32[]{:S(2)}, u32[]{:S(2)}) collective-permute-start(bf16[256,128]{1,0:T(8,128)(2,1)S(1)} %get-tuple-element.101), channel_id=1, source_target_pairs={{0,96},{1,97},{2,98},{3,99},{4,100},{5,101},{6,102},{7,103},{8,104... | collective-permute-start | bytes 196616 | tf_op jit(solution)/shard_map/ppermute | solution.py:30
  99.4 2.8 %collective-permute-done.30.z2_ref.refs_5_ = bf16[256,128]{1,0:T(8,128)(2,1)S(1)} collective-permute-done((bf16[256,128]{1,0:T(8,128)(2,1)S(1)}, bf16[256,128]{1,0:T(8,128)(2,1)S(1)}, u32[]{:S(2)}, u32[]{:S(2)}) %collective-permute-start.30) | collective-permute-done | bytes 65568 | tf_op jit(solution)/shard_map/ppermute | solution.py:30
  102.2 4.6 %collective-permute-start.32 = (bf16[128,128]{1,0:T(8,128)(2,1)S(1)}, bf16[128,128]{1,0:T(8,128)(2,1)S(1)}, u32[]{:S(2)}, u32[]{:S(2)}) collective-permute-start(bf16[128,128]{1,0:T(8,128)(2,1)S(1)} %own4.1.a_ref), channel_id=1, source_target_pairs={{0,128},{1,129},{2,130},{3,131},{4,132},{5,133},{6,134},{7,135},{8... | collective-permute-start | bytes 98312 | tf_op jit(solution)/shard_map/ppermute | solution.py:30
  110.0 3.2 %collective-permute-start.35 = (bf16[640,128]{1,0:T(8,128)(2,1)S(1)}, bf16[640,128]{1,0:T(8,128)(2,1)S(1)}, u32[]{:S(2)}, u32[]{:S(2)}) collective-permute-start(bf16[640,128]{1,0:T(8,128)(2,1)S(1)} %solve_4.1.b0_ref), channel_id=1, source_target_pairs={{0,2},{1,3},{2,4},{3,5},{4,6},{5,7},{6,0},{7,1},{8,10},{9,11},{10,... | collective-permute-start | bytes 491528 | tf_op jit(solution)/shard_map/ppermute | solution.py:30
  113.2 2.2 %collective-permute-start.34 = (bf16[640,128]{1,0:T(8,128)(2,1)S(1)}, bf16[640,128]{1,0:T(8,128)(2,1)S(1)}, u32[]{:S(2)}, u32[]{:S(2)}) collective-permute-start(bf16[640,128]{1,0:T(8,128)(2,1)S(1)} %solve_4.1.b0_ref), channel_id=1, source_target_pairs={{0,4},{1,5},{2,6},{3,7},{4,0},{5,1},{6,2},{7,3},{8,12},{9,13},{10,... | collective-permute-start | bytes 491528 | tf_op jit(solution)/shard_map/ppermute | solution.py:30
  116.9 3.1 %collective-permute-done.34.b2_ref = bf16[640,128]{1,0:T(8,128)(2,1)S(1)} collective-permute-done((bf16[640,128]{1,0:T(8,128)(2,1)S(1)}, bf16[640,128]{1,0:T(8,128)(2,1)S(1)}, u32[]{:S(2)}, u32[]{:S(2)}) %collective-permute-start.34) | collective-permute-done | bytes 163872 | tf_op jit(solution)/shard_map/ppermute | solution.py:30
  120.4 3.9 %collective-permute-start.36 = (bf16[640,512]{1,0:T(8,128)(2,1)S(1)}, bf16[640,512]{1,0:T(8,128)(2,1)S(1)}, u32[]{:S(2)}, u32[]{:S(2)}) collective-permute-start(bf16[640,512]{1,0:T(8,128)(2,1)S(1)} %columns.1.t0_ref), channel_id=1, source_target_pairs={{0,1},{1,0},{2,3},{3,2},{4,5},{5,4},{6,7},{7,6},{8,9},{9,8},{10,11... | collective-permute-start | bytes 1966088 | tf_op jit(solution)/shard_map/ppermute | solution.py:30
  126.0 2.4 %update.1 = f32[512,1024]{1,0:T(8,128)} custom-call(s32[4]{0:T(128)S(1)} %pad_add_fusion.scalar_ref, f32[512,512]{1,0:T(8,128)S(1)} %get-tuple-element.87.y0_ref, f32[512,512]{1,0:T(8,128)S(1)} %get-tuple-element.88.y1_ref, bf16[5,512,128]{2,1,0:T(8,128)(2,1)S(1)} %get-tuple-element.89.u_ref, bf16[640,512]{1,0:T(8,128)(2,1)S(1)} %columns.1.t0_ref, ...), custom_call_target="tpu_custom_call" | custom-call | tf_op jit(solution)/shard_map/update/pallas_call | solution.py:525
  (101 shorter events, 47.2 us)
Async XLA Ops:
  8.6 11.6 %collective-permute-start.14 = (bf16[512,4096]{1,0:T(8,128)(2,1)}, bf16[512,4096]{1,0:T(8,128)(2,1)S(1)}, u32[]{:S(2)}, u32[]{:S(2)}) collective-permute-start(bf16[512,4096]{1,0:T(8,128)(2,1)} %a0_hbm.1), channel_id=1, source_target_pairs={{0,1},{1,0},{2,3},{3,2},{4,5},{5,4},{6,7},{7,6},{8,9},{9,8},{10,11... | collective-permute-start | bytes 12582920 | tf_op jit(solution)/shard_map/ppermute | solution.py:30
  9.1 8.1 %collective-permute-start.11 = (bf16[640,512]{1,0:T(8,128)(2,1)S(1)}, bf16[640,512]{1,0:T(8,128)(2,1)S(1)}, u32[]{:S(2)}, u32[]{:S(2)}) collective-permute-start(bf16[640,512]{1,0:T(8,128)(2,1)S(1)} %get-tuple-element.71.va_ref), channel_id=1, source_target_pairs={{0,1},{1,0},{2,3},{3,2},{4,5},{5,4},{6,7},{7,6},{8,9},{9,8},{10,11... | collective-permute-start | bytes 1966088 | tf_op jit(solution)/shard_map/ppermute | solution.py:30
  11.8 7.5 %collective-permute-start.2 = (bf16[15,16,128]{2,1,0:T(8,128)(2,1)S(1)}, bf16[15,16,128]{2,1,0:T(8,128)(2,1)S(1)}, u32[]{:S(2)}, u32[]{:S(2)}) collective-permute-start(bf16[15,16,128]{2,1,0:T(8,128)(2,1)S(1)} %get-tuple-element.58), channel_id=1, source_target_pairs={{0,4},{1,5},{2,6},{3,7},{4,0},{5,1},{6,2},{7,3},{8,12},{9,13},{10,... | collective-permute-start | bytes 184328 | tf_op jit(solution)/shard_map/ppermute | solution.py:30
  17.8 25.1 %collective-permute-start.13 = (bf16[1024,512]{1,0:T(8,128)(2,1)S(1)}, bf16[1024,512]{1,0:T(8,128)(2,1)S(1)}, u32[]{:S(2)}, u32[]{:S(2)}) collective-permute-start(bf16[1024,512]{1,0:T(8,128)(2,1)S(1)} %chip.1.b0_ref), channel_id=1, source_target_pairs={{0,2},{1,3},{2,4},{3,5},{4,6},{5,7},{6,0},{7,1},{8,10},{9,11},{10,... | collective-permute-start | bytes 3145736 | tf_op jit(solution)/shard_map/ppermute | solution.py:30
  20.2 22.7 %collective-permute-start.15 = (bf16[1024,512]{1,0:T(8,128)(2,1)S(1)}, bf16[1024,512]{1,0:T(8,128)(2,1)S(1)}, u32[]{:S(2)}, u32[]{:S(2)}) collective-permute-start(bf16[1024,512]{1,0:T(8,128)(2,1)S(1)} %chip.1.b0_ref), channel_id=1, source_target_pairs={{0,6},{1,7},{2,0},{3,1},{4,2},{5,3},{6,4},{7,5},{8,14},{9,15},{10,... | collective-permute-start | bytes 3145736 | tf_op jit(solution)/shard_map/ppermute | solution.py:30
  21.5 6.6 %collective-permute-start.4 = (bf16[15,16,128]{2,1,0:T(8,128)(2,1)S(1)}, bf16[15,16,128]{2,1,0:T(8,128)(2,1)S(1)}, u32[]{:S(2)}, u32[]{:S(2)}) collective-permute-start(bf16[15,16,128]{2,1,0:T(8,128)(2,1)S(1)} %get-tuple-element.61), channel_id=1, source_target_pairs={{0,8},{1,9},{2,10},{3,11},{4,12},{5,13},{6,14},{7,15},{8,0},{9,1},... | collective-permute-start | bytes 184328 | tf_op jit(solution)/shard_map/ppermute | solution.py:30
  28.1 8.3 %collective-permute-start.7 = (bf16[6,16,128]{2,1,0:T(8,128)(2,1)S(1)}, bf16[6,16,128]{2,1,0:T(8,128)(2,1)S(1)}, u32[]{:S(2)}, u32[]{:S(2)}) collective-permute-start(bf16[6,16,128]{2,1,0:T(8,128)(2,1)S(1)} %get-tuple-element.65), channel_id=1, source_target_pairs={{0,32},{1,33},{2,34},{3,35},{4,36},{5,37},{6,38},{7,39},{8,40},{9,... | collective-permute-start | bytes 73736 | tf_op jit(solution)/shard_map/ppermute | solution.py:30
  36.4 6.5 %collective-permute-start.10 = (f32[1,16,128]{2,1,0:T(8,128)S(1)}, f32[1,16,128]{2,1,0:T(8,128)S(1)}, u32[]{:S(2)}, u32[]{:S(2)}) collective-permute-start(f32[1,16,128]{2,1,0:T(8,128)S(1)} %get-tuple-element.68.own4_ref), channel_id=1, source_target_pairs={{0,128},{1,129},{2,130},{3,131},{4,132},{5,133},{6,134},{7,135},{8... | collective-permute-start | bytes 24584 | tf_op jit(solution)/shard_map/ppermute | solution.py:30
  44.0 16.7 %collective-permute-start.20 = (bf16[512,512]{1,0:T(8,128)(2,1)}, bf16[512,512]{1,0:T(8,128)(2,1)}, u32[]{:S(2)}, u32[]{:S(2)}) collective-permute-start(bf16[512,512]{1,0:T(8,128)(2,1)} %get-tuple-element.82), channel_id=1, source_target_pairs={{0,6},{1,7},{2,0},{3,1},{4,2},{5,3},{6,4},{7,5},{8,14},{9,15},{10,... | collective-permute-start | bytes 1572872 | tf_op jit(solution)/shard_map/ppermute | solution.py:30
  45.9 14.7 %collective-permute-start.19 = (bf16[512,512]{1,0:T(8,128)(2,1)}, bf16[512,512]{1,0:T(8,128)(2,1)}, u32[]{:S(2)}, u32[]{:S(2)}) collective-permute-start(bf16[512,512]{1,0:T(8,128)(2,1)} %get-tuple-element.77), channel_id=1, source_target_pairs={{0,2},{1,3},{2,4},{3,5},{4,6},{5,7},{6,0},{7,1},{8,10},{9,11},{10,... | collective-permute-start | bytes 1572872 | tf_op jit(solution)/shard_map/ppermute | solution.py:30
  45.9 13.8 %collective-permute-start.18 = (bf16[30,16,128]{2,1,0:T(8,128)(2,1)S(1)}, bf16[30,16,128]{2,1,0:T(8,128)(2,1)S(1)}, u32[]{:S(2)}, u32[]{:S(2)}) collective-permute-start(bf16[30,16,128]{2,1,0:T(8,128)(2,1)S(1)} %cap_both.1.b0_ref), channel_id=1, source_target_pairs={{0,2},{1,3},{2,4},{3,5},{4,6},{5,7},{6,0},{7,1},{8,10},{9,11},{10,... | collective-permute-start | bytes 368648 | tf_op jit(solution)/shard_map/ppermute | solution.py:30
  45.9 13.8 %collective-permute-start.17 = (bf16[30,16,128]{2,1,0:T(8,128)(2,1)S(1)}, bf16[30,16,128]{2,1,0:T(8,128)(2,1)S(1)}, u32[]{:S(2)}, u32[]{:S(2)}) collective-permute-start(bf16[30,16,128]{2,1,0:T(8,128)(2,1)S(1)} %cap_both.1.b0_ref), channel_id=1, source_target_pairs={{0,4},{1,5},{2,6},{3,7},{4,0},{5,1},{6,2},{7,3},{8,12},{9,13},{10,... | collective-permute-start | bytes 368648 | tf_op jit(solution)/shard_map/ppermute | solution.py:30
  49.8 9.9 %collective-permute-start.16 = (bf16[30,16,128]{2,1,0:T(8,128)(2,1)S(1)}, bf16[30,16,128]{2,1,0:T(8,128)(2,1)}, u32[]{:S(2)}, u32[]{:S(2)}) collective-permute-start(bf16[30,16,128]{2,1,0:T(8,128)(2,1)S(1)} %cap_both.1.b0_ref), channel_id=1, source_target_pairs={{0,6},{1,7},{2,0},{3,1},{4,2},{5,3},{6,4},{7,5},{8,14},{9,15},{10,... | collective-permute-start | bytes 368648 | tf_op jit(solution)/shard_map/ppermute | solution.py:30
  64.8 15.8 %collective-permute-start.21 = (f32[512,512]{1,0:T(8,128)S(1)}, f32[512,512]{1,0:T(8,128)}, u32[]{:S(2)}, u32[]{:S(2)}) collective-permute-start(f32[512,512]{1,0:T(8,128)S(1)} %get-tuple-element.86.y1_ref), channel_id=1, source_target_pairs={{0,1},{1,0},{2,3},{3,2},{4,5},{5,4},{6,7},{7,6},{8,9},{9,8},{10,11... | collective-permute-start | bytes 3145736 | tf_op jit(solution)/shard_map/ppermute | solution.py:30
  72.1 6.0 %collective-permute-start.22 = (bf16[30,64,128]{2,1,0:T(8,128)(2,1)S(1)}, bf16[30,64,128]{2,1,0:T(8,128)(2,1)S(1)}, u32[]{:S(2)}, u32[]{:S(2)}) collective-permute-start(bf16[30,64,128]{2,1,0:T(8,128)(2,1)S(1)} %cap_stack.1.mine_ref), channel_id=1, source_target_pairs={{0,1},{1,0},{2,3},{3,2},{4,5},{5,4},{6,7},{7,6},{8,9},{9,8},{10,11... | collective-permute-start | bytes 1474568 | tf_op jit(solution)/shard_map/ppermute | solution.py:30
  72.1 10.3 %collective-permute-start.23 = (bf16[640,128]{1,0:T(8,128)(2,1)}, bf16[640,128]{1,0:T(8,128)(2,1)S(1)}, u32[]{:S(2)}, u32[]{:S(2)}) collective-permute-start(bf16[640,128]{1,0:T(8,128)(2,1)} %copy-done.10), channel_id=1, source_target_pairs={{0,2},{1,3},{2,4},{3,5},{4,6},{5,7},{6,0},{7,1},{8,10},{9,11},{10,... | collective-permute-start | bytes 491528 | tf_op jit(solution)/shard_map/ppermute | solution.py:30
  72.2 10.3 %collective-permute-start.24 = (bf16[640,128]{1,0:T(8,128)(2,1)}, bf16[640,128]{1,0:T(8,128)(2,1)S(1)}, u32[]{:S(2)}, u32[]{:S(2)}) collective-permute-start(bf16[640,128]{1,0:T(8,128)(2,1)} %copy-done.9), channel_id=1, source_target_pairs={{0,4},{1,5},{2,6},{3,7},{4,0},{5,1},{6,2},{7,3},{8,12},{9,13},{10,... | collective-permute-start | bytes 491528 | tf_op jit(solution)/shard_map/ppermute | solution.py:30
  73.5 9.3 %collective-permute-start.25 = (bf16[640,128]{1,0:T(8,128)(2,1)}, bf16[640,128]{1,0:T(8,128)(2,1)S(1)}, u32[]{:S(2)}, u32[]{:S(2)}) collective-permute-start(bf16[640,128]{1,0:T(8,128)(2,1)} %copy-done.8), channel_id=1, source_target_pairs={{0,6},{1,7},{2,0},{3,1},{4,2},{5,3},{6,4},{7,5},{8,14},{9,15},{10,... | collective-permute-start | bytes 491528 | tf_op jit(solution)/shard_map/ppermute | solution.py:30
  83.5 8.7 %collective-permute-start.26 = (bf16[640,128]{1,0:T(8,128)(2,1)S(1)}, bf16[640,128]{1,0:T(8,128)(2,1)S(1)}, u32[]{:S(2)}, u32[]{:S(2)}) collective-permute-start(bf16[640,128]{1,0:T(8,128)(2,1)S(1)} %get-tuple-element.99.e_ref.refs_3_), channel_id=1, source_target_pairs={{0,8},{1,9},{2,10},{3,11},{4,12},{5,13},{6,14},{7,15},{8,0},{9,1},... | collective-permute-start | bytes 491528 | tf_op jit(solution)/shard_map/ppermute | solution.py:30
  85.5 6.7 %collective-permute-start.27 = (bf16[512,128]{1,0:T(8,128)(2,1)S(1)}, bf16[512,128]{1,0:T(8,128)(2,1)S(1)}, u32[]{:S(2)}, u32[]{:S(2)}) collective-permute-start(bf16[512,128]{1,0:T(8,128)(2,1)S(1)} %get-tuple-element.97), channel_id=1, source_target_pairs={{0,16},{1,17},{2,18},{3,19},{4,20},{5,21},{6,22},{7,23},{8,24},{9,... | collective-permute-start | bytes 393224 | tf_op jit(solution)/shard_map/ppermute | solution.py:30
  92.2 9.9 %collective-permute-start.29 = (bf16[384,128]{1,0:T(8,128)(2,1)S(1)}, bf16[384,128]{1,0:T(8,128)(2,1)S(1)}, u32[]{:S(2)}, u32[]{:S(2)}) collective-permute-start(bf16[384,128]{1,0:T(8,128)(2,1)S(1)} %get-tuple-element.102.quad_ref.refs_3_), channel_id=1, source_target_pairs={{0,32},{1,33},{2,34},{3,35},{4,36},{5,37},{6,38},{7,39},{8,40},{9,... | collective-permute-start | bytes 294920 | tf_op jit(solution)/shard_map/ppermute | solution.py:30
  102.2 6.8 %collective-permute-start.32 = (bf16[128,128]{1,0:T(8,128)(2,1)S(1)}, bf16[128,128]{1,0:T(8,128)(2,1)S(1)}, u32[]{:S(2)}, u32[]{:S(2)}) collective-permute-start(bf16[128,128]{1,0:T(8,128)(2,1)S(1)} %own4.1.a_ref), channel_id=1, source_target_pairs={{0,128},{1,129},{2,130},{3,131},{4,132},{5,133},{6,134},{7,135},{8... | collective-permute-start | bytes 98312 | tf_op jit(solution)/shard_map/ppermute | solution.py:30
  110.0 6.9 %collective-permute-start.35 = (bf16[640,128]{1,0:T(8,128)(2,1)S(1)}, bf16[640,128]{1,0:T(8,128)(2,1)S(1)}, u32[]{:S(2)}, u32[]{:S(2)}) collective-permute-start(bf16[640,128]{1,0:T(8,128)(2,1)S(1)} %solve_4.1.b0_ref), channel_id=1, source_target_pairs={{0,2},{1,3},{2,4},{3,5},{4,6},{5,7},{6,0},{7,1},{8,10},{9,11},{10,... | collective-permute-start | bytes 491528 | tf_op jit(solution)/shard_map/ppermute | solution.py:30
  113.2 6.9 %collective-permute-start.34 = (bf16[640,128]{1,0:T(8,128)(2,1)S(1)}, bf16[640,128]{1,0:T(8,128)(2,1)S(1)}, u32[]{:S(2)}, u32[]{:S(2)}) collective-permute-start(bf16[640,128]{1,0:T(8,128)(2,1)S(1)} %solve_4.1.b0_ref), channel_id=1, source_target_pairs={{0,4},{1,5},{2,6},{3,7},{4,0},{5,1},{6,2},{7,3},{8,12},{9,13},{10,... | collective-permute-start | bytes 491528 | tf_op jit(solution)/shard_map/ppermute | solution.py:30
  (25 other events, 220.9 us)

commit v5 on v4

--- a/solution.py
+++ b/solution.py
@@ -133,6 +133,7 @@
         out_specs=(vmem, vmem),
         scratch_shapes=[pltpu.VMEM(rhs.shape, F32), pltpu.SemaphoreType.DMA((4,))],
         compiler_params=pltpu.CompilerParams(vmem_limit_bytes=VMEM_LIMIT),
+        cost_estimate=cost(2.1),
         name="live_rhs",
     )(scalars, rhs)
 
@@ -343,6 +344,7 @@
             pltpu.SemaphoreType.DMA((Y, 2)),
         ],
         compiler_params=pltpu.CompilerParams(vmem_limit_bytes=VMEM_LIMIT),
+        cost_estimate=cost(5.6),
         name="leaf",
     )(jnp.stack(chips), a_own, a_oth, *blocks)
 

time: 129 us -> 126 us (0.977)
  Pallas kernels: 28.8 us -> 27.3 us
    unnamed x24 -> x18, local copies, waits for them, and re-layouts: 2.92 us -> 2.21 us
  transfers between devices with their start and end apart: 37 -> 37, of which waited for: 19 -> 18; matrix products, arithmetic and copies ran while one was open for 0% -> 0% of each run, Pallas kernels for 13% -> 14%
where the time goes in v5:
time: 126 us
  starting transfers between devices  59.8 us (47%)
  waiting for transfers between devices  35.1 us (28%)
  Pallas kernels  27.3 us (22%)
  local copies, waits for them, and re-layouts  2.21 us (2%)
    ppermute x37, starting transfers between devices, move(): return lax.ppermute(block, ('partner', 'row'), route)  59.8 us
    ppermute x37, waiting for transfers between devices, move(): return lax.ppermute(block, ('partner', 'row'), route)  35.1 us
    pallas_call x1, Pallas kernels, leaf(): pl.pallas_call(leaf_body, out_shape=out_shape, in_specs=[pl.BlockSpec(mem...  5.62 us
    pallas_call x1, Pallas kernels, shards(): kernel_call(elimination_body, (struct((N_H * R, 2 * R), BF), struct((LEVE...  2.92 us
    pallas_call x1, Pallas kernels, shards(): kernel_call(leaf_end_body, [struct((rows, columns // C), F32)] * 2 + [str...  2.66 us
  transfers between devices with their start and end apart: 37, of which 18 were waited for; matrix products, arithmetic and copies ran while one was open for 0% of the time, Pallas kernels for 14%

profile of v5, /device:TPU:1, one launch (start us, length us, event | category | flops | bytes accessed | tf_op | source)
XLA Modules:
  0.0 125.8 jit_solution(781255546087060683)
XLA Ops:
  0.7 2.4 %prepare.1 = (bf16[640,512]{1,0:T(8,128)(2,1)S(1)}, f32[15,64,128]{2,1,0:T(8,128)S(1)}, f32[15,64,128]{2,1,0:T(8,128)S(1)}) custom-call(s32[4]{0:T(128)S(1)} %pad_add_fusion.scalar_ref, bf16[5,512,128]{2,1,0:T(8,128)(2,1)} %refs_2_.1, bf16[5,512,128]{2,1,0:T(8,128)(2,1)} %v_hbm.1), custom_call_target="tpu_custom_call" | custom-call | tf_op jit(solution)/shard_map/prepare/pallas_call | solution.py:196
  3.2 3.3 %collective-permute-start = (f32[15,64,128]{2,1,0:T(8,128)S(1)}, f32[15,64,128]{2,1,0:T(8,128)S(1)}, u32[]{:S(2)}, u32[]{:S(2)}) collective-permute-start(f32[15,64,128]{2,1,0:T(8,128)S(1)} %get-tuple-element.55), channel_id=1, source_target_pairs={{0,1},{1,0},{2,3},{3,2},{4,5},{5,4},{6,7},{7,6},{8,9},{9,8},{10,11... | collective-permute-start | bytes 1474568 | tf_op jit(solution)/shard_map/ppermute | solution.py:30
  9.2 2.1 %live_rhs.1 = (bf16[512,512]{1,0:T(8,128)(2,1)S(1)}, bf16[512,512]{1,0:T(8,128)(2,1)S(1)}) custom-call(s32[4]{0:T(128)S(1)} %pad_add_fusion.scalar_ref, f32[512,1024]{1,0:T(8,128)} %rhs_hbm.1), custom_call_target="tpu_custom_call" | custom-call | flops 2310000128 | bytes 2100000 | tf_op jit(solution)/shard_map/live_rhs/pallas_call | solution.py:129
  11.8 2.2 %collective-permute-start.2 = (bf16[15,16,128]{2,1,0:T(8,128)(2,1)S(1)}, bf16[15,16,128]{2,1,0:T(8,128)(2,1)S(1)}, u32[]{:S(2)}, u32[]{:S(2)}) collective-permute-start(bf16[15,16,128]{2,1,0:T(8,128)(2,1)S(1)} %get-tuple-element.58), channel_id=1, source_target_pairs={{0,4},{1,5},{2,6},{3,7},{4,0},{5,1},{6,2},{7,3},{8,12},{9,13},{10,... | collective-permute-start | bytes 184328 | tf_op jit(solution)/shard_map/ppermute | solution.py:30
  14.0 3.2 %collective-permute-done.1.r1_ref = bf16[15,16,128]{2,1,0:T(8,128)(2,1)S(1)} collective-permute-done((bf16[15,16,128]{2,1,0:T(8,128)(2,1)S(1)}, bf16[15,16,128]{2,1,0:T(8,128)(2,1)S(1)}, u32[]{:S(2)}, u32[]{:S(2)}) %collective-permute-start.1) | collective-permute-done | bytes 61472 | tf_op jit(solution)/shard_map/ppermute | solution.py:30
  28.1 4.4 %collective-permute-start.9 = (bf16[3,16,128]{2,1,0:T(8,128)(2,1)S(1)}, bf16[3,16,128]{2,1,0:T(8,128)(2,1)S(1)}, u32[]{:S(2)}, u32[]{:S(2)}) collective-permute-start(bf16[3,16,128]{2,1,0:T(8,128)(2,1)S(1)} %get-tuple-element.66), channel_id=1, source_target_pairs={{0,96},{1,97},{2,98},{3,99},{4,100},{5,101},{6,102},{7,103},{8,104... | collective-permute-start | bytes 36872 | tf_op jit(solution)/shard_map/ppermute | solution.py:30
  33.6 2.7 %collective-permute-done.8.z2_ref = bf16[3,16,128]{2,1,0:T(8,128)(2,1)S(1)} collective-permute-done((bf16[3,16,128]{2,1,0:T(8,128)(2,1)S(1)}, bf16[3,16,128]{2,1,0:T(8,128)(2,1)S(1)}, u32[]{:S(2)}, u32[]{:S(2)}) %collective-permute-start.8) | collective-permute-done | bytes 12320 | tf_op jit(solution)/shard_map/ppermute | solution.py:30
  36.3 4.3 %collective-permute-start.10 = (f32[1,16,128]{2,1,0:T(8,128)S(1)}, f32[1,16,128]{2,1,0:T(8,128)S(1)}, u32[]{:S(2)}, u32[]{:S(2)}) collective-permute-start(f32[1,16,128]{2,1,0:T(8,128)S(1)} %get-tuple-element.68.own4_ref), channel_id=1, source_target_pairs={{0,128},{1,129},{2,130},{3,131},{4,132},{5,133},{6,134},{7,135},{8... | collective-permute-start | bytes 24584 | tf_op jit(solution)/shard_map/ppermute | solution.py:30
  43.0 3.2 %collective-permute-start.17 = (bf16[30,16,128]{2,1,0:T(8,128)(2,1)S(1)}, bf16[30,16,128]{2,1,0:T(8,128)(2,1)S(1)}, u32[]{:S(2)}, u32[]{:S(2)}) collective-permute-start(bf16[30,16,128]{2,1,0:T(8,128)(2,1)S(1)} %cap_both.1.b0_ref), channel_id=1, source_target_pairs={{0,4},{1,5},{2,6},{3,7},{4,0},{5,1},{6,2},{7,3},{8,12},{9,13},{10,... | collective-permute-start | bytes 368648 | tf_op jit(solution)/shard_map/ppermute | solution.py:30
  48.9 5.6 %leaf.1 = (f32[512,512]{1,0:T(8,128)S(1)}, f32[512,512]{1,0:T(8,128)S(1)}, bf16[512,1024]{1,0:T(8,128)(2,1)S(1)}, bf16[512,1024]{1,0:T(8,128)(2,1)S(1)}) custom-call(s32[4]{0:T(128)S(1)} %pad_add_fusion.2.chip_ref, bf16[512,4096]{1,0:T(8,128)(2,1)} %a0_hbm.1, bf16[512,4096]{1,0:T(8,128)(2,1)} %copy-done.8, bf16[1024,512]{1,0:T(8,128)(2,1)S(1)} %chip.1.b0_ref, ...), custom_call_target="tpu_custom_call" | custom-call | flops 6160000000 | bytes 5600000 | tf_op jit(solution)/shard_map/leaf/pallas_call | solution.py:337
  55.2 2.1 %collective-permute-done.20.bottom_ref = bf16[512,512]{1,0:T(8,128)(2,1)S(1)} collective-permute-done((bf16[512,512]{1,0:T(8,128)(2,1)S(1)}, bf16[512,512]{1,0:T(8,128)(2,1)S(1)}, u32[]{:S(2)}, u32[]{:S(2)}) %collective-permute-start.20) | collective-permute-done | bytes 524320 | tf_op jit(solution)/shard_map/ppermute | solution.py:30
  58.5 2.7 %leaf_end.1 = (f32[512,512]{1,0:T(8,128)S(1)}, f32[512,512]{1,0:T(8,128)S(1)}, bf16[640,128]{1,0:T(8,128)(2,1)S(1)}, bf16[640,128]{1,0:T(8,128)(2,1)S(1)}, bf16[640,128]{1,0:T(8,128)(2,1)S(1)}) custom-call(s32[3]{0:T(128)S(1)} %pad_add_fusion.1.scalar_ref.place_ref, bf16[512,1024]{1,0:T(8,128)(2,1)S(1)} %get-tuple-element.80.a0_ref, ...), custom_call_target="tpu_custom_call" | custom-call | flops 4400000000 | bytes 4000000 | tf_op jit(solution)/shard_map/leaf_end/pallas_call | solution.py:625
  61.1 6.3 %collective-permute-start.21 = (f32[512,512]{1,0:T(8,128)S(1)}, f32[512,512]{1,0:T(8,128)}, u32[]{:S(2)}, u32[]{:S(2)}) collective-permute-start(f32[512,512]{1,0:T(8,128)S(1)} %get-tuple-element.86.y1_ref), channel_id=1, source_target_pairs={{0,1},{1,0},{2,3},{3,2},{4,5},{5,4},{6,7},{7,6},{8,9},{9,8},{10,11... | collective-permute-start | bytes 3145736 | tf_op jit(solution)/shard_map/ppermute | solution.py:30
  67.8 3.3 %collective-permute-start.24 = (bf16[640,128]{1,0:T(8,128)(2,1)S(1)}, bf16[640,128]{1,0:T(8,128)(2,1)S(1)}, u32[]{:S(2)}, u32[]{:S(2)}) collective-permute-start(bf16[640,128]{1,0:T(8,128)(2,1)S(1)} %get-tuple-element.92), channel_id=1, source_target_pairs={{0,4},{1,5},{2,6},{3,7},{4,0},{5,1},{6,2},{7,3},{8,12},{9,13},{10,... | collective-permute-start | bytes 491528 | tf_op jit(solution)/shard_map/ppermute | solution.py:30
  74.4 2.9 %elimination.1 = (bf16[1280,256]{1,0:T(8,128)(2,1)S(1)}, bf16[5,2,128,128]{3,2,1,0:T(8,128)(2,1)S(1)}) custom-call(s32[4]{0:T(128)S(1)} %pad_add_fusion.scalar_ref, s32[5]{0:T(128)S(1)} %shift-right-arithmetic_and_fusion.side_ref.refs_0_, bf16[30,64,128]{2,1,0:T(8,128)(2,1)S(1)} %cap_stack.1.mine_ref, ...), custom_call_target="tpu_custom_call" | custom-call | flops 2750000128 | bytes 2500000 | tf_op jit(solution)/shard_map/elimination/pallas_call | solution.py:614
  82.6 2.5 %collective-permute-done.28.r3_ref.refs_6_ = bf16[512,128]{1,0:T(8,128)(2,1)S(1)} collective-permute-done((bf16[512,128]{1,0:T(8,128)(2,1)S(1)}, bf16[512,128]{1,0:T(8,128)(2,1)S(1)}, u32[]{:S(2)}, u32[]{:S(2)}) %collective-permute-start.28) | collective-permute-done | bytes 131104 | tf_op jit(solution)/shard_map/ppermute | solution.py:30
  85.0 3.7 %collective-permute-done.27.r2_ref.refs_5_ = bf16[512,128]{1,0:T(8,128)(2,1)S(1)} collective-permute-done((bf16[512,128]{1,0:T(8,128)(2,1)S(1)}, bf16[512,128]{1,0:T(8,128)(2,1)S(1)}, u32[]{:S(2)}, u32[]{:S(2)}) %collective-permute-start.27) | collective-permute-done | bytes 131104 | tf_op jit(solution)/shard_map/ppermute | solution.py:30
  90.8 2.8 %collective-permute-start.31 = (bf16[256,128]{1,0:T(8,128)(2,1)S(1)}, bf16[256,128]{1,0:T(8,128)(2,1)S(1)}, u32[]{:S(2)}, u32[]{:S(2)}) collective-permute-start(bf16[256,128]{1,0:T(8,128)(2,1)S(1)} %get-tuple-element.101), channel_id=1, source_target_pairs={{0,96},{1,97},{2,98},{3,99},{4,100},{5,101},{6,102},{7,103},{8,104... | collective-permute-start | bytes 196616 | tf_op jit(solution)/shard_map/ppermute | solution.py:30
  96.2 3.5 %collective-permute-done.30.z2_ref.refs_5_ = bf16[256,128]{1,0:T(8,128)(2,1)S(1)} collective-permute-done((bf16[256,128]{1,0:T(8,128)(2,1)S(1)}, bf16[256,128]{1,0:T(8,128)(2,1)S(1)}, u32[]{:S(2)}, u32[]{:S(2)}) %collective-permute-start.30) | collective-permute-done | bytes 65568 | tf_op jit(solution)/shard_map/ppermute | solution.py:30
  99.7 5.5 %collective-permute-start.32 = (bf16[128,128]{1,0:T(8,128)(2,1)S(1)}, bf16[128,128]{1,0:T(8,128)(2,1)S(1)}, u32[]{:S(2)}, u32[]{:S(2)}) collective-permute-start(bf16[128,128]{1,0:T(8,128)(2,1)S(1)} %own4.1.a_ref), channel_id=1, source_target_pairs={{0,128},{1,129},{2,130},{3,131},{4,132},{5,133},{6,134},{7,135},{8... | collective-permute-start | bytes 98312 | tf_op jit(solution)/shard_map/ppermute | solution.py:30
  108.7 3.8 %collective-permute-start.34 = (bf16[640,128]{1,0:T(8,128)(2,1)S(1)}, bf16[640,128]{1,0:T(8,128)(2,1)S(1)}, u32[]{:S(2)}, u32[]{:S(2)}) collective-permute-start(bf16[640,128]{1,0:T(8,128)(2,1)S(1)} %solve_4.1.b0_ref), channel_id=1, source_target_pairs={{0,4},{1,5},{2,6},{3,7},{4,0},{5,1},{6,2},{7,3},{8,12},{9,13},{10,... | collective-permute-start | bytes 491528 | tf_op jit(solution)/shard_map/ppermute | solution.py:30
  114.1 4.0 %collective-permute-done.34.b2_ref = bf16[640,128]{1,0:T(8,128)(2,1)S(1)} collective-permute-done((bf16[640,128]{1,0:T(8,128)(2,1)S(1)}, bf16[640,128]{1,0:T(8,128)(2,1)S(1)}, u32[]{:S(2)}, u32[]{:S(2)}) %collective-permute-start.34) | collective-permute-done | bytes 163872 | tf_op jit(solution)/shard_map/ppermute | solution.py:30
  118.2 3.3 %collective-permute-start.36 = (bf16[640,512]{1,0:T(8,128)(2,1)S(1)}, bf16[640,512]{1,0:T(8,128)(2,1)S(1)}, u32[]{:S(2)}, u32[]{:S(2)}) collective-permute-start(bf16[640,512]{1,0:T(8,128)(2,1)S(1)} %columns.1.t0_ref), channel_id=1, source_target_pairs={{0,1},{1,0},{2,3},{3,2},{4,5},{5,4},{6,7},{7,6},{8,9},{9,8},{10,11... | collective-permute-start | bytes 1966088 | tf_op jit(solution)/shard_map/ppermute | solution.py:30
  123.2 2.4 %update.1 = f32[512,1024]{1,0:T(8,128)} custom-call(s32[4]{0:T(128)S(1)} %pad_add_fusion.scalar_ref, f32[512,512]{1,0:T(8,128)S(1)} %get-tuple-element.87.y0_ref, f32[512,512]{1,0:T(8,128)S(1)} %get-tuple-element.88.y1_ref, bf16[5,512,128]{2,1,0:T(8,128)(2,1)S(1)} %get-tuple-element.89.u_ref, bf16[640,512]{1,0:T(8,128)(2,1)S(1)} %columns.1.t0_ref, ...), custom_call_target="tpu_custom_call" | custom-call | tf_op jit(solution)/shard_map/update/pallas_call | solution.py:527
  (95 shorter events, 42.4 us)
Async XLA Ops:
  8.6 11.6 %collective-permute-start.14 = (bf16[512,4096]{1,0:T(8,128)(2,1)}, bf16[512,4096]{1,0:T(8,128)(2,1)S(1)}, u32[]{:S(2)}, u32[]{:S(2)}) collective-permute-start(bf16[512,4096]{1,0:T(8,128)(2,1)} %a0_hbm.1), channel_id=1, source_target_pairs={{0,1},{1,0},{2,3},{3,2},{4,5},{5,4},{6,7},{7,6},{8,9},{9,8},{10,11... | collective-permute-start | bytes 12582920 | tf_op jit(solution)/shard_map/ppermute | solution.py:30
  9.1 8.1 %collective-permute-start.11 = (bf16[640,512]{1,0:T(8,128)(2,1)S(1)}, bf16[640,512]{1,0:T(8,128)(2,1)S(1)}, u32[]{:S(2)}, u32[]{:S(2)}) collective-permute-start(bf16[640,512]{1,0:T(8,128)(2,1)S(1)} %get-tuple-element.71.va_ref), channel_id=1, source_target_pairs={{0,1},{1,0},{2,3},{3,2},{4,5},{5,4},{6,7},{7,6},{8,9},{9,8},{10,11... | collective-permute-start | bytes 1966088 | tf_op jit(solution)/shard_map/ppermute | solution.py:30
  11.8 7.5 %collective-permute-start.2 = (bf16[15,16,128]{2,1,0:T(8,128)(2,1)S(1)}, bf16[15,16,128]{2,1,0:T(8,128)(2,1)S(1)}, u32[]{:S(2)}, u32[]{:S(2)}) collective-permute-start(bf16[15,16,128]{2,1,0:T(8,128)(2,1)S(1)} %get-tuple-element.58), channel_id=1, source_target_pairs={{0,4},{1,5},{2,6},{3,7},{4,0},{5,1},{6,2},{7,3},{8,12},{9,13},{10,... | collective-permute-start | bytes 184328 | tf_op jit(solution)/shard_map/ppermute | solution.py:30
  17.8 25.0 %collective-permute-start.13 = (bf16[1024,512]{1,0:T(8,128)(2,1)S(1)}, bf16[1024,512]{1,0:T(8,128)(2,1)S(1)}, u32[]{:S(2)}, u32[]{:S(2)}) collective-permute-start(bf16[1024,512]{1,0:T(8,128)(2,1)S(1)} %chip.1.b0_ref), channel_id=1, source_target_pairs={{0,2},{1,3},{2,4},{3,5},{4,6},{5,7},{6,0},{7,1},{8,10},{9,11},{10,... | collective-permute-start | bytes 3145736 | tf_op jit(solution)/shard_map/ppermute | solution.py:30
  20.2 22.6 %collective-permute-start.15 = (bf16[1024,512]{1,0:T(8,128)(2,1)S(1)}, bf16[1024,512]{1,0:T(8,128)(2,1)S(1)}, u32[]{:S(2)}, u32[]{:S(2)}) collective-permute-start(bf16[1024,512]{1,0:T(8,128)(2,1)S(1)} %chip.1.b0_ref), channel_id=1, source_target_pairs={{0,6},{1,7},{2,0},{3,1},{4,2},{5,3},{6,4},{7,5},{8,14},{9,15},{10,... | collective-permute-start | bytes 3145736 | tf_op jit(solution)/shard_map/ppermute | solution.py:30
  21.5 6.6 %collective-permute-start.4 = (bf16[15,16,128]{2,1,0:T(8,128)(2,1)S(1)}, bf16[15,16,128]{2,1,0:T(8,128)(2,1)S(1)}, u32[]{:S(2)}, u32[]{:S(2)}) collective-permute-start(bf16[15,16,128]{2,1,0:T(8,128)(2,1)S(1)} %get-tuple-element.61), channel_id=1, source_target_pairs={{0,8},{1,9},{2,10},{3,11},{4,12},{5,13},{6,14},{7,15},{8,0},{9,1},... | collective-permute-start | bytes 184328 | tf_op jit(solution)/shard_map/ppermute | solution.py:30
  36.3 6.5 %collective-permute-start.10 = (f32[1,16,128]{2,1,0:T(8,128)S(1)}, f32[1,16,128]{2,1,0:T(8,128)S(1)}, u32[]{:S(2)}, u32[]{:S(2)}) collective-permute-start(f32[1,16,128]{2,1,0:T(8,128)S(1)} %get-tuple-element.68.own4_ref), channel_id=1, source_target_pairs={{0,128},{1,129},{2,130},{3,131},{4,132},{5,133},{6,134},{7,135},{8... | collective-permute-start | bytes 24584 | tf_op jit(solution)/shard_map/ppermute | solution.py:30
  42.9 11.6 %collective-permute-start.18 = (bf16[30,16,128]{2,1,0:T(8,128)(2,1)S(1)}, bf16[30,16,128]{2,1,0:T(8,128)(2,1)S(1)}, u32[]{:S(2)}, u32[]{:S(2)}) collective-permute-start(bf16[30,16,128]{2,1,0:T(8,128)(2,1)S(1)} %cap_both.1.b0_ref), channel_id=1, source_target_pairs={{0,2},{1,3},{2,4},{3,5},{4,6},{5,7},{6,0},{7,1},{8,10},{9,11},{10,... | collective-permute-start | bytes 368648 | tf_op jit(solution)/shard_map/ppermute | solution.py:30
  43.0 11.5 %collective-permute-start.17 = (bf16[30,16,128]{2,1,0:T(8,128)(2,1)S(1)}, bf16[30,16,128]{2,1,0:T(8,128)(2,1)S(1)}, u32[]{:S(2)}, u32[]{:S(2)}) collective-permute-start(bf16[30,16,128]{2,1,0:T(8,128)(2,1)S(1)} %cap_both.1.b0_ref), channel_id=1, source_target_pairs={{0,4},{1,5},{2,6},{3,7},{4,0},{5,1},{6,2},{7,3},{8,12},{9,13},{10,... | collective-permute-start | bytes 368648 | tf_op jit(solution)/shard_map/ppermute | solution.py:30
  46.2 8.3 %collective-permute-start.16 = (bf16[30,16,128]{2,1,0:T(8,128)(2,1)S(1)}, bf16[30,16,128]{2,1,0:T(8,128)(2,1)S(1)}, u32[]{:S(2)}, u32[]{:S(2)}) collective-permute-start(bf16[30,16,128]{2,1,0:T(8,128)(2,1)S(1)} %cap_both.1.b0_ref), channel_id=1, source_target_pairs={{0,6},{1,7},{2,0},{3,1},{4,2},{5,3},{6,4},{7,5},{8,14},{9,15},{10,... | collective-permute-start | bytes 368648 | tf_op jit(solution)/shard_map/ppermute | solution.py:30
  46.2 12.2 %collective-permute-start.19 = (bf16[512,512]{1,0:T(8,128)(2,1)S(1)}, bf16[512,512]{1,0:T(8,128)(2,1)S(1)}, u32[]{:S(2)}, u32[]{:S(2)}) collective-permute-start(bf16[512,512]{1,0:T(8,128)(2,1)S(1)} %get-tuple-element.77), channel_id=1, source_target_pairs={{0,2},{1,3},{2,4},{3,5},{4,6},{5,7},{6,0},{7,1},{8,10},{9,11},{10,... | collective-permute-start | bytes 1572872 | tf_op jit(solution)/shard_map/ppermute | solution.py:30
  47.7 9.6 %collective-permute-start.20 = (bf16[512,512]{1,0:T(8,128)(2,1)S(1)}, bf16[512,512]{1,0:T(8,128)(2,1)S(1)}, u32[]{:S(2)}, u32[]{:S(2)}) collective-permute-start(bf16[512,512]{1,0:T(8,128)(2,1)S(1)} %get-tuple-element.82), channel_id=1, source_target_pairs={{0,6},{1,7},{2,0},{3,1},{4,2},{5,3},{6,4},{7,5},{8,14},{9,15},{10,... | collective-permute-start | bytes 1572872 | tf_op jit(solution)/shard_map/ppermute | solution.py:30
  61.1 16.2 %collective-permute-start.21 = (f32[512,512]{1,0:T(8,128)S(1)}, f32[512,512]{1,0:T(8,128)}, u32[]{:S(2)}, u32[]{:S(2)}) collective-permute-start(f32[512,512]{1,0:T(8,128)S(1)} %get-tuple-element.86.y1_ref), channel_id=1, source_target_pairs={{0,1},{1,0},{2,3},{3,2},{4,5},{5,4},{6,7},{7,6},{8,9},{9,8},{10,11... | collective-permute-start | bytes 3145736 | tf_op jit(solution)/shard_map/ppermute | solution.py:30
  67.4 7.0 %collective-permute-start.22 = (bf16[30,64,128]{2,1,0:T(8,128)(2,1)S(1)}, bf16[30,64,128]{2,1,0:T(8,128)(2,1)}, u32[]{:S(2)}, u32[]{:S(2)}) collective-permute-start(bf16[30,64,128]{2,1,0:T(8,128)(2,1)S(1)} %cap_stack.1.mine_ref), channel_id=1, source_target_pairs={{0,1},{1,0},{2,3},{3,2},{4,5},{5,4},{6,7},{7,6},{8,9},{9,8},{10,11... | collective-permute-start | bytes 1474568 | tf_op jit(solution)/shard_map/ppermute | solution.py:30
  67.6 9.8 %collective-permute-start.23 = (bf16[640,128]{1,0:T(8,128)(2,1)S(1)}, bf16[640,128]{1,0:T(8,128)(2,1)S(1)}, u32[]{:S(2)}, u32[]{:S(2)}) collective-permute-start(bf16[640,128]{1,0:T(8,128)(2,1)S(1)} %get-tuple-element.91), channel_id=1, source_target_pairs={{0,2},{1,3},{2,4},{3,5},{4,6},{5,7},{6,0},{7,1},{8,10},{9,11},{10,... | collective-permute-start | bytes 491528 | tf_op jit(solution)/shard_map/ppermute | solution.py:30
  67.8 10.7 %collective-permute-start.24 = (bf16[640,128]{1,0:T(8,128)(2,1)S(1)}, bf16[640,128]{1,0:T(8,128)(2,1)S(1)}, u32[]{:S(2)}, u32[]{:S(2)}) collective-permute-start(bf16[640,128]{1,0:T(8,128)(2,1)S(1)} %get-tuple-element.92), channel_id=1, source_target_pairs={{0,4},{1,5},{2,6},{3,7},{4,0},{5,1},{6,2},{7,3},{8,12},{9,13},{10,... | collective-permute-start | bytes 491528 | tf_op jit(solution)/shard_map/ppermute | solution.py:30
  71.2 7.4 %collective-permute-start.25 = (bf16[640,128]{1,0:T(8,128)(2,1)S(1)}, bf16[640,128]{1,0:T(8,128)(2,1)S(1)}, u32[]{:S(2)}, u32[]{:S(2)}) collective-permute-start(bf16[640,128]{1,0:T(8,128)(2,1)S(1)} %get-tuple-element.93), channel_id=1, source_target_pairs={{0,6},{1,7},{2,0},{3,1},{4,2},{5,3},{6,4},{7,5},{8,14},{9,15},{10,... | collective-permute-start | bytes 491528 | tf_op jit(solution)/shard_map/ppermute | solution.py:30
  79.2 9.6 %collective-permute-start.26 = (bf16[640,128]{1,0:T(8,128)(2,1)S(1)}, bf16[640,128]{1,0:T(8,128)(2,1)S(1)}, u32[]{:S(2)}, u32[]{:S(2)}) collective-permute-start(bf16[640,128]{1,0:T(8,128)(2,1)S(1)} %get-tuple-element.99.e_ref.refs_3_), channel_id=1, source_target_pairs={{0,8},{1,9},{2,10},{3,11},{4,12},{5,13},{6,14},{7,15},{8,0},{9,1},... | collective-permute-start | bytes 491528 | tf_op jit(solution)/shard_map/ppermute | solution.py:30
  81.8 7.0 %collective-permute-start.27 = (bf16[512,128]{1,0:T(8,128)(2,1)S(1)}, bf16[512,128]{1,0:T(8,128)(2,1)S(1)}, u32[]{:S(2)}, u32[]{:S(2)}) collective-permute-start(bf16[512,128]{1,0:T(8,128)(2,1)S(1)} %get-tuple-element.97), channel_id=1, source_target_pairs={{0,16},{1,17},{2,18},{3,19},{4,20},{5,21},{6,22},{7,23},{8,24},{9,... | collective-permute-start | bytes 393224 | tf_op jit(solution)/shard_map/ppermute | solution.py:30
  88.9 10.8 %collective-permute-start.29 = (bf16[384,128]{1,0:T(8,128)(2,1)S(1)}, bf16[384,128]{1,0:T(8,128)(2,1)S(1)}, u32[]{:S(2)}, u32[]{:S(2)}) collective-permute-start(bf16[384,128]{1,0:T(8,128)(2,1)S(1)} %get-tuple-element.102.quad_ref.refs_3_), channel_id=1, source_target_pairs={{0,32},{1,33},{2,34},{3,35},{4,36},{5,37},{6,38},{7,39},{8,40},{9,... | collective-permute-start | bytes 294920 | tf_op jit(solution)/shard_map/ppermute | solution.py:30
  93.6 6.1 %collective-permute-start.30 = (bf16[256,128]{1,0:T(8,128)(2,1)S(1)}, bf16[256,128]{1,0:T(8,128)(2,1)S(1)}, u32[]{:S(2)}, u32[]{:S(2)}) collective-permute-start(bf16[256,128]{1,0:T(8,128)(2,1)S(1)} %get-tuple-element.101), channel_id=1, source_target_pairs={{0,64},{1,65},{2,66},{3,67},{4,68},{5,69},{6,70},{7,71},{8,72},{9,... | collective-permute-start | bytes 196616 | tf_op jit(solution)/shard_map/ppermute | solution.py:30
  99.7 6.9 %collective-permute-start.32 = (bf16[128,128]{1,0:T(8,128)(2,1)S(1)}, bf16[128,128]{1,0:T(8,128)(2,1)S(1)}, u32[]{:S(2)}, u32[]{:S(2)}) collective-permute-start(bf16[128,128]{1,0:T(8,128)(2,1)S(1)} %own4.1.a_ref), channel_id=1, source_target_pairs={{0,128},{1,129},{2,130},{3,131},{4,132},{5,133},{6,134},{7,135},{8... | collective-permute-start | bytes 98312 | tf_op jit(solution)/shard_map/ppermute | solution.py:30
  107.6 6.5 %collective-permute-start.35 = (bf16[640,128]{1,0:T(8,128)(2,1)S(1)}, bf16[640,128]{1,0:T(8,128)(2,1)S(1)}, u32[]{:S(2)}, u32[]{:S(2)}) collective-permute-start(bf16[640,128]{1,0:T(8,128)(2,1)S(1)} %solve_4.1.b0_ref), channel_id=1, source_target_pairs={{0,2},{1,3},{2,4},{3,5},{4,6},{5,7},{6,0},{7,1},{8,10},{9,11},{10,... | collective-permute-start | bytes 491528 | tf_op jit(solution)/shard_map/ppermute | solution.py:30
  108.7 9.3 %collective-permute-start.34 = (bf16[640,128]{1,0:T(8,128)(2,1)S(1)}, bf16[640,128]{1,0:T(8,128)(2,1)S(1)}, u32[]{:S(2)}, u32[]{:S(2)}) collective-permute-start(bf16[640,128]{1,0:T(8,128)(2,1)S(1)} %solve_4.1.b0_ref), channel_id=1, source_target_pairs={{0,4},{1,5},{2,6},{3,7},{4,0},{5,1},{6,2},{7,3},{8,12},{9,13},{10,... | collective-permute-start | bytes 491528 | tf_op jit(solution)/shard_map/ppermute | solution.py:30
  (22 other events, 151.2 us)
